TPU v7x, 512 devices: a whole 4x8x8 slice. The times are simulated.
512 devices in a mesh: dp: 64 (over y, x, core), tensor: 8 (over z).
Axes of the slice: x: 4, y: 8, z: 8, core: 2. Of those that a mesh axis runs over, the one named last changes fastest.
Arguments:
- tokens: bfloat16 [32768, 6144], P('dp', 'tensor'), may hold values from -6 to 6
- old_master: float32 [6144, 7168], P('dp', 'tensor'), may hold values from -0.078125 to 0.078125
- old_first: float32 [6144, 7168], P('dp', 'tensor'), may hold values from -4 to 4
- old_second: float32 [6144, 7168], P('dp', 'tensor'), may hold values from 0.01 to 1
- piece_lengths: int32 [64], replicated, may hold values from 1 to 15, 672 in all
- piece_shifts: int32 [64], replicated, may hold values from 0 to 63, each once
Outputs:
- new_master: float32 [6144, 7168], P('dp', 'tensor')
- new_first: float32 [6144, 7168], P('dp', 'tensor')
- new_second: float32 [6144, 7168], P('dp', 'tensor')
- query: bfloat16 [32768, 6144], P('dp', 'tensor')
- key: bfloat16 [32768, 1024], P('dp', 'tensor')
Inputs may be any that keep to these rules, and one draw needn't show every extreme that they name: `piece_lengths`: they sum to 672, and the longest is exactly 15. `piece_shifts`: each of 0 to 63 appears once.
All inputs are finite; a program needn't handle non-finite values.
Results may differ from a plain program's by a relative error of at most 0.0065.
Values may be sent and summed in bfloat16 or wider, within the bound.
No kernel may reach another device: no remote copies, remote signals or barrier semaphores. Data moves between devices by JAX's collectives and lax.ppermute only.
A program may use at most 128 MiB of HBM per device.

v0:
```python
import jax
import jax.numpy as jnp
from jax import lax
from jax.sharding import PartitionSpec as P

HQ = 48
HS = 128


def per_device(tokens, old_master, old_first, old_second, piece_lengths, piece_shifts):
    dp_count = lax.axis_size("dp")
    tensor_count = lax.axis_size("tensor")
    own_index = lax.axis_index("dp")
    depth_dev, block_cols = old_master.shape
    heads_dev = block_cols // HS
    row_count = depth_dev * heads_dev
    bucket_rows = 3 * row_count // (2 * dp_count)
    seg_ends = jnp.cumsum(piece_lengths)
    seg_starts = seg_ends - piece_lengths
    peer_ids = jnp.arange(dp_count, dtype=jnp.int32)
    targets = (own_index + piece_shifts) % dp_count
    matches = (targets[:, None] == peer_ids[None, :]).astype(jnp.int32)
    send_start = jnp.sum(matches * seg_starts[:, None], axis=0)
    send_length = jnp.sum(matches * piece_lengths[:, None], axis=0)
    offsets = jnp.arange(bucket_rows, dtype=jnp.int32)
    send_index = send_start[:, None] + offsets[None, :]
    send_valid = (offsets[None, :] < send_length[:, None])[:, :, None]
    slot_ids = jnp.arange(row_count, dtype=jnp.int32)
    member = (
        (slot_ids[:, None] >= seg_starts[None, :]) & (slot_ids[:, None] < seg_ends[None, :])
    ).astype(jnp.int32)
    slot_start = jnp.sum(member * seg_starts[None, :], axis=1)
    slot_shift = jnp.sum(member * piece_shifts[None, :], axis=1)
    recv_index = (own_index - slot_shift) % dp_count * bucket_rows + slot_ids - slot_start

    def pack(block):
        padded = jnp.concatenate(
            [block.reshape(row_count, HS), jnp.zeros((bucket_rows, HS), block.dtype)], axis=0
        )
        return jnp.where(send_valid, padded[send_index], jnp.zeros((), block.dtype))

    def unpack(received):
        return received.reshape(dp_count * bucket_rows, HS)[recv_index].reshape(
            depth_dev, block_cols
        )

    whole_tokens = lax.all_gather(tokens, "tensor", axis=1, tiled=True)
    new_master = unpack(
        lax.all_to_all(
            pack(old_master).astype(jnp.bfloat16), "dp", split_axis=0, concat_axis=0, tiled=True
        ).astype(jnp.float32)
    )
    new_first = unpack(
        lax.all_to_all(
            pack(old_first).astype(jnp.bfloat16), "dp", split_axis=0, concat_axis=0, tiled=True
        ).astype(jnp.float32)
    )
    new_second = unpack(
        lax.all_to_all(
            pack(old_second).astype(jnp.bfloat16), "dp", split_axis=0, concat_axis=0, tiled=True
        ).astype(jnp.float32)
    )
    product = jnp.dot(
        whole_tokens,
        lax.all_gather(new_master.astype(jnp.bfloat16), "dp", axis=0, tiled=True),
        preferred_element_type=jnp.float32,
    )
    query_cols = HQ // tensor_count * HS
    query = product[:, :query_cols].astype(jnp.bfloat16)
    key = product[:, query_cols:].astype(jnp.bfloat16)
    return (new_master, new_first, new_second, query, key)


def solution(mesh):
    return jax.shard_map(
        per_device,
        mesh=mesh,
        in_specs=(
            P("dp", "tensor"),
            P("dp", "tensor"),
            P("dp", "tensor"),
            P("dp", "tensor"),
            P(),
            P(),
        ),
        out_specs=(
            P("dp", "tensor"),
            P("dp", "tensor"),
            P("dp", "tensor"),
            P("dp", "tensor"),
            P("dp", "tensor"),
        ),
        check_vma=False,
    )
```

profile of v0, /device:TPU:1, one launch (start us, length us, event | category | flops | bytes accessed | tf_op | source)
XLA Modules:
  0.0 208.4 jit_solution(14950141859150892020)
XLA Ops:
  7.9 0.7 copy.17
  10.2 0.8 select_reduce_fusion.3
  11.2 1.2 reshape.203
  12.4 3.3 %gather_fusion = bf16[960,128]{1,0:T(8,128)(2,1)S(1)} fusion(bf16[687,128]{1,0:T(8,128)(2,1)S(1)} %concatenate.9, s32[1024]{0:T(1024)S(1)} %pad_clamp_fusion.1), kind=kCustom, calls=%fused_computation | custom fusion | bytes 495360 | tf_op jit(solution)/shard_map/gather | solution.py:40
  15.8 1.2 reshape.209
  17.0 3.3 %gather_fusion.2 = bf16[960,128]{1,0:T(8,128)(2,1)S(1)} fusion(bf16[687,128]{1,0:T(8,128)(2,1)S(1)} %concatenate.10, s32[1024]{0:T(1024)S(1)} %pad_clamp_fusion.1), kind=kCustom, calls=%fused_computation.2 | custom fusion | bytes 495360 | tf_op jit(solution)/shard_map/gather | solution.py:40
  20.6 3.3 %gather_fusion.4 = bf16[960,128]{1,0:T(8,128)(2,1)S(1)} fusion(bf16[687,128]{1,0:T(8,128)(2,1)S(1)} %concatenate.11, s32[1024]{0:T(1024)S(1)} %pad_clamp_fusion.1), kind=kCustom, calls=%fused_computation.4 | custom fusion | bytes 495360 | tf_op jit(solution)/shard_map/gather | solution.py:40
  24.1 1.1 select_convert_fusion
  25.1 11.6 %all-to-all-start = ((bf16[64,15,128]{2,1,0:T(8,128)(2,1)}), bf16[64,15,128]{2,1,0:T(8,128)(2,1)S(1)}, u32[]{:S(2)}, u32[]{:S(2)}) async-start(bf16[64,15,128]{2,1,0:T(8,128)(2,1)} %get-tuple-element.26), calls=%async_computation | async-start | bytes 524288 | tf_op jit(solution)/shard_map/all_to_all | solution.py:49
  37.0 12.9 %all-to-all-done = bf16[64,15,128]{2,1,0:T(8,128)(2,1)S(1)} async-done(((bf16[64,15,128]{2,1,0:T(8,128)(2,1)}), bf16[64,15,128]{2,1,0:T(8,128)(2,1)S(1)}, u32[]{:S(2)}, u32[]{:S(2)}) %all-to-all-start) | async-done | bytes 245792 | tf_op jit(solution)/shard_map/all_to_all | solution.py:49
  50.0 1.7 gather_fusion.1
  51.8 0.7 convert_element_type.22
  52.6 17.7 %all_to_all.15 = bf16[64,15,128]{2,1,0:T(8,128)(2,1)S(1)} all-to-all(bf16[64,15,128]{2,1,0:T(8,128)(2,1)S(1)} %get-tuple-element.25), channel_id=1, replica_groups=mesh['dp'=64,'tensor'=8] {'dp'}, dimensions={0} | all-to-all | bytes 491520 | tf_op jit(solution)/shard_map/all_to_all | solution.py:54
  70.2 4.7 %all-to-all-start.2 = ((bf16[64,15,128]{2,1,0:T(8,128)(2,1)}), bf16[64,15,128]{2,1,0:T(8,128)(2,1)S(1)}, u32[]{:S(2)}, u32[]{:S(2)}) async-start(bf16[64,15,128]{2,1,0:T(8,128)(2,1)} %get-tuple-element.24), calls=%async_computation.2 | async-start | bytes 524288 | tf_op jit(solution)/shard_map/all_to_all | solution.py:59
  75.0 1.7 gather_fusion.3
  76.7 0.8 reshape.212
  77.5 10.6 %all-to-all-done.2 = bf16[64,15,128]{2,1,0:T(8,128)(2,1)S(1)} async-done(((bf16[64,15,128]{2,1,0:T(8,128)(2,1)}), bf16[64,15,128]{2,1,0:T(8,128)(2,1)S(1)}, u32[]{:S(2)}, u32[]{:S(2)}) %all-to-all-start.2) | async-done | bytes 245792 | tf_op jit(solution)/shard_map/all_to_all | solution.py:59
  88.2 1.7 gather_fusion.5
  89.9 0.8 reshape.216
  90.7 2.8 %all-gather.5.cloned.1.call-done = bf16[512,6144]{1,0:T(8,128)(2,1)} async-done(((bf16[512,768]{1,0:T(8,128)(2,1)}), bf16[512,6144]{1,0:T(8,128)(2,1)}) %all-gather.5.cloned.1.call-update) | async-done | bytes 6291472 | tf_op jit(solution)/shard_map/all_gather | solution.py:47
  93.5 94.8 %all-gather.3.cloned.1.call-done = bf16[6144,896]{1,0:T(8,128)(2,1)} async-done(((bf16[96,896]{1,0:T(8,128)(2,1)}), bf16[6144,896]{1,0:T(8,128)(2,1)}) %all-gather.3.cloned.1.call-update) | async-done | bytes 11010064 | tf_op jit(solution)/shard_map/all_gather | solution.py:65
  188.3 11.2 %fusion = bf16[512,896]{0,1:T(8,128)(2,1)S(1)} fusion(bf16[6144,896]{1,0:T(8,128)(2,1)} %all-gather.3.cloned.1.call-done, bf16[512,6144]{1,0:T(8,128)(2,1)} %all-gather.5.cloned.1.call-done), kind=kOutput, calls=%fused_computation.7 | convolution fusion | flops 5637603328 | bytes 18219008 | tf_op jit(solution)/shard_map/dot_general | solution.py:63
  199.6 1.2 copy.18
  200.8 0.8 copy.19
  (35 shorter events, 3.6 us)
Async XLA Ops:
  7.2 13.2 %copy-start.1 = (f32[96,896]{1,0:T(8,128)S(1)}, f32[96,896]{1,0:T(8,128)}, u32[]{:S(2)}) copy-start(f32[96,896]{1,0:T(8,128)} %param.9) | copy-start | bytes 1032196
  7.2 86.3 %all-gather.5.cloned.1.call-start = ((), (), s32[]{:S(2)}) async-start(), calls=%async_computation.4 | async-start | bytes 7077888 | tf_op jit(solution)/shard_map/all_gather | solution.py:47
  12.4 24.5 %copy-start.2 = (s32[64]{0:T(128)S(1)}, s32[64]{0:T(128)}, u32[]{:S(2)}) copy-start(s32[64]{0:T(128)} %param.11) | copy-start | bytes 772
  25.1 24.8 %all-to-all-start = ((bf16[64,15,128]{2,1,0:T(8,128)(2,1)}), bf16[64,15,128]{2,1,0:T(8,128)(2,1)S(1)}, u32[]{:S(2)}, u32[]{:S(2)}) async-start(bf16[64,15,128]{2,1,0:T(8,128)(2,1)} %get-tuple-element.26), calls=%async_computation | async-start | bytes 524288 | tf_op jit(solution)/shard_map/all_to_all | solution.py:49
  36.8 151.6 %all-gather.3.cloned.1.call-start = ((), (), s32[]{:S(2)}) async-start(), calls=%async_computation.3 | async-start | bytes 11182080 | tf_op jit(solution)/shard_map/all_gather | solution.py:65
  51.8 147.8 %copy-start = (f32[96,896]{1,0:T(8,128)}, f32[96,896]{1,0:T(8,128)S(1)}, u32[]{:S(2)}) copy-start(f32[96,896]{1,0:T(8,128)S(1)} %reshape.208) | copy-start | bytes 1032196
  70.2 17.9 %all-to-all-start.2 = ((bf16[64,15,128]{2,1,0:T(8,128)(2,1)}), bf16[64,15,128]{2,1,0:T(8,128)(2,1)S(1)}, u32[]{:S(2)}, u32[]{:S(2)}) async-start(bf16[64,15,128]{2,1,0:T(8,128)(2,1)} %get-tuple-element.24), calls=%async_computation.2 | async-start | bytes 524288 | tf_op jit(solution)/shard_map/all_to_all | solution.py:59
Sparse Core Ops, SparseCore 0:
  10.1 83.3 all-gather.4
  97.4 90.8 all-gather.2
where the time goes:
time: 209 us; the launch traced here: 208 us
  waiting for transfers between devices  122 us (58%)
  local copies, waits for them, and re-layouts  22.5 us (11%)
  blocking collectives  17.7 us (8%)
  starting transfers between devices  16.4 us (8%)
  between operations  14.3 us (7%)
  matrix products  11.2 us (5%)
  other arithmetic  4.44 us (2%)
    all_gather x1, waiting for transfers between devices, per_device(): lax.all_gather(new_master.astype(jnp.bfloat16), 'dp', axis=0, tiled=True)  94.8 us
    all_to_all x1, blocking collectives, per_device(): lax.all_to_all(pack(old_first).astype(jnp.bfloat16), 'dp', split_axis=0,...  17.7 us
    all_to_all x1, waiting for transfers between devices, per_device(): lax.all_to_all(pack(old_master).astype(jnp.bfloat16), 'dp', split_axis=0,...  12.9 us
    all_to_all x1, starting transfers between devices, per_device(): lax.all_to_all(pack(old_master).astype(jnp.bfloat16), 'dp', split_axis=0,...  11.6 us
    dot_general x1, matrix products, per_device(): jnp.dot(whole_tokens, lax.all_gather(new_master.astype(jnp.bfloat16), 'dp...  11.2 us
    all_to_all x1, waiting for transfers between devices, per_device(): lax.all_to_all(pack(old_second).astype(jnp.bfloat16), 'dp', split_axis=0,...  10.6 us
    gather x6, local copies, waits for them, and re-layouts, pack(): return jnp.where(send_valid, padded[send_index], jnp.zeros((), block.dtype))  10.2 us
    gather x3, local copies, waits for them, and re-layouts, unpack(): received.reshape(dp_count * bucket_rows, HS)[recv_index]  5.04 us
  transfers between devices with their start and end apart: 4, of which 4 were waited for; matrix products, arithmetic and copies ran while one was open for 12% of the time, Pallas kernels for 0%

commit v1 on v0

v1 whole, which is shorter than its diff:
```python
import functools

import jax
import jax.numpy as jnp
from jax import lax
from jax.experimental import pallas as pl
from jax.experimental.pallas import tpu as pltpu
from jax.sharding import PartitionSpec as P

HQ = 48
HS = 128
NX = 4
NC = 2
HEADS = 7
ROWS = 96
SLOTS = ROWS * HEADS
HALF = SLOTS // 2
BUCKET = 16
N_DP = 64
NY = N_DP // (NX * NC)
GROUP = 16 * HEADS
VMEM_LIMIT = 56 * 1024 * 1024


def dp_moves(dy, dx, dc):
    moves = []
    for y in range(NY):
        for x in range(NX):
            for c in range(NC):
                source = (y * NX + x) * NC + c
                target = ((y + dy) % NY * NX + (x + dx) % NX) * NC + (c + dc) % NC
                moves.append((source, target))
    return moves


X_UP, X_DOWN = dp_moves(0, 1, 0), dp_moves(0, -1, 0)
Y_UP, Y_DOWN = dp_moves(1, 0, 0), dp_moves(-1, 0, 0)
SIBLING = dp_moves(0, 0, 1)


def move(array, moves):
    return lax.ppermute(array, "dp", moves)


def pack_kernel(lengths, shifts, own, first, second, out, first_rows, second_rows):
    for rows, state in ((first_rows, first), (second_rows, second)):
        for head in range(HEADS):
            rows[pl.ds(head, ROWS, stride=HEADS), :] = state[:, head * HS : (head + 1) * HS]
        rows[SLOTS : SLOTS + BUCKET, :] = jnp.zeros((BUCKET, HS), jnp.float32)
    me = own[0]

    def piece(j, start):
        target = (me + shifts[j]) & (N_DP - 1)
        out[target, :, 0:HS] = first_rows[pl.ds(start, BUCKET), :].astype(jnp.bfloat16)
        out[target, :, HS : 2 * HS] = second_rows[pl.ds(start, BUCKET), :].astype(jnp.bfloat16)
        return start + lengths[j]

    lax.fori_loop(0, N_DP, piece, jnp.int32(0))


def unpack_kernel(lengths, shifts, own, received, first, second, first_rows, second_rows):
    me = own[0]

    def piece(j, start):
        source = (me - shifts[j]) & (N_DP - 1)
        first_rows[pl.ds(start, BUCKET), :] = received[source, :, 0:HS].astype(jnp.float32)
        second_rows[pl.ds(start, BUCKET), :] = received[source, :, HS : 2 * HS].astype(jnp.float32)
        return start + lengths[j]

    lax.fori_loop(0, N_DP, piece, jnp.int32(0))
    for rows, state in ((first_rows, first), (second_rows, second)):
        for head in range(HEADS):
            state[:, head * HS : (head + 1) * HS] = rows[pl.ds(head, ROWS, stride=HEADS), :]


def weights_kernel(spans, lengths, shifts, own, *refs):
    n = len(spans)
    arrays, (weights, master), (blocks, rows, starts, firsts, places, sems) = refs[:n], refs[n : n + 2], refs[n + 2 :]
    group = pl.program_id(0)
    me = own[0]

    def copy(i):
        half, at, count = spans[i]
        return pltpu.make_async_copy(
            arrays[i], blocks.at[pl.ds(at, count), pl.ds(half * HALF, HALF), :], sems.at[i]
        )

    @pl.when(group == 0)
    def _():
        for i in range(n):
            copy(i).start()

        def piece(j, start):
            starts[j] = start
            firsts[(start + 15) >> 4] = j
            return start + lengths[j]

        lax.fori_loop(0, N_DP, piece, jnp.int32(0))
        my_y, my_x, my_c = me // (NX * NC), (me // NC) % NX, me % NC

        def place(q, carry):
            y = (q // (NX * NC) - my_y) & (NY - 1)
            x = ((q // NC) % NX - my_x) & (NX - 1)
            c = (q - my_c) & (NC - 1)
            y = jnp.where(y < NY // 2, 2 * y, 2 * NY - 1 - 2 * y)
            x = jnp.where(x < NX // 2, 2 * x, 2 * NX - 1 - 2 * x)
            for again in range(2):
                places[again * N_DP + q] = c * (NX * NY) + y * NX + x
                places[(2 + again) * N_DP + q] = c * (NX * NY) + x * NY + y
            return carry

        lax.fori_loop(0, N_DP, place, jnp.int32(0))

    for half in range(2):

        @pl.when(group == half * (HALF // GROUP))
        def _():
            for i in range(n):
                if spans[i][0] == half:
                    copy(i).wait()

    table = jnp.where(group >= HALF // GROUP, 2 * N_DP, 0)
    sublane = lax.broadcasted_iota(jnp.int32, (16, HS), 0)

    def tile(t, carry):
        whole = group * HEADS + t
        offset = pl.multiple_of(whole * 16, 16)
        begin, end = firsts[whole], firsts[whole + 1]

        def chunk(part, carry):
            def load(j):
                base = table + N_DP - shifts[j] + part * 8
                return [blocks[places[base + i], pl.ds(offset, 16), :].astype(jnp.float32) for i in range(8)]

            def later(j, held):
                keep = sublane >= starts[j] - offset
                return [jnp.where(keep, new, old) for new, old in zip(load(j), held)]

            held = lax.fori_loop(begin + 1, end + 1, later, load(begin))
            for i in range(8):
                rows[part * 8 + i, pl.ds(pl.multiple_of(t * 16, 16), 16), :] = held[i]
            return carry

        return lax.fori_loop(0, N_DP // 8, chunk, carry)

    lax.fori_loop(0, HEADS, tile, jnp.int32(0))

    def spread(p, carry):
        for head in range(HEADS):
            weights[p, :, head * HS : (head + 1) * HS] = rows[p, pl.ds(head, 16, stride=HEADS), :].astype(
                jnp.bfloat16
            )
        return carry

    lax.fori_loop(0, N_DP, spread, jnp.int32(0))
    for head in range(HEADS):
        master[:, head * HS : (head + 1) * HS] = rows[me, pl.ds(head, 16, stride=HEADS), :]


def product_kernel(tokens, weights, query, key, total):
    step = pl.program_id(0)
    part = jnp.dot(tokens[...], weights[...], preferred_element_type=jnp.float32)

    @pl.when(step == 0)
    def _():
        total[...] = part

    @pl.when(step > 0)
    def _():
        total[...] += part

    @pl.when(step == pl.num_programs(0) - 1)
    def _():
        query[...] = total[:, : query.shape[1]].astype(query.dtype)
        key[...] = total[:, query.shape[1] :].astype(key.dtype)


SMEM = pl.BlockSpec(memory_space=pltpu.SMEM)
VMEM = pl.BlockSpec(memory_space=pltpu.VMEM)


def gather_weights(master):
    low, high = master[:HALF][None], master[HALF:][None]
    spans, arrays = [], []

    def add(half, at, array):
        spans.append((half, at, array.shape[0]))
        arrays.append(array)

    up = move(low, X_UP)
    down = move(low, X_DOWN)
    row = jnp.concatenate([low, up, down, move(up, X_UP)], axis=0)
    ups, downs = [high], [high]
    for _ in range(3):
        ups.append(move(ups[-1], Y_UP))
        downs.append(move(downs[-1], Y_DOWN))
    column = [high]
    for k in range(1, 4):
        column += [ups[k], downs[k]]
    column = jnp.concatenate(column + [move(ups[3], Y_UP)], axis=0)

    row_ups, row_downs = [row], [row]
    for _ in range(3):
        row_ups.append(move(row_ups[-1], Y_UP))
        row_downs.append(move(row_downs[-1], Y_DOWN))
    last = [move(row_ups[3][: NX // 2], Y_UP), move(row_downs[3][NX // 2 :], Y_DOWN)]
    parts = [row]
    for k in range(1, 4):
        parts += [row_ups[k], row_downs[k]]
    parts += last
    at = 0
    for part in parts:
        add(0, at, part)
        at += part.shape[0]
    add(0, NX * NY, move(jnp.concatenate(parts[:3], axis=0), SIBLING))
    add(0, NX * NY + 3 * NX, move(jnp.concatenate(parts[3:], axis=0), SIBLING))

    column_up = move(column, X_UP)
    column_down = move(column, X_DOWN)
    last = [move(column_up[: NY // 2], X_UP), move(column_down[NY // 2 :], X_DOWN)]
    parts = [column, column_up, column_down] + last
    at = 0
    for part in parts:
        add(1, at, part)
        at += part.shape[0]
    add(1, NX * NY, move(column, SIBLING))
    add(1, NX * NY + NY, move(jnp.concatenate(parts[1:3], axis=0), SIBLING))
    add(1, NX * NY + 3 * NY, move(jnp.concatenate(parts[3:], axis=0), SIBLING))
    return tuple(spans), arrays


def per_device(tokens, old_master, old_first, old_second, piece_lengths, piece_shifts):
    own = lax.axis_index("dp").astype(jnp.int32)[None]
    depth_dev, block_cols = old_master.shape
    state = jax.ShapeDtypeStruct((depth_dev, block_cols), jnp.float32)
    slots = pltpu.VMEM((SLOTS + BUCKET, HS), jnp.float32)
    params = pltpu.CompilerParams(vmem_limit_bytes=VMEM_LIMIT)

    whole_tokens = lax.all_gather(tokens, "tensor", axis=1, tiled=True)

    spans, arrays = gather_weights(old_master.astype(jnp.bfloat16).reshape(SLOTS, HS))

    packed = pl.pallas_call(
        pack_kernel,
        out_shape=jax.ShapeDtypeStruct((N_DP, BUCKET, 2 * HS), jnp.bfloat16),
        in_specs=[SMEM] * 3 + [VMEM] * 2,
        out_specs=VMEM,
        scratch_shapes=[slots, slots],
        name="pack",
    )(piece_lengths, piece_shifts, own, old_first, old_second)
    received = lax.all_to_all(packed, "dp", split_axis=0, concat_axis=0, tiled=True)
    new_first, new_second = pl.pallas_call(
        unpack_kernel,
        out_shape=[state, state],
        in_specs=[SMEM] * 3 + [VMEM],
        out_specs=[VMEM] * 2,
        scratch_shapes=[slots, slots],
        name="unpack",
    )(piece_lengths, piece_shifts, own, received)

    weights, new_master = pl.pallas_call(
        functools.partial(weights_kernel, spans),
        grid=(SLOTS // GROUP,),
        out_shape=[jax.ShapeDtypeStruct((N_DP, depth_dev, block_cols), jnp.bfloat16), state],
        in_specs=[SMEM] * 3 + [pl.BlockSpec(memory_space=pl.ANY)] * len(arrays),
        out_specs=[
            pl.BlockSpec((N_DP, 16, block_cols), lambda g: (0, g, 0)),
            pl.BlockSpec((16, block_cols), lambda g: (g, 0)),
        ],
        scratch_shapes=[
            pltpu.VMEM((N_DP, SLOTS, HS), jnp.bfloat16),
            pltpu.VMEM((N_DP, GROUP, HS), jnp.float32),
            pltpu.SMEM((N_DP,), jnp.int32),
            pltpu.SMEM((SLOTS // 16 + 8,), jnp.int32),
            pltpu.SMEM((4 * N_DP,), jnp.int32),
            pltpu.SemaphoreType.DMA((len(arrays),)),
        ],
        compiler_params=params,
        name="weights",
    )(piece_lengths, piece_shifts, own, *arrays)

    tokens_dev, width = whole_tokens.shape
    query_cols = HQ // lax.axis_size("tensor") * HS
    step = width // 8
    query, key = pl.pallas_call(
        product_kernel,
        grid=(width // step,),
        out_shape=[
            jax.ShapeDtypeStruct((tokens_dev, query_cols), jnp.bfloat16),
            jax.ShapeDtypeStruct((tokens_dev, block_cols - query_cols), jnp.bfloat16),
        ],
        in_specs=[
            pl.BlockSpec((tokens_dev, step), lambda k: (0, k)),
            pl.BlockSpec((step, block_cols), lambda k: (k, 0)),
        ],
        out_specs=[
            pl.BlockSpec((tokens_dev, query_cols), lambda k: (0, 0)),
            pl.BlockSpec((tokens_dev, block_cols - query_cols), lambda k: (0, 0)),
        ],
        scratch_shapes=[pltpu.VMEM((tokens_dev, block_cols), jnp.float32)],
        compiler_params=params,
        cost_estimate=pl.CostEstimate(
            flops=2 * tokens_dev * width * block_cols, bytes_accessed=2 * width * (tokens_dev + block_cols), transcendentals=0
        ),
        name="product",
    )(whole_tokens, weights.reshape(width, block_cols))
    return (new_master, new_first, new_second, query, key)


def solution(mesh):
    blocked = P("dp", "tensor")
    return jax.shard_map(
        per_device,
        mesh=mesh,
        in_specs=(blocked,) * 4 + (P(), P()),
        out_specs=(blocked,) * 5,
        check_vma=False,
    )
```

time: 209 us -> 193 us (0.923)
  waiting for transfers between devices: 122 us -> 12.5 us
  starting transfers between devices: 16.4 us -> 97.3 us
  Pallas kernels: 0 us -> 49.5 us
  blocking collectives: 17.7 us -> 0 us
  matrix products: 11.2 us -> 0 us
  local copies, waits for them, and re-layouts: 22.5 us -> 15.8 us
    all_gather x1 -> x0, waiting for transfers between devices: 94.8 us -> none  [per_device(): lax.all_gather(new_master.astype(jnp.bfloat16), 'dp', axis=0, tiled=True)]
    ppermute x0 -> x27, starting transfers between devices: none -> 91.2 us  [move(): return lax.ppermute(array, 'dp', moves)]
    pallas_call x0 -> x4, Pallas kernels: none -> 49.5 us  [the longest x1 31.2 us: per_device(): pl.pallas_call(functools.partial(weights_kernel, spans), grid=(SLOTS // G...]
    all_to_all x2 -> x1, waiting for transfers between devices: 23.5 us -> 0.01 us  [per_device(): lax.all_to_all(packed, 'dp', split_axis=0, concat_axis=0, tiled=True)]
    all_to_all x1 -> x0, blocking collectives: 17.7 us -> none  [per_device(): lax.all_to_all(pack(old_first).astype(jnp.bfloat16), 'dp', split_axis=0,...]
    gather x9 -> x0, local copies, waits for them, and re-layouts: 15.2 us -> none  [the longest x6 10.2 us: pack(): return jnp.where(send_valid, padded[send_index], jnp.zeros((), block.dtype))]
    ppermute x0 -> x27, waiting for transfers between devices: none -> 11.8 us  [move(): return lax.ppermute(array, 'dp', moves)]
    unnamed x8 -> x47, local copies, waits for them, and re-layouts: 1.93 us -> 13.4 us
  transfers between devices with their start and end apart: 4 -> 29, of which waited for: 4 -> 3; matrix products, arithmetic and copies ran while one was open for 12% -> 9% of each run, Pallas kernels for 0% -> 19%
where the time goes in v1:
time: 193 us; the launch traced here: 192 us
  starting transfers between devices  97.3 us (50%)
  Pallas kernels  49.5 us (26%)
  local copies, waits for them, and re-layouts  15.8 us (8%)
  between operations  14.6 us (8%)
  waiting for transfers between devices  12.5 us (6%)
  other arithmetic  2.47 us (1%)
    ppermute x27, starting transfers between devices, move(): return lax.ppermute(array, 'dp', moves)  91.2 us
    pallas_call x1, Pallas kernels, per_device(): pl.pallas_call(functools.partial(weights_kernel, spans), grid=(SLOTS // G...  31.2 us
    unnamed x47, local copies, waits for them, and re-layouts  13.4 us
    pallas_call x1, Pallas kernels, per_device(): pl.pallas_call(product_kernel, grid=(width // step,), out_shape=[jax.Shap...  13.3 us
    ppermute x27, waiting for transfers between devices, move(): return lax.ppermute(array, 'dp', moves)  11.8 us
    all_to_all x1, starting transfers between devices, per_device(): lax.all_to_all(packed, 'dp', split_axis=0, concat_axis=0, tiled=True)  6.02 us
  transfers between devices with their start and end apart: 29, of which 3 were waited for; matrix products, arithmetic and copies ran while one was open for 9% of the time, Pallas kernels for 19%

profile of v1, /device:TPU:1, one launch (start us, length us, event | category | flops | bytes accessed | tf_op | source)
XLA Modules:
  0.0 192.1 jit_solution(9553312514507214110)
XLA Ops:
  9.0 3.9 %collective-permute-start = (bf16[1,336,128]{2,1,0:T(8,128)(2,1)S(1)}, bf16[1,336,128]{2,1,0:T(8,128)(2,1)S(1)}, u32[]{:S(2)}, u32[]{:S(2)}) collective-permute-start(bf16[1,336,128]{2,1,0:T(8,128)(2,1)S(1)} %broadcast_in_dim.10), channel_id=1, source_target_pairs={{0,16},{8,24},{16,32},{24,40},{32,48},{40,56},{48,0},{56,8},{64,80... | collective-permute-start | bytes 258056 | tf_op jit(solution)/shard_map/ppermute | solution.py:42
  13.0 3.2 %collective-permute-start.1 = (bf16[1,336,128]{2,1,0:T(8,128)(2,1)S(1)}, bf16[1,336,128]{2,1,0:T(8,128)(2,1)S(1)}, u32[]{:S(2)}, u32[]{:S(2)}) collective-permute-start(bf16[1,336,128]{2,1,0:T(8,128)(2,1)S(1)} %broadcast_in_dim.10), channel_id=1, source_target_pairs={{0,48},{8,56},{16,0},{24,8},{32,16},{40,24},{48,32},{56,40},{64,11... | collective-permute-start | bytes 258056 | tf_op jit(solution)/shard_map/ppermute | solution.py:42
  20.2 3.5 %collective-permute-done.2 = bf16[1,336,128]{2,1,0:T(8,128)(2,1)S(1)} collective-permute-done((bf16[1,336,128]{2,1,0:T(8,128)(2,1)S(1)}, bf16[1,336,128]{2,1,0:T(8,128)(2,1)S(1)}, u32[]{:S(2)}, u32[]{:S(2)}) %collective-permute-start.2) | collective-permute-done | bytes 86048 | tf_op jit(solution)/shard_map/ppermute | solution.py:42
  24.4 2.9 %collective-permute-start.3 = (bf16[4,336,128]{2,1,0:T(8,128)(2,1)S(1)}, bf16[4,336,128]{2,1,0:T(8,128)(2,1)S(1)}, u32[]{:S(2)}, u32[]{:S(2)}) collective-permute-start(bf16[4,336,128]{2,1,0:T(8,128)(2,1)S(1)} %get-tuple-element.20.refs_0_), channel_id=1, source_target_pairs={{0,64},{8,72},{16,80},{24,88},{32,96},{40,104},{48,112},{56,120},{... | collective-permute-start | bytes 1032200 | tf_op jit(solution)/shard_map/ppermute | solution.py:42
  27.3 3.8 %collective-permute-start.4 = (bf16[4,336,128]{2,1,0:T(8,128)(2,1)S(1)}, bf16[4,336,128]{2,1,0:T(8,128)(2,1)S(1)}, u32[]{:S(2)}, u32[]{:S(2)}) collective-permute-start(bf16[4,336,128]{2,1,0:T(8,128)(2,1)S(1)} %get-tuple-element.20.refs_0_), channel_id=1, source_target_pairs={{0,448},{8,456},{16,464},{24,472},{32,480},{40,488},{48,496},{56,5... | collective-permute-start | bytes 1032200 | tf_op jit(solution)/shard_map/ppermute | solution.py:42
  33.2 4.6 %collective-permute-start.14 = (bf16[1,336,128]{2,1,0:T(8,128)(2,1)S(1)}, bf16[1,336,128]{2,1,0:T(8,128)(2,1)S(1)}, u32[]{:S(2)}, u32[]{:S(2)}) collective-permute-start(bf16[1,336,128]{2,1,0:T(8,128)(2,1)S(1)} %broadcast_in_dim.11), channel_id=1, source_target_pairs={{0,448},{8,456},{16,464},{24,472},{32,480},{40,488},{48,496},{56,5... | collective-permute-start | bytes 258056 | tf_op jit(solution)/shard_map/ppermute | solution.py:42
  40.3 4.6 %collective-permute-start.16 = (bf16[1,336,128]{2,1,0:T(8,128)(2,1)S(1)}, bf16[1,336,128]{2,1,0:T(8,128)(2,1)S(1)}, u32[]{:S(2)}, u32[]{:S(2)}) collective-permute-start(bf16[1,336,128]{2,1,0:T(8,128)(2,1)S(1)} %collective-permute-done.14), channel_id=1, source_target_pairs={{0,448},{8,456},{16,464},{24,472},{32,480},{40,488},{48,496},{56,5... | collective-permute-start | bytes 258056 | tf_op jit(solution)/shard_map/ppermute | solution.py:42
  48.1 2.9 %collective-permute-start.5 = (bf16[4,336,128]{2,1,0:T(8,128)(2,1)S(1)}, bf16[4,336,128]{2,1,0:T(8,128)(2,1)S(1)}, u32[]{:S(2)}, u32[]{:S(2)}) collective-permute-start(bf16[4,336,128]{2,1,0:T(8,128)(2,1)S(1)} %collective-permute-done.3.refs_1_), channel_id=1, source_target_pairs={{0,64},{8,72},{16,80},{24,88},{32,96},{40,104},{48,112},{56,120},{... | collective-permute-start | bytes 1032200 | tf_op jit(solution)/shard_map/ppermute | solution.py:42
  51.0 3.6 %collective-permute-start.6 = (bf16[4,336,128]{2,1,0:T(8,128)(2,1)S(1)}, bf16[4,336,128]{2,1,0:T(8,128)(2,1)S(1)}, u32[]{:S(2)}, u32[]{:S(2)}) collective-permute-start(bf16[4,336,128]{2,1,0:T(8,128)(2,1)S(1)} %collective-permute-done.4.refs_2_), channel_id=1, source_target_pairs={{0,448},{8,456},{16,464},{24,472},{32,480},{40,488},{48,496},{56,5... | collective-permute-start | bytes 1032200 | tf_op jit(solution)/shard_map/ppermute | solution.py:42
  55.3 3.4 %collective-permute-start.18 = (bf16[1,336,128]{2,1,0:T(8,128)(2,1)S(1)}, bf16[1,336,128]{2,1,0:T(8,128)(2,1)S(1)}, u32[]{:S(2)}, u32[]{:S(2)}) collective-permute-start(bf16[1,336,128]{2,1,0:T(8,128)(2,1)S(1)} %collective-permute-done.16), channel_id=1, source_target_pairs={{0,448},{8,456},{16,464},{24,472},{32,480},{40,488},{48,496},{56,5... | collective-permute-start | bytes 258056 | tf_op jit(solution)/shard_map/ppermute | solution.py:42
  62.5 4.4 %collective-permute-start.7 = (bf16[4,336,128]{2,1,0:T(8,128)(2,1)S(1)}, bf16[4,336,128]{2,1,0:T(8,128)(2,1)S(1)}, u32[]{:S(2)}, u32[]{:S(2)}) collective-permute-start(bf16[4,336,128]{2,1,0:T(8,128)(2,1)S(1)} %collective-permute-done.5.refs_3_), channel_id=1, source_target_pairs={{0,64},{8,72},{16,80},{24,88},{32,96},{40,104},{48,112},{56,120},{... | collective-permute-start | bytes 1032200 | tf_op jit(solution)/shard_map/ppermute | solution.py:42
  71.6 4.6 %collective-permute-start.21 = (bf16[8,336,128]{2,1,0:T(8,128)(2,1)}, bf16[8,336,128]{2,1,0:T(8,128)(2,1)S(1)}, u32[]{:S(2)}, u32[]{:S(2)}) collective-permute-start(bf16[8,336,128]{2,1,0:T(8,128)(2,1)} %constant_dynamic-update-slice_fusion.16.refs_11_), channel_id=1, source_target_pairs={{0,48},{8,56},{16,0},{24,8},{32,16},{40,24},{48,32},{56,40},{64,11... | collective-permute-start | bytes 2064392 | tf_op jit(solution)/shard_map/ppermute | solution.py:42
  77.8 3.2 %collective-permute-start.9 = (bf16[2,336,128]{2,1,0:T(8,128)(2,1)S(1)}, bf16[2,336,128]{2,1,0:T(8,128)(2,1)S(1)}, u32[]{:S(2)}, u32[]{:S(2)}) collective-permute-start(bf16[2,336,128]{2,1,0:T(8,128)(2,1)S(1)} %slice.27), channel_id=1, source_target_pairs={{0,64},{8,72},{16,80},{24,88},{32,96},{40,104},{48,112},{56,120},{... | collective-permute-start | bytes 516104 | tf_op jit(solution)/shard_map/ppermute | solution.py:42
  81.0 3.3 %collective-permute-start.10 = (bf16[2,336,128]{2,1,0:T(8,128)(2,1)S(1)}, bf16[2,336,128]{2,1,0:T(8,128)(2,1)S(1)}, u32[]{:S(2)}, u32[]{:S(2)}) collective-permute-start(bf16[2,336,128]{2,1,0:T(8,128)(2,1)S(1)} %slice.28), channel_id=1, source_target_pairs={{0,448},{8,456},{16,464},{24,472},{32,480},{40,488},{48,496},{56,5... | collective-permute-start | bytes 516104 | tf_op jit(solution)/shard_map/ppermute | solution.py:42
  89.1 12.9 %collective-permute-start.12 = (bf16[20,336,128]{2,1,0:T(8,128)(2,1)}, bf16[20,336,128]{2,1,0:T(8,128)(2,1)}, u32[]{:S(2)}, u32[]{:S(2)}) collective-permute-start(bf16[20,336,128]{2,1,0:T(8,128)(2,1)} %constant_dynamic-update-slice_fusion.10), channel_id=1, source_target_pairs={{0,8},{8,0},{16,24},{24,16},{32,40},{40,32},{48,56},{56,48},{64,72... | collective-permute-start | bytes 5160968 | tf_op jit(solution)/shard_map/ppermute | solution.py:42
  107.9 6.0 %all-to-all-start = ((bf16[64,16,256]{2,1,0:T(8,128)(2,1)}), bf16[64,16,256]{2,1,0:T(8,128)(2,1)S(1)}, u32[]{:S(2)}, u32[]{:S(2)}) async-start(bf16[64,16,256]{2,1,0:T(8,128)(2,1)} %pack.1), calls=%async_computation | async-start | bytes 1048576 | tf_op jit(solution)/shard_map/all_to_all | solution.py:251
  113.9 3.3 %collective-permute-start.22 = (bf16[4,336,128]{2,1,0:T(8,128)(2,1)S(1)}, bf16[4,336,128]{2,1,0:T(8,128)(2,1)S(1)}, u32[]{:S(2)}, u32[]{:S(2)}) collective-permute-start(bf16[4,336,128]{2,1,0:T(8,128)(2,1)S(1)} %slice.30), channel_id=1, source_target_pairs={{0,16},{8,24},{16,32},{24,40},{32,48},{40,56},{48,0},{56,8},{64,80... | collective-permute-start | bytes 1032200 | tf_op jit(solution)/shard_map/ppermute | solution.py:42
  117.3 3.2 %collective-permute-start.23 = (bf16[4,336,128]{2,1,0:T(8,128)(2,1)S(1)}, bf16[4,336,128]{2,1,0:T(8,128)(2,1)S(1)}, u32[]{:S(2)}, u32[]{:S(2)}) collective-permute-start(bf16[4,336,128]{2,1,0:T(8,128)(2,1)S(1)} %slice.31), channel_id=1, source_target_pairs={{0,48},{8,56},{16,0},{24,8},{32,16},{40,24},{48,32},{56,40},{64,11... | collective-permute-start | bytes 1032200 | tf_op jit(solution)/shard_map/ppermute | solution.py:42
  122.0 2.9 %collective-permute-start.11 = (bf16[12,336,128]{2,1,0:T(8,128)(2,1)}, bf16[12,336,128]{2,1,0:T(8,128)(2,1)S(1)}, u32[]{:S(2)}, u32[]{:S(2)}) collective-permute-start(bf16[12,336,128]{2,1,0:T(8,128)(2,1)} %constant_dynamic-update-slice_fusion.4), channel_id=1, source_target_pairs={{0,8},{8,0},{16,24},{24,16},{32,40},{40,32},{48,56},{56,48},{64,72... | collective-permute-start | bytes 3096584 | tf_op jit(solution)/shard_map/ppermute | solution.py:42
  124.9 6.4 %collective-permute-done.22.refs_14_ = bf16[4,336,128]{2,1,0:T(8,128)(2,1)S(1)} collective-permute-done((bf16[4,336,128]{2,1,0:T(8,128)(2,1)S(1)}, bf16[4,336,128]{2,1,0:T(8,128)(2,1)S(1)}, u32[]{:S(2)}, u32[]{:S(2)}) %collective-permute-start.22) | collective-permute-done | bytes 344096 | tf_op jit(solution)/shard_map/ppermute | solution.py:42
  131.3 3.0 %collective-permute-start.24 = (bf16[8,336,128]{2,1,0:T(8,128)(2,1)}, bf16[8,336,128]{2,1,0:T(8,128)(2,1)}, u32[]{:S(2)}, u32[]{:S(2)}) collective-permute-start(bf16[8,336,128]{2,1,0:T(8,128)(2,1)} %constant_dynamic-update-slice_fusion.16.refs_11_), channel_id=1, source_target_pairs={{0,8},{8,0},{16,24},{24,16},{32,40},{40,32},{48,56},{56,48},{64,72... | collective-permute-start | bytes 2064392 | tf_op jit(solution)/shard_map/ppermute | solution.py:42
  137.1 2.5 %unpack.1 = (f32[96,896]{1,0:T(8,128)}, f32[96,896]{1,0:T(8,128)}) custom-call(s32[64]{0:T(128)} %lengths.5, s32[64]{0:T(128)} %shifts.5, s32[1]{0:T(128)} %bitcast.own, bf16[64,16,256]{2,1,0:T(8,128)(2,1)} %copy-done.4), custom_call_target="tpu_custom_call" | custom-call | tf_op jit(solution)/shard_map/unpack/pallas_call | solution.py:252
  140.6 31.2 %weights.1 = (bf16[64,96,896]{2,1,0:T(8,128)(2,1)}, f32[96,896]{1,0:T(8,128)}) custom-call(s32[64]{0:T(128)} %lengths.5, s32[64]{0:T(128)} %shifts.5, s32[1]{0:T(128)} %bitcast.own, bf16[4,336,128]{2,1,0:T(8,128)(2,1)} %copy-done.14, bf16[4,336,128]{2,1,0:T(8,128)(2,1)} %copy-done.5, bf16[4,336,128]{2,1,0:T(8,128)(2,1)} %copy-done.6, ...), custom_call_target="tpu_custom_call" | custom-call | tf_op jit(solution)/shard_map/weights/pallas_call | solution.py:261
  171.9 13.3 %product.1 = (bf16[512,768]{1,0:T(8,128)(2,1)}, bf16[512,128]{1,0:T(8,128)(2,1)}) custom-call(bf16[512,6144]{1,0:T(8,128)(2,1)} %all-gather.2.cloned.1.call-done.tokens, bf16[6144,896]{1,0:T(8,128)(2,1)} %bitcast.2), custom_call_target="tpu_custom_call" | custom-call | flops 5637144576 | bytes 17301504 | tf_op jit(solution)/shard_map/product/pallas_call | solution.py:285
  (99 shorter events, 40.8 us)
Async XLA Ops:
  7.2 164.7 %all-gather.2.cloned.1.call-start = ((), (), s32[]{:S(2)}) async-start(), calls=%async_computation.1 | async-start | bytes 7077888 | tf_op jit(solution)/shard_map/all_gather | solution.py:239
  9.0 7.8 %collective-permute-start = (bf16[1,336,128]{2,1,0:T(8,128)(2,1)S(1)}, bf16[1,336,128]{2,1,0:T(8,128)(2,1)S(1)}, u32[]{:S(2)}, u32[]{:S(2)}) collective-permute-start(bf16[1,336,128]{2,1,0:T(8,128)(2,1)S(1)} %broadcast_in_dim.10), channel_id=1, source_target_pairs={{0,16},{8,24},{16,32},{24,40},{32,48},{40,56},{48,0},{56,8},{64,80... | collective-permute-start | bytes 258056 | tf_op jit(solution)/shard_map/ppermute | solution.py:42
  24.4 23.7 %collective-permute-start.3 = (bf16[4,336,128]{2,1,0:T(8,128)(2,1)S(1)}, bf16[4,336,128]{2,1,0:T(8,128)(2,1)S(1)}, u32[]{:S(2)}, u32[]{:S(2)}) collective-permute-start(bf16[4,336,128]{2,1,0:T(8,128)(2,1)S(1)} %get-tuple-element.20.refs_0_), channel_id=1, source_target_pairs={{0,64},{8,72},{16,80},{24,88},{32,96},{40,104},{48,112},{56,120},{... | collective-permute-start | bytes 1032200 | tf_op jit(solution)/shard_map/ppermute | solution.py:42
  27.3 23.7 %collective-permute-start.4 = (bf16[4,336,128]{2,1,0:T(8,128)(2,1)S(1)}, bf16[4,336,128]{2,1,0:T(8,128)(2,1)S(1)}, u32[]{:S(2)}, u32[]{:S(2)}) collective-permute-start(bf16[4,336,128]{2,1,0:T(8,128)(2,1)S(1)} %get-tuple-element.20.refs_0_), channel_id=1, source_target_pairs={{0,448},{8,456},{16,464},{24,472},{32,480},{40,488},{48,496},{56,5... | collective-permute-start | bytes 1032200 | tf_op jit(solution)/shard_map/ppermute | solution.py:42
  31.2 7.2 %collective-permute-start.13 = (bf16[1,336,128]{2,1,0:T(8,128)(2,1)S(1)}, bf16[1,336,128]{2,1,0:T(8,128)(2,1)S(1)}, u32[]{:S(2)}, u32[]{:S(2)}) collective-permute-start(bf16[1,336,128]{2,1,0:T(8,128)(2,1)S(1)} %broadcast_in_dim.11), channel_id=1, source_target_pairs={{0,64},{8,72},{16,80},{24,88},{32,96},{40,104},{48,112},{56,120},{... | collective-permute-start | bytes 258056 | tf_op jit(solution)/shard_map/ppermute | solution.py:42
  38.4 7.8 %collective-permute-start.15 = (bf16[1,336,128]{2,1,0:T(8,128)(2,1)S(1)}, bf16[1,336,128]{2,1,0:T(8,128)(2,1)S(1)}, u32[]{:S(2)}, u32[]{:S(2)}) collective-permute-start(bf16[1,336,128]{2,1,0:T(8,128)(2,1)S(1)} %collective-permute-done.13), channel_id=1, source_target_pairs={{0,64},{8,72},{16,80},{24,88},{32,96},{40,104},{48,112},{56,120},{... | collective-permute-start | bytes 258056 | tf_op jit(solution)/shard_map/ppermute | solution.py:42
  40.3 15.0 %collective-permute-start.16 = (bf16[1,336,128]{2,1,0:T(8,128)(2,1)S(1)}, bf16[1,336,128]{2,1,0:T(8,128)(2,1)S(1)}, u32[]{:S(2)}, u32[]{:S(2)}) collective-permute-start(bf16[1,336,128]{2,1,0:T(8,128)(2,1)S(1)} %collective-permute-done.14), channel_id=1, source_target_pairs={{0,448},{8,456},{16,464},{24,472},{32,480},{40,488},{48,496},{56,5... | collective-permute-start | bytes 258056 | tf_op jit(solution)/shard_map/ppermute | solution.py:42
  46.2 13.1 %collective-permute-start.17 = (bf16[1,336,128]{2,1,0:T(8,128)(2,1)S(1)}, bf16[1,336,128]{2,1,0:T(8,128)(2,1)S(1)}, u32[]{:S(2)}, u32[]{:S(2)}) collective-permute-start(bf16[1,336,128]{2,1,0:T(8,128)(2,1)S(1)} %collective-permute-done.15), channel_id=1, source_target_pairs={{0,64},{8,72},{16,80},{24,88},{32,96},{40,104},{48,112},{56,120},{... | collective-permute-start | bytes 258056 | tf_op jit(solution)/shard_map/ppermute | solution.py:42
  48.1 14.4 %collective-permute-start.5 = (bf16[4,336,128]{2,1,0:T(8,128)(2,1)S(1)}, bf16[4,336,128]{2,1,0:T(8,128)(2,1)S(1)}, u32[]{:S(2)}, u32[]{:S(2)}) collective-permute-start(bf16[4,336,128]{2,1,0:T(8,128)(2,1)S(1)} %collective-permute-done.3.refs_1_), channel_id=1, source_target_pairs={{0,64},{8,72},{16,80},{24,88},{32,96},{40,104},{48,112},{56,120},{... | collective-permute-start | bytes 1032200 | tf_op jit(solution)/shard_map/ppermute | solution.py:42
  51.0 15.9 %collective-permute-start.6 = (bf16[4,336,128]{2,1,0:T(8,128)(2,1)S(1)}, bf16[4,336,128]{2,1,0:T(8,128)(2,1)S(1)}, u32[]{:S(2)}, u32[]{:S(2)}) collective-permute-start(bf16[4,336,128]{2,1,0:T(8,128)(2,1)S(1)} %collective-permute-done.4.refs_2_), channel_id=1, source_target_pairs={{0,448},{8,456},{16,464},{24,472},{32,480},{40,488},{48,496},{56,5... | collective-permute-start | bytes 1032200 | tf_op jit(solution)/shard_map/ppermute | solution.py:42
  59.3 9.7 %collective-permute-start.19 = (bf16[1,336,128]{2,1,0:T(8,128)(2,1)S(1)}, bf16[1,336,128]{2,1,0:T(8,128)(2,1)S(1)}, u32[]{:S(2)}, u32[]{:S(2)}) collective-permute-start(bf16[1,336,128]{2,1,0:T(8,128)(2,1)S(1)} %collective-permute-done.17), channel_id=1, source_target_pairs={{0,64},{8,72},{16,80},{24,88},{32,96},{40,104},{48,112},{56,120},{... | collective-permute-start | bytes 258056 | tf_op jit(solution)/shard_map/ppermute | solution.py:42
  62.5 15.2 %collective-permute-start.7 = (bf16[4,336,128]{2,1,0:T(8,128)(2,1)S(1)}, bf16[4,336,128]{2,1,0:T(8,128)(2,1)S(1)}, u32[]{:S(2)}, u32[]{:S(2)}) collective-permute-start(bf16[4,336,128]{2,1,0:T(8,128)(2,1)S(1)} %collective-permute-done.5.refs_3_), channel_id=1, source_target_pairs={{0,64},{8,72},{16,80},{24,88},{32,96},{40,104},{48,112},{56,120},{... | collective-permute-start | bytes 1032200 | tf_op jit(solution)/shard_map/ppermute | solution.py:42
  67.0 14.0 %collective-permute-start.8 = (bf16[4,336,128]{2,1,0:T(8,128)(2,1)S(1)}, bf16[4,336,128]{2,1,0:T(8,128)(2,1)S(1)}, u32[]{:S(2)}, u32[]{:S(2)}) collective-permute-start(bf16[4,336,128]{2,1,0:T(8,128)(2,1)S(1)} %collective-permute-done.6.refs_4_), channel_id=1, source_target_pairs={{0,448},{8,456},{16,464},{24,472},{32,480},{40,488},{48,496},{56,5... | collective-permute-start | bytes 1032200 | tf_op jit(solution)/shard_map/ppermute | solution.py:42
  69.7 32.4 %collective-permute-start.20 = (bf16[8,336,128]{2,1,0:T(8,128)(2,1)}, bf16[8,336,128]{2,1,0:T(8,128)(2,1)S(1)}, u32[]{:S(2)}, u32[]{:S(2)}) collective-permute-start(bf16[8,336,128]{2,1,0:T(8,128)(2,1)} %constant_dynamic-update-slice_fusion.16.refs_11_), channel_id=1, source_target_pairs={{0,16},{8,24},{16,32},{24,40},{32,48},{40,56},{48,0},{56,8},{64,80... | collective-permute-start | bytes 2064392 | tf_op jit(solution)/shard_map/ppermute | solution.py:42
  71.6 30.5 %collective-permute-start.21 = (bf16[8,336,128]{2,1,0:T(8,128)(2,1)}, bf16[8,336,128]{2,1,0:T(8,128)(2,1)S(1)}, u32[]{:S(2)}, u32[]{:S(2)}) collective-permute-start(bf16[8,336,128]{2,1,0:T(8,128)(2,1)} %constant_dynamic-update-slice_fusion.16.refs_11_), channel_id=1, source_target_pairs={{0,48},{8,56},{16,0},{24,8},{32,16},{40,24},{48,32},{56,40},{64,11... | collective-permute-start | bytes 2064392 | tf_op jit(solution)/shard_map/ppermute | solution.py:42
  77.8 8.1 %collective-permute-start.9 = (bf16[2,336,128]{2,1,0:T(8,128)(2,1)S(1)}, bf16[2,336,128]{2,1,0:T(8,128)(2,1)S(1)}, u32[]{:S(2)}, u32[]{:S(2)}) collective-permute-start(bf16[2,336,128]{2,1,0:T(8,128)(2,1)S(1)} %slice.27), channel_id=1, source_target_pairs={{0,64},{8,72},{16,80},{24,88},{32,96},{40,104},{48,112},{56,120},{... | collective-permute-start | bytes 516104 | tf_op jit(solution)/shard_map/ppermute | solution.py:42
  81.0 7.4 %collective-permute-start.10 = (bf16[2,336,128]{2,1,0:T(8,128)(2,1)S(1)}, bf16[2,336,128]{2,1,0:T(8,128)(2,1)S(1)}, u32[]{:S(2)}, u32[]{:S(2)}) collective-permute-start(bf16[2,336,128]{2,1,0:T(8,128)(2,1)S(1)} %slice.28), channel_id=1, source_target_pairs={{0,448},{8,456},{16,464},{24,472},{32,480},{40,488},{48,496},{56,5... | collective-permute-start | bytes 516104 | tf_op jit(solution)/shard_map/ppermute | solution.py:42
  89.1 50.5 %collective-permute-start.12 = (bf16[20,336,128]{2,1,0:T(8,128)(2,1)}, bf16[20,336,128]{2,1,0:T(8,128)(2,1)}, u32[]{:S(2)}, u32[]{:S(2)}) collective-permute-start(bf16[20,336,128]{2,1,0:T(8,128)(2,1)} %constant_dynamic-update-slice_fusion.10), channel_id=1, source_target_pairs={{0,8},{8,0},{16,24},{24,16},{32,40},{40,32},{48,56},{56,48},{64,72... | collective-permute-start | bytes 5160968 | tf_op jit(solution)/shard_map/ppermute | solution.py:42
  103.6 36.1 %collective-permute-start.25 = (bf16[16,336,128]{2,1,0:T(8,128)(2,1)}, bf16[16,336,128]{2,1,0:T(8,128)(2,1)}, u32[]{:S(2)}, u32[]{:S(2)}) collective-permute-start(bf16[16,336,128]{2,1,0:T(8,128)(2,1)} %pad_maximum_fusion), channel_id=1, source_target_pairs={{0,8},{8,0},{16,24},{24,16},{32,40},{40,32},{48,56},{56,48},{64,72... | collective-permute-start | bytes 4128776 | tf_op jit(solution)/shard_map/ppermute | solution.py:42
  107.9 28.4 %all-to-all-start = ((bf16[64,16,256]{2,1,0:T(8,128)(2,1)}), bf16[64,16,256]{2,1,0:T(8,128)(2,1)S(1)}, u32[]{:S(2)}, u32[]{:S(2)}) async-start(bf16[64,16,256]{2,1,0:T(8,128)(2,1)} %pack.1), calls=%async_computation | async-start | bytes 1048576 | tf_op jit(solution)/shard_map/all_to_all | solution.py:251
  113.9 17.3 %collective-permute-start.22 = (bf16[4,336,128]{2,1,0:T(8,128)(2,1)S(1)}, bf16[4,336,128]{2,1,0:T(8,128)(2,1)S(1)}, u32[]{:S(2)}, u32[]{:S(2)}) collective-permute-start(bf16[4,336,128]{2,1,0:T(8,128)(2,1)S(1)} %slice.30), channel_id=1, source_target_pairs={{0,16},{8,24},{16,32},{24,40},{32,48},{40,56},{48,0},{56,8},{64,80... | collective-permute-start | bytes 1032200 | tf_op jit(solution)/shard_map/ppermute | solution.py:42
  117.3 17.0 %collective-permute-start.23 = (bf16[4,336,128]{2,1,0:T(8,128)(2,1)S(1)}, bf16[4,336,128]{2,1,0:T(8,128)(2,1)S(1)}, u32[]{:S(2)}, u32[]{:S(2)}) collective-permute-start(bf16[4,336,128]{2,1,0:T(8,128)(2,1)S(1)} %slice.31), channel_id=1, source_target_pairs={{0,48},{8,56},{16,0},{24,8},{32,16},{40,24},{48,32},{56,40},{64,11... | collective-permute-start | bytes 1032200 | tf_op jit(solution)/shard_map/ppermute | solution.py:42
  122.0 17.6 %collective-permute-start.11 = (bf16[12,336,128]{2,1,0:T(8,128)(2,1)}, bf16[12,336,128]{2,1,0:T(8,128)(2,1)S(1)}, u32[]{:S(2)}, u32[]{:S(2)}) collective-permute-start(bf16[12,336,128]{2,1,0:T(8,128)(2,1)} %constant_dynamic-update-slice_fusion.4), channel_id=1, source_target_pairs={{0,8},{8,0},{16,24},{24,16},{32,40},{40,32},{48,56},{56,48},{64,72... | collective-permute-start | bytes 3096584 | tf_op jit(solution)/shard_map/ppermute | solution.py:42
  131.3 8.3 %collective-permute-start.24 = (bf16[8,336,128]{2,1,0:T(8,128)(2,1)}, bf16[8,336,128]{2,1,0:T(8,128)(2,1)}, u32[]{:S(2)}, u32[]{:S(2)}) collective-permute-start(bf16[8,336,128]{2,1,0:T(8,128)(2,1)} %constant_dynamic-update-slice_fusion.16.refs_11_), channel_id=1, source_target_pairs={{0,8},{8,0},{16,24},{24,16},{32,40},{40,32},{48,56},{56,48},{64,72... | collective-permute-start | bytes 2064392 | tf_op jit(solution)/shard_map/ppermute | solution.py:42
  (20 other events, 390.5 us)
Sparse Core Ops, SparseCore 0:
  10.1 83.3 all-gather.1

commit v2 on v1

v2 whole, which is shorter than its diff:
```python
import functools

import jax
import jax.numpy as jnp
from jax import lax
from jax.experimental import pallas as pl
from jax.experimental.pallas import tpu as pltpu
from jax.sharding import PartitionSpec as P

HQ = 48
HS = 128
NX = 4
NC = 2
HEADS = 7
ROWS = 96
SLOTS = ROWS * HEADS
HALF = SLOTS // 2
BUCKET = 16
N_DP = 64
NY = N_DP // (NX * NC)
GROUP = 16 * HEADS
CHUNK = 32
N_Z = 8
P_LOW = N_DP // N_Z
VMEM_LIMIT = 56 * 1024 * 1024


def dp_index(y, x, c):
    return (y * NX + x) * NC + c


X_GROUPS = [[dp_index(y, x, c) for x in range(NX)] for y in range(NY) for c in range(NC)]
Y_GROUPS = [[dp_index(y, x, c) for y in range(NY) for c in range(NC)] for x in range(NX)]


def pack_kernel(lengths, shifts, own, first, second, out, first_rows, second_rows):
    for rows, state in ((first_rows, first), (second_rows, second)):
        for head in range(HEADS):
            rows[pl.ds(head, ROWS, stride=HEADS), :] = state[:, head * HS : (head + 1) * HS]
        rows[SLOTS : SLOTS + BUCKET, :] = jnp.zeros((BUCKET, HS), jnp.float32)
    me = own[0]

    def piece(j, start):
        target = (me + shifts[j]) & (N_DP - 1)
        out[target, :, 0:HS] = first_rows[pl.ds(start, BUCKET), :].astype(jnp.bfloat16)
        out[target, :, HS : 2 * HS] = second_rows[pl.ds(start, BUCKET), :].astype(jnp.bfloat16)
        return start + lengths[j]

    lax.fori_loop(0, N_DP, piece, jnp.int32(0))


def unpack_kernel(lengths, shifts, own, received, first, second, first_rows, second_rows):
    me = own[0]

    def piece(j, start):
        source = (me - shifts[j]) & (N_DP - 1)
        first_rows[pl.ds(start, BUCKET), :] = received[source, :, 0:HS].astype(jnp.float32)
        second_rows[pl.ds(start, BUCKET), :] = received[source, :, HS : 2 * HS].astype(jnp.float32)
        return start + lengths[j]

    lax.fori_loop(0, N_DP, piece, jnp.int32(0))
    for rows, state in ((first_rows, first), (second_rows, second)):
        for head in range(HEADS):
            state[:, head * HS : (head + 1) * HS] = rows[pl.ds(head, ROWS, stride=HEADS), :]


def product_kernel(places, lengths, shifts, own, gathered, *refs):
    tokens, (master, query, key), (held, rows, weights, total, starts, firsts, sems) = refs[:-10], refs[-10:-7], refs[-7:]
    group = pl.program_id(0)
    me, my_z = own[0], own[1]
    blocks = held.reshape(2 * N_DP, SLOTS, HS)

    def copies(g):
        slots = pl.ds(pl.multiple_of(g * GROUP, GROUP), GROUP)
        return [
            pltpu.make_async_copy(
                gathered.at[:, c, x, slots, :],
                held.at[pl.ds(again * NY, NY), x, c, slots, :],
                sems.at[g, (again * NX + x) * NC + c],
            )
            for again in range(2)
            for x in range(NX)
            for c in range(NC)
        ]

    @pl.when(group == 0)
    def _():
        for g in range(SLOTS // GROUP):
            for copy in copies(g):
                copy.start()

        def piece(j, start):
            starts[j] = start
            firsts[(start + 15) >> 4] = j
            return start + lengths[j]

        lax.fori_loop(0, N_DP, piece, jnp.int32(0))

    for copy in copies(group):
        copy.wait()

    sublane = lax.broadcasted_iota(jnp.int32, (16, HS), 0).astype(jnp.int16)

    def tile(t, carry):
        whole = group * HEADS + t
        offset = pl.multiple_of(whole * 16, 16)
        begin, end = firsts[whole], firsts[whole + 1]

        def chunk(part, carry):
            def load(j):
                base = N_DP - shifts[j] + part * CHUNK
                return [blocks[base + i, pl.ds(offset, 16), :] for i in range(CHUNK)]

            def later(j, kept):
                take = sublane >= (starts[j] - offset).astype(jnp.int16)
                return [jnp.where(take, new, old) for new, old in zip(load(j), kept)]

            kept = lax.fori_loop(begin + 1, end + 1, later, load(begin))
            for i in range(CHUNK):
                rows[part * CHUNK + i, pl.ds(pl.multiple_of(t * 16, 16), 16), :] = kept[i].astype(jnp.float32)
            return carry

        return lax.fori_loop(0, N_DP // CHUNK, chunk, carry)

    lax.fori_loop(0, HEADS, tile, jnp.int32(0))

    def spread(low, carry):
        for i, distance in enumerate(places):
            p = ((my_z + distance) & (N_Z - 1)) * P_LOW + low
            at = pl.ds(pl.multiple_of((i * P_LOW + low) * 16, 16), 16)
            for head in range(HEADS):
                weights[at, head * HS : (head + 1) * HS] = rows[p, pl.ds(head, 16, stride=HEADS), :].astype(
                    jnp.bfloat16
                )
        return carry

    lax.fori_loop(0, P_LOW, spread, jnp.int32(0))
    for head in range(HEADS):
        master[:, head * HS : (head + 1) * HS] = rows[me, pl.ds(head, 16, stride=HEADS), :]

    last = jnp.concatenate([tokens[-2][...], tokens[-1][...]], axis=0)
    columns = jnp.concatenate([block[...] for block in tokens[:-2]] + [last], axis=1)
    part = jnp.dot(columns, weights[...], preferred_element_type=jnp.float32)

    @pl.when(group == 0)
    def _():
        total[...] = part

    @pl.when(group > 0)
    def _():
        total[...] += part

    @pl.when(group == pl.num_programs(0) - 1)
    def _():
        query[...] = total[:, : query.shape[1]].astype(query.dtype)
        key[...] = total[:, query.shape[1] :].astype(key.dtype)


SMEM = pl.BlockSpec(memory_space=pltpu.SMEM)
VMEM = pl.BlockSpec(memory_space=pltpu.VMEM)


def gather_tokens(tokens):
    up = [(z, (z + 1) % N_Z) for z in range(N_Z)]
    down = [(z, (z - 1) % N_Z) for z in range(N_Z)]
    half = tokens.shape[0] // 2
    from_below, from_above = tokens, tokens
    distances, arrays = [0], [tokens]
    for distance in range(1, N_Z // 2):
        from_below = lax.ppermute(from_below, "tensor", up)
        from_above = lax.ppermute(from_above, "tensor", down)
        distances += [-distance, distance]
        arrays += [from_below, from_above]
    distances.append(N_Z // 2)
    arrays.append(lax.ppermute(from_below[:half], "tensor", up))
    arrays.append(lax.ppermute(from_above[half:], "tensor", down))
    return tuple(distances), arrays


def per_device(tokens, old_master, old_first, old_second, piece_lengths, piece_shifts):
    own = jnp.stack([lax.axis_index("dp"), lax.axis_index("tensor")]).astype(jnp.int32)
    depth_dev, block_cols = old_master.shape
    state = jax.ShapeDtypeStruct((depth_dev, block_cols), jnp.float32)
    slots = pltpu.VMEM((SLOTS + BUCKET, HS), jnp.float32)

    column = old_master.astype(jnp.bfloat16).reshape(SLOTS, HS)
    row = lax.all_gather(column, "dp", axis_index_groups=X_GROUPS, axis=0, tiled=True)
    gathered = lax.all_gather(row, "dp", axis_index_groups=Y_GROUPS, axis=0, tiled=True)
    gathered = gathered.reshape(NY, NC, NX, SLOTS, HS)

    tokens_dev, width = tokens.shape
    old = jnp.arange(width, dtype=jnp.int32)
    low, depth = old // depth_dev, old % depth_dev
    new = (depth // 16 * P_LOW + low) * 16 + depth % 16
    order = (new[:, None] == old[None, :]).astype(jnp.bfloat16)
    ordered = jnp.dot(tokens, order, preferred_element_type=jnp.float32).astype(jnp.bfloat16)
    distances, blocks = gather_tokens(ordered)

    packed = pl.pallas_call(
        pack_kernel,
        out_shape=jax.ShapeDtypeStruct((N_DP, BUCKET, 2 * HS), jnp.bfloat16),
        in_specs=[SMEM] * 3 + [VMEM] * 2,
        out_specs=VMEM,
        scratch_shapes=[slots, slots],
        name="pack",
    )(piece_lengths, piece_shifts, own, old_first, old_second)
    received = lax.all_to_all(packed, "dp", split_axis=0, concat_axis=0, tiled=True)
    new_first, new_second = pl.pallas_call(
        unpack_kernel,
        out_shape=[state, state],
        in_specs=[SMEM] * 3 + [VMEM],
        out_specs=[VMEM] * 2,
        scratch_shapes=[slots, slots],
        name="unpack",
    )(piece_lengths, piece_shifts, own, received)

    query_cols = HQ // lax.axis_size("tensor") * HS
    key_cols = block_cols - query_cols
    group_cols = P_LOW * 16
    new_master, query, key = pl.pallas_call(
        functools.partial(product_kernel, distances),
        grid=(SLOTS // GROUP,),
        out_shape=[
            state,
            jax.ShapeDtypeStruct((tokens_dev, query_cols), jnp.bfloat16),
            jax.ShapeDtypeStruct((tokens_dev, key_cols), jnp.bfloat16),
        ],
        in_specs=[SMEM] * 3
        + [pl.BlockSpec(memory_space=pl.ANY)]
        + [pl.BlockSpec((block.shape[0], group_cols), lambda g: (0, g)) for block in blocks],
        out_specs=[
            pl.BlockSpec((16, block_cols), lambda g: (g, 0)),
            pl.BlockSpec((tokens_dev, query_cols), lambda g: (0, 0)),
            pl.BlockSpec((tokens_dev, key_cols), lambda g: (0, 0)),
        ],
        scratch_shapes=[
            pltpu.VMEM((2 * NY, NX, NC, SLOTS, HS), jnp.bfloat16),
            pltpu.VMEM((N_DP, GROUP, HS), jnp.float32),
            pltpu.VMEM((N_Z * group_cols, block_cols), jnp.bfloat16),
            pltpu.VMEM((tokens_dev, block_cols), jnp.float32),
            pltpu.SMEM((N_DP,), jnp.int32),
            pltpu.SMEM((SLOTS // 16 + 8,), jnp.int32),
            pltpu.SemaphoreType.DMA((SLOTS // GROUP, 2 * NX * NC)),
        ],
        compiler_params=pltpu.CompilerParams(vmem_limit_bytes=VMEM_LIMIT),
        cost_estimate=pl.CostEstimate(
            flops=2 * tokens_dev * width * N_Z * block_cols,
            bytes_accessed=2 * width * N_Z * (tokens_dev + block_cols),
            transcendentals=0,
        ),
        name="product",
    )(piece_lengths, piece_shifts, own, gathered, *blocks)
    return (new_master, new_first, new_second, query, key)


def solution(mesh):
    blocked = P("dp", "tensor")
    return jax.shard_map(
        per_device,
        mesh=mesh,
        in_specs=(blocked,) * 4 + (P(), P()),
        out_specs=(blocked,) * 5,
        check_vma=False,
    )
```

time: 193 us -> 146 us (0.76)
  starting transfers between devices: 97.3 us -> 45.4 us
  waiting for transfers between devices: 12.5 us -> 39.2 us
  Pallas kernels: 49.5 us -> 28.8 us
  local copies, waits for them, and re-layouts: 15.8 us -> 2.75 us
  blocking collectives: 0 us -> 12.9 us
    ppermute x27 -> x8, starting transfers between devices: 91.2 us -> 32.4 us  [the longest x3 17.7 us: gather_tokens(): from_above = lax.ppermute(from_above, 'tensor', down)]
    pallas_call x2 -> x1, Pallas kernels: 44.6 us -> 23.9 us  [per_device(): pl.pallas_call(functools.partial(product_kernel, distances), grid=(SLOTS...]
    ppermute x27 -> x8, waiting for transfers between devices: 11.8 us -> 26.1 us  [the longest x3 26.1 us: gather_tokens(): from_below = lax.ppermute(from_below, 'tensor', up)]
    all_to_all x1, waiting for transfers between devices: 0.01 us -> 13 us  [per_device(): lax.all_to_all(packed, 'dp', split_axis=0, concat_axis=0, tiled=True)]
    all_gather x0 -> x1, blocking collectives: none -> 12.9 us  [per_device(): lax.all_gather(column, 'dp', axis_index_groups=X_GROUPS, axis=0, tiled=True)]
    unnamed x47 -> x16, local copies, waits for them, and re-layouts: 13.4 us -> 1.52 us
    all_to_all x1, starting transfers between devices: 6.02 us -> 13 us  [per_device(): lax.all_to_all(packed, 'dp', split_axis=0, concat_axis=0, tiled=True)]
    concatenate x3 -> x0, local copies, waits for them, and re-layouts: 2.1 us -> none  [the longest x1 0.75 us: gather_weights(): add(0, NX * NY, move(jnp.concatenate(parts[:3], axis=0), SIBLING))]
  transfers between devices with their start and end apart: 29 -> 10, of which waited for: 3 -> 3; matrix products, arithmetic and copies ran while one was open for 9% -> 2% of each run, Pallas kernels for 19% -> 3%
where the time goes in v2:
time: 146 us
  starting transfers between devices  45.4 us (31%)
  waiting for transfers between devices  39.2 us (27%)
  Pallas kernels  28.8 us (20%)
  between operations  14.3 us (10%)
  blocking collectives  12.9 us (9%)
  local copies, waits for them, and re-layouts  2.75 us (2%)
  other arithmetic  1.7 us (1%)
    ppermute x3, waiting for transfers between devices, gather_tokens(): from_below = lax.ppermute(from_below, 'tensor', up)  26.1 us
    pallas_call x1, Pallas kernels, per_device(): pl.pallas_call(functools.partial(product_kernel, distances), grid=(SLOTS...  23.9 us
    ppermute x3, starting transfers between devices, gather_tokens(): from_above = lax.ppermute(from_above, 'tensor', down)  17.7 us
    all_to_all x1, starting transfers between devices, per_device(): lax.all_to_all(packed, 'dp', split_axis=0, concat_axis=0, tiled=True)  13 us
    all_to_all x1, waiting for transfers between devices, per_device(): lax.all_to_all(packed, 'dp', split_axis=0, concat_axis=0, tiled=True)  13 us
    all_gather x1, blocking collectives, per_device(): lax.all_gather(column, 'dp', axis_index_groups=X_GROUPS, axis=0, tiled=True)  12.9 us
    ppermute x3, starting transfers between devices, gather_tokens(): from_below = lax.ppermute(from_below, 'tensor', up)  8.13 us
    ppermute x1, starting transfers between devices, gather_tokens(): arrays.append(lax.ppermute(from_above[half:], 'tensor', down))  4.57 us
  transfers between devices with their start and end apart: 10, of which 3 were waited for; matrix products, arithmetic and copies ran while one was open for 2% of the time, Pallas kernels for 3%

profile of v2, /device:TPU:1, one launch (start us, length us, event | category | flops | bytes accessed | tf_op | source)
XLA Modules:
  0.0 145.9 jit_solution(5039701712568349662)
XLA Ops:
  7.2 0.0 all-gather.2.cloned.1.call-start
  7.2 1.1 convert_element_type.9
  8.3 0.2 reshape.63
  8.5 12.9 %all_gather.6 = bf16[2688,128]{1,0:T(8,128)(2,1)} all-gather(bf16[672,128]{1,0:T(8,128)(2,1)S(1)} %reshape.63), channel_id=1, replica_groups={{0,16,32,48},{8,24,40,56},{64,80,96,112},{72,88,104,120},{128,144,160,1..., dimensions={0}, use_global_device_ids=true | all-gather | bytes 860160 | tf_op jit(solution)/shard_map/all_gather | solution.py:187
  21.4 1.0 fusion.2.refs_0_
  22.4 4.3 %collective-permute-start = (bf16[512,768]{1,0:T(8,128)(2,1)S(1)}, bf16[512,768]{1,0:T(8,128)(2,1)S(1)}, u32[]{:S(2)}, u32[]{:S(2)}) collective-permute-start(bf16[512,768]{1,0:T(8,128)(2,1)S(1)} %fusion.2.refs_0_), channel_id=1, source_target_pairs={{0,1},{1,2},{2,3},{3,4},{4,5},{5,6},{6,7},{7,0},{8,9},{9,10},{10,1... | collective-permute-start | bytes 2359304 | tf_op jit(solution)/shard_map/ppermute | solution.py:170
  26.7 8.6 %collective-permute-start.1 = (bf16[512,768]{1,0:T(8,128)(2,1)S(1)}, bf16[512,768]{1,0:T(8,128)(2,1)S(1)}, u32[]{:S(2)}, u32[]{:S(2)}) collective-permute-start(bf16[512,768]{1,0:T(8,128)(2,1)S(1)} %fusion.2.refs_0_), channel_id=1, source_target_pairs={{0,7},{1,0},{2,1},{3,2},{4,3},{5,4},{6,5},{7,6},{8,15},{9,8},{10,9... | collective-permute-start | bytes 2359304 | tf_op jit(solution)/shard_map/ppermute | solution.py:171
  35.3 13.5 %collective-permute-done.refs_1_ = bf16[512,768]{1,0:T(8,128)(2,1)S(1)} collective-permute-done((bf16[512,768]{1,0:T(8,128)(2,1)S(1)}, bf16[512,768]{1,0:T(8,128)(2,1)S(1)}, u32[]{:S(2)}, u32[]{:S(2)}) %collective-permute-start) | collective-permute-done | bytes 786464 | tf_op jit(solution)/shard_map/ppermute | solution.py:170
  48.8 1.9 %collective-permute-start.2 = (bf16[512,768]{1,0:T(8,128)(2,1)S(1)}, bf16[512,768]{1,0:T(8,128)(2,1)S(1)}, u32[]{:S(2)}, u32[]{:S(2)}) collective-permute-start(bf16[512,768]{1,0:T(8,128)(2,1)S(1)} %collective-permute-done.refs_1_), channel_id=1, source_target_pairs={{0,1},{1,2},{2,3},{3,4},{4,5},{5,6},{6,7},{7,0},{8,9},{9,10},{10,1... | collective-permute-start | bytes 2359304 | tf_op jit(solution)/shard_map/ppermute | solution.py:170
  50.7 4.6 %collective-permute-start.3 = (bf16[512,768]{1,0:T(8,128)(2,1)S(1)}, bf16[512,768]{1,0:T(8,128)(2,1)}, u32[]{:S(2)}, u32[]{:S(2)}) collective-permute-start(bf16[512,768]{1,0:T(8,128)(2,1)S(1)} %collective-permute-done.1.refs_2_), channel_id=1, source_target_pairs={{0,7},{1,0},{2,1},{3,2},{4,3},{5,4},{6,5},{7,6},{8,15},{9,8},{10,9... | collective-permute-start | bytes 2359304 | tf_op jit(solution)/shard_map/ppermute | solution.py:171
  55.3 12.6 %collective-permute-done.2.refs_3_ = bf16[512,768]{1,0:T(8,128)(2,1)S(1)} collective-permute-done((bf16[512,768]{1,0:T(8,128)(2,1)S(1)}, bf16[512,768]{1,0:T(8,128)(2,1)S(1)}, u32[]{:S(2)}, u32[]{:S(2)}) %collective-permute-start.2) | collective-permute-done | bytes 786464 | tf_op jit(solution)/shard_map/ppermute | solution.py:170
  67.9 1.9 %collective-permute-start.4 = (bf16[512,768]{1,0:T(8,128)(2,1)S(1)}, bf16[512,768]{1,0:T(8,128)(2,1)S(1)}, u32[]{:S(2)}, u32[]{:S(2)}) collective-permute-start(bf16[512,768]{1,0:T(8,128)(2,1)S(1)} %collective-permute-done.2.refs_3_), channel_id=1, source_target_pairs={{0,1},{1,2},{2,3},{3,4},{4,5},{5,6},{6,7},{7,0},{8,9},{9,10},{10,1... | collective-permute-start | bytes 2359304 | tf_op jit(solution)/shard_map/ppermute | solution.py:170
  69.9 4.6 %collective-permute-start.5 = (bf16[512,768]{1,0:T(8,128)(2,1)}, bf16[512,768]{1,0:T(8,128)(2,1)}, u32[]{:S(2)}, u32[]{:S(2)}) collective-permute-start(bf16[512,768]{1,0:T(8,128)(2,1)} %collective-permute-done.3.refs_4_), channel_id=1, source_target_pairs={{0,7},{1,0},{2,1},{3,2},{4,3},{5,4},{6,5},{7,6},{8,15},{9,8},{10,9... | collective-permute-start | bytes 2359304 | tf_op jit(solution)/shard_map/ppermute | solution.py:171
  74.5 0.6 pad_add_fusion.own
  75.1 2.4 %pack.1 = bf16[64,16,256]{2,1,0:T(8,128)(2,1)} custom-call(s32[64]{0:T(128)} %lengths.5, s32[64]{0:T(128)} %shifts.5, s32[2]{0:T(128)} %pad_add_fusion.own, f32[96,896]{1,0:T(8,128)} %first.1, f32[96,896]{1,0:T(8,128)} %second.1), custom_call_target="tpu_custom_call" | custom-call | tf_op jit(solution)/shard_map/pack/pallas_call | solution.py:199
  77.5 13.0 %all-to-all-start = ((bf16[64,16,256]{2,1,0:T(8,128)(2,1)}), bf16[64,16,256]{2,1,0:T(8,128)(2,1)S(1)}, u32[]{:S(2)}, u32[]{:S(2)}) async-start(bf16[64,16,256]{2,1,0:T(8,128)(2,1)} %pack.1), calls=%async_computation | async-start | bytes 1048576 | tf_op jit(solution)/shard_map/all_to_all | solution.py:207
  90.5 1.9 %collective-permute-start.6 = (bf16[256,768]{1,0:T(8,128)(2,1)S(1)}, bf16[256,768]{1,0:T(8,128)(2,1)S(1)}, u32[]{:S(2)}, u32[]{:S(2)}) collective-permute-start(bf16[256,768]{1,0:T(8,128)(2,1)S(1)} %slice.8), channel_id=1, source_target_pairs={{0,1},{1,2},{2,3},{3,4},{4,5},{5,6},{6,7},{7,0},{8,9},{9,10},{10,1... | collective-permute-start | bytes 1179656 | tf_op jit(solution)/shard_map/ppermute | solution.py:175
  92.5 1.0 slice.9
  93.5 4.6 %collective-permute-start.7 = (bf16[256,768]{1,0:T(8,128)(2,1)S(1)}, bf16[256,768]{1,0:T(8,128)(2,1)}, u32[]{:S(2)}, u32[]{:S(2)}) collective-permute-start(bf16[256,768]{1,0:T(8,128)(2,1)S(1)} %slice.9), channel_id=1, source_target_pairs={{0,7},{1,0},{2,1},{3,2},{4,3},{5,4},{6,5},{7,6},{8,15},{9,8},{10,9... | collective-permute-start | bytes 1179656 | tf_op jit(solution)/shard_map/ppermute | solution.py:176
  98.1 13.0 %all-to-all-done.received = bf16[64,16,256]{2,1,0:T(8,128)(2,1)S(1)} async-done(((bf16[64,16,256]{2,1,0:T(8,128)(2,1)}), bf16[64,16,256]{2,1,0:T(8,128)(2,1)S(1)}, u32[]{:S(2)}, u32[]{:S(2)}) %all-to-all-start) | async-done | bytes 524320 | tf_op jit(solution)/shard_map/all_to_all | solution.py:207
  111.1 0.8 copy-done.1
  111.9 2.5 %unpack.1 = (f32[96,896]{1,0:T(8,128)}, f32[96,896]{1,0:T(8,128)}) custom-call(s32[64]{0:T(128)} %lengths.5, s32[64]{0:T(128)} %shifts.5, s32[2]{0:T(128)} %pad_add_fusion.own, bf16[64,16,256]{2,1,0:T(8,128)(2,1)} %copy-done.1), custom_call_target="tpu_custom_call" | custom-call | tf_op jit(solution)/shard_map/unpack/pallas_call | solution.py:208
  114.5 0.7 copy-done.7
  115.2 23.9 %product.1 = (f32[96,896]{1,0:T(8,128)}, bf16[512,768]{1,0:T(8,128)(2,1)}, bf16[512,128]{1,0:T(8,128)(2,1)}) custom-call(s32[64]{0:T(128)} %lengths.5, s32[64]{0:T(128)} %shifts.5, s32[2]{0:T(128)} %pad_add_fusion.own, bf16[8,2,4,672,128]{4,3,2,1,0:T(8,128)(2,1)} %bitcast.6, bf16[512,768]{1,0:T(8,128)(2,1)} %copy-done.3, bf16[512,768]{1,0:T(8,128)(2,1)} %copy-done.4, ...), custom_call_target="tpu_custom_call" | custom-call | flops 5637144576 | bytes 17301504 | tf_op jit(solution)/shard_map/product/pallas_call | solution.py:220
  (24 shorter events, 0.1 us)
Async XLA Ops:
  7.2 14.2 %copy-start = (bf16[512,768]{1,0:T(8,128)(2,1)S(1)}, bf16[512,768]{1,0:T(8,128)(2,1)}, u32[]{:S(2)}) copy-start(bf16[512,768]{1,0:T(8,128)(2,1)} %param.6) | copy-start | bytes 2359300
  7.2 107.3 %all-gather.2.cloned.1.call-start = ((), (), s32[]{:S(2)}) async-start(), calls=%async_computation.1 | async-start | bytes 11698176 | tf_op jit(solution)/shard_map/all_gather | solution.py:188
  22.4 32.9 %copy-start.3 = (bf16[512,768]{1,0:T(8,128)(2,1)}, bf16[512,768]{1,0:T(8,128)(2,1)S(1)}, u32[]{:S(2)}) copy-start(bf16[512,768]{1,0:T(8,128)(2,1)S(1)} %fusion.2.refs_0_) | copy-start | bytes 2359300
  22.4 26.4 %collective-permute-start = (bf16[512,768]{1,0:T(8,128)(2,1)S(1)}, bf16[512,768]{1,0:T(8,128)(2,1)S(1)}, u32[]{:S(2)}, u32[]{:S(2)}) collective-permute-start(bf16[512,768]{1,0:T(8,128)(2,1)S(1)} %fusion.2.refs_0_), channel_id=1, source_target_pairs={{0,1},{1,2},{2,3},{3,4},{4,5},{5,6},{6,7},{7,0},{8,9},{9,10},{10,1... | collective-permute-start | bytes 2359304 | tf_op jit(solution)/shard_map/ppermute | solution.py:170
  26.7 24.0 %collective-permute-start.1 = (bf16[512,768]{1,0:T(8,128)(2,1)S(1)}, bf16[512,768]{1,0:T(8,128)(2,1)S(1)}, u32[]{:S(2)}, u32[]{:S(2)}) collective-permute-start(bf16[512,768]{1,0:T(8,128)(2,1)S(1)} %fusion.2.refs_0_), channel_id=1, source_target_pairs={{0,7},{1,0},{2,1},{3,2},{4,3},{5,4},{6,5},{7,6},{8,15},{9,8},{10,9... | collective-permute-start | bytes 2359304 | tf_op jit(solution)/shard_map/ppermute | solution.py:171
  48.8 19.2 %copy-start.4 = (bf16[512,768]{1,0:T(8,128)(2,1)}, bf16[512,768]{1,0:T(8,128)(2,1)S(1)}, u32[]{:S(2)}) copy-start(bf16[512,768]{1,0:T(8,128)(2,1)S(1)} %collective-permute-done.refs_1_) | copy-start | bytes 2359300
  48.8 19.2 %collective-permute-start.2 = (bf16[512,768]{1,0:T(8,128)(2,1)S(1)}, bf16[512,768]{1,0:T(8,128)(2,1)S(1)}, u32[]{:S(2)}, u32[]{:S(2)}) collective-permute-start(bf16[512,768]{1,0:T(8,128)(2,1)S(1)} %collective-permute-done.refs_1_), channel_id=1, source_target_pairs={{0,1},{1,2},{2,3},{3,4},{4,5},{5,6},{6,7},{7,0},{8,9},{9,10},{10,1... | collective-permute-start | bytes 2359304 | tf_op jit(solution)/shard_map/ppermute | solution.py:170
  50.7 19.2 %copy-start.5 = (bf16[512,768]{1,0:T(8,128)(2,1)}, bf16[512,768]{1,0:T(8,128)(2,1)S(1)}, u32[]{:S(2)}) copy-start(bf16[512,768]{1,0:T(8,128)(2,1)S(1)} %collective-permute-done.1.refs_2_) | copy-start | bytes 2359300
  50.7 19.2 %collective-permute-start.3 = (bf16[512,768]{1,0:T(8,128)(2,1)S(1)}, bf16[512,768]{1,0:T(8,128)(2,1)}, u32[]{:S(2)}, u32[]{:S(2)}) collective-permute-start(bf16[512,768]{1,0:T(8,128)(2,1)S(1)} %collective-permute-done.1.refs_2_), channel_id=1, source_target_pairs={{0,7},{1,0},{2,1},{3,2},{4,3},{5,4},{6,5},{7,6},{8,15},{9,8},{10,9... | collective-permute-start | bytes 2359304 | tf_op jit(solution)/shard_map/ppermute | solution.py:171
  67.9 22.5 %copy-start.6 = (bf16[512,768]{1,0:T(8,128)(2,1)}, bf16[512,768]{1,0:T(8,128)(2,1)S(1)}, u32[]{:S(2)}) copy-start(bf16[512,768]{1,0:T(8,128)(2,1)S(1)} %collective-permute-done.2.refs_3_) | copy-start | bytes 2359300
  67.9 22.5 %collective-permute-start.4 = (bf16[512,768]{1,0:T(8,128)(2,1)S(1)}, bf16[512,768]{1,0:T(8,128)(2,1)S(1)}, u32[]{:S(2)}, u32[]{:S(2)}) collective-permute-start(bf16[512,768]{1,0:T(8,128)(2,1)S(1)} %collective-permute-done.2.refs_3_), channel_id=1, source_target_pairs={{0,1},{1,2},{2,3},{3,4},{4,5},{5,6},{6,7},{7,0},{8,9},{9,10},{10,1... | collective-permute-start | bytes 2359304 | tf_op jit(solution)/shard_map/ppermute | solution.py:170
  69.9 22.6 %collective-permute-start.5 = (bf16[512,768]{1,0:T(8,128)(2,1)}, bf16[512,768]{1,0:T(8,128)(2,1)}, u32[]{:S(2)}, u32[]{:S(2)}) collective-permute-start(bf16[512,768]{1,0:T(8,128)(2,1)} %collective-permute-done.3.refs_4_), channel_id=1, source_target_pairs={{0,7},{1,0},{2,1},{3,2},{4,3},{5,4},{6,5},{7,6},{8,15},{9,8},{10,9... | collective-permute-start | bytes 2359304 | tf_op jit(solution)/shard_map/ppermute | solution.py:171
  77.5 33.6 %all-to-all-start = ((bf16[64,16,256]{2,1,0:T(8,128)(2,1)}), bf16[64,16,256]{2,1,0:T(8,128)(2,1)S(1)}, u32[]{:S(2)}, u32[]{:S(2)}) async-start(bf16[64,16,256]{2,1,0:T(8,128)(2,1)} %pack.1), calls=%async_computation | async-start | bytes 1048576 | tf_op jit(solution)/shard_map/all_to_all | solution.py:207
  90.5 24.0 %copy-start.2 = (bf16[512,768]{1,0:T(8,128)(2,1)}, bf16[512,768]{1,0:T(8,128)(2,1)S(1)}, u32[]{:S(2)}) copy-start(bf16[512,768]{1,0:T(8,128)(2,1)S(1)} %collective-permute-done.4.refs_5_) | copy-start | bytes 2359300
  90.5 23.9 %collective-permute-start.6 = (bf16[256,768]{1,0:T(8,128)(2,1)S(1)}, bf16[256,768]{1,0:T(8,128)(2,1)S(1)}, u32[]{:S(2)}, u32[]{:S(2)}) collective-permute-start(bf16[256,768]{1,0:T(8,128)(2,1)S(1)} %slice.8), channel_id=1, source_target_pairs={{0,1},{1,2},{2,3},{3,4},{4,5},{5,6},{6,7},{7,0},{8,9},{9,10},{10,1... | collective-permute-start | bytes 1179656 | tf_op jit(solution)/shard_map/ppermute | solution.py:175
  93.5 20.9 %collective-permute-start.7 = (bf16[256,768]{1,0:T(8,128)(2,1)S(1)}, bf16[256,768]{1,0:T(8,128)(2,1)}, u32[]{:S(2)}, u32[]{:S(2)}) collective-permute-start(bf16[256,768]{1,0:T(8,128)(2,1)S(1)} %slice.9), channel_id=1, source_target_pairs={{0,7},{1,0},{2,1},{3,2},{4,3},{5,4},{6,5},{7,6},{8,15},{9,8},{10,9... | collective-permute-start | bytes 1179656 | tf_op jit(solution)/shard_map/ppermute | solution.py:176
  111.1 0.8 copy-start.1
  114.4 0.7 copy-start.7
Sparse Core Ops, SparseCore 0:
  21.5 85.3 all-gather.1

commit v3 on v2

--- a/solution.py
+++ b/solution.py
@@ -9,28 +9,18 @@
 
 HQ = 48
 HS = 128
-NX = 4
-NC = 2
 HEADS = 7
 ROWS = 96
 SLOTS = ROWS * HEADS
 HALF = SLOTS // 2
 BUCKET = 16
 N_DP = 64
-NY = N_DP // (NX * NC)
-GROUP = 16 * HEADS
+GROUP_ROWS = 32
+GROUP = GROUP_ROWS * HEADS
 CHUNK = 32
 N_Z = 8
 P_LOW = N_DP // N_Z
 VMEM_LIMIT = 56 * 1024 * 1024
-
-
-def dp_index(y, x, c):
-    return (y * NX + x) * NC + c
-
-
-X_GROUPS = [[dp_index(y, x, c) for x in range(NX)] for y in range(NY) for c in range(NC)]
-Y_GROUPS = [[dp_index(y, x, c) for y in range(NY) for c in range(NC)] for x in range(NX)]
 
 
 def pack_kernel(lengths, shifts, own, first, second, out, first_rows, second_rows):
@@ -65,22 +55,16 @@
 
 
 def product_kernel(places, lengths, shifts, own, gathered, *refs):
-    tokens, (master, query, key), (held, rows, weights, total, starts, firsts, sems) = refs[:-10], refs[-10:-7], refs[-7:]
+    tokens, (master, query, key), (blocks, rows, weights, total, starts, firsts, sems) = refs[:-10], refs[-10:-7], refs[-7:]
     group = pl.program_id(0)
     me, my_z = own[0], own[1]
-    blocks = held.reshape(2 * N_DP, SLOTS, HS)
-
     def copies(g):
         slots = pl.ds(pl.multiple_of(g * GROUP, GROUP), GROUP)
         return [
             pltpu.make_async_copy(
-                gathered.at[:, c, x, slots, :],
-                held.at[pl.ds(again * NY, NY), x, c, slots, :],
-                sems.at[g, (again * NX + x) * NC + c],
+                gathered.at[:, slots, :], blocks.at[pl.ds(again * N_DP, N_DP), slots, :], sems.at[g, again]
             )
             for again in range(2)
-            for x in range(NX)
-            for c in range(NC)
         ]
 
     @pl.when(group == 0)
@@ -102,7 +86,7 @@
     sublane = lax.broadcasted_iota(jnp.int32, (16, HS), 0).astype(jnp.int16)
 
     def tile(t, carry):
-        whole = group * HEADS + t
+        whole = group * (GROUP // 16) + t
         offset = pl.multiple_of(whole * 16, 16)
         begin, end = firsts[whole], firsts[whole + 1]
 
@@ -122,21 +106,21 @@
 
         return lax.fori_loop(0, N_DP // CHUNK, chunk, carry)
 
-    lax.fori_loop(0, HEADS, tile, jnp.int32(0))
+    lax.fori_loop(0, GROUP // 16, tile, jnp.int32(0))
 
     def spread(low, carry):
         for i, distance in enumerate(places):
             p = ((my_z + distance) & (N_Z - 1)) * P_LOW + low
-            at = pl.ds(pl.multiple_of((i * P_LOW + low) * 16, 16), 16)
+            at = pl.ds(pl.multiple_of((i * P_LOW + low) * GROUP_ROWS, GROUP_ROWS), GROUP_ROWS)
             for head in range(HEADS):
-                weights[at, head * HS : (head + 1) * HS] = rows[p, pl.ds(head, 16, stride=HEADS), :].astype(
+                weights[at, head * HS : (head + 1) * HS] = rows[p, pl.ds(head, GROUP_ROWS, stride=HEADS), :].astype(
                     jnp.bfloat16
                 )
         return carry
 
     lax.fori_loop(0, P_LOW, spread, jnp.int32(0))
     for head in range(HEADS):
-        master[:, head * HS : (head + 1) * HS] = rows[me, pl.ds(head, 16, stride=HEADS), :]
+        master[:, head * HS : (head + 1) * HS] = rows[me, pl.ds(head, GROUP_ROWS, stride=HEADS), :]
 
     last = jnp.concatenate([tokens[-2][...], tokens[-1][...]], axis=0)
     columns = jnp.concatenate([block[...] for block in tokens[:-2]] + [last], axis=1)
@@ -184,14 +168,12 @@
     slots = pltpu.VMEM((SLOTS + BUCKET, HS), jnp.float32)
 
     column = old_master.astype(jnp.bfloat16).reshape(SLOTS, HS)
-    row = lax.all_gather(column, "dp", axis_index_groups=X_GROUPS, axis=0, tiled=True)
-    gathered = lax.all_gather(row, "dp", axis_index_groups=Y_GROUPS, axis=0, tiled=True)
-    gathered = gathered.reshape(NY, NC, NX, SLOTS, HS)
+    gathered = lax.all_gather(column, "dp")
 
     tokens_dev, width = tokens.shape
     old = jnp.arange(width, dtype=jnp.int32)
     low, depth = old // depth_dev, old % depth_dev
-    new = (depth // 16 * P_LOW + low) * 16 + depth % 16
+    new = (depth // GROUP_ROWS * P_LOW + low) * GROUP_ROWS + depth % GROUP_ROWS
     order = (new[:, None] == old[None, :]).astype(jnp.bfloat16)
     ordered = jnp.dot(tokens, order, preferred_element_type=jnp.float32).astype(jnp.bfloat16)
     distances, blocks = gather_tokens(ordered)
@@ -216,7 +198,7 @@
 
     query_cols = HQ // lax.axis_size("tensor") * HS
     key_cols = block_cols - query_cols
-    group_cols = P_LOW * 16
+    group_cols = P_LOW * GROUP_ROWS
     new_master, query, key = pl.pallas_call(
         functools.partial(product_kernel, distances),
         grid=(SLOTS // GROUP,),
@@ -229,18 +211,18 @@
         + [pl.BlockSpec(memory_space=pl.ANY)]
         + [pl.BlockSpec((block.shape[0], group_cols), lambda g: (0, g)) for block in blocks],
         out_specs=[
-            pl.BlockSpec((16, block_cols), lambda g: (g, 0)),
+            pl.BlockSpec((GROUP_ROWS, block_cols), lambda g: (g, 0)),
             pl.BlockSpec((tokens_dev, query_cols), lambda g: (0, 0)),
             pl.BlockSpec((tokens_dev, key_cols), lambda g: (0, 0)),
         ],
         scratch_shapes=[
-            pltpu.VMEM((2 * NY, NX, NC, SLOTS, HS), jnp.bfloat16),
+            pltpu.VMEM((2 * N_DP, SLOTS, HS), jnp.bfloat16),
             pltpu.VMEM((N_DP, GROUP, HS), jnp.float32),
             pltpu.VMEM((N_Z * group_cols, block_cols), jnp.bfloat16),
             pltpu.VMEM((tokens_dev, block_cols), jnp.float32),
             pltpu.SMEM((N_DP,), jnp.int32),
             pltpu.SMEM((SLOTS // 16 + 8,), jnp.int32),
-            pltpu.SemaphoreType.DMA((SLOTS // GROUP, 2 * NX * NC)),
+            pltpu.SemaphoreType.DMA((SLOTS // GROUP, 2)),
         ],
         compiler_params=pltpu.CompilerParams(vmem_limit_bytes=VMEM_LIMIT),
         cost_estimate=pl.CostEstimate(

time: 146 us -> 150 us (1.027)
  waiting for transfers between devices: 39.2 us -> 56.4 us
  blocking collectives: 12.9 us -> 0 us
    all_gather x1 -> x0, blocking collectives: 12.9 us -> none  [per_device(): lax.all_gather(column, 'dp', axis_index_groups=X_GROUPS, axis=0, tiled=True)]
    all_gather x1, waiting for transfers between devices: 0.02 us -> 11.3 us  [per_device(): gathered = lax.all_gather(column, 'dp')]
    ppermute x3, waiting for transfers between devices: 26.1 us -> 29.7 us  [gather_tokens(): from_below = lax.ppermute(from_below, 'tensor', up)]
    all_to_all x1, waiting for transfers between devices: 13 us -> 15.4 us  [per_device(): lax.all_to_all(packed, 'dp', split_axis=0, concat_axis=0, tiled=True)]
  transfers between devices with their start and end apart: 10 -> 10, of which waited for: 3 -> 4; matrix products, arithmetic and copies ran while one was open for 2% -> 2% of each run, Pallas kernels for 3% -> 3%
where the time goes in v3:
time: 150 us; the launch traced here: 149 us
  waiting for transfers between devices  56.4 us (38%)
  starting transfers between devices  45.7 us (30%)
  Pallas kernels  27.5 us (18%)
  between operations  14.2 us (9%)
  local copies, waits for them, and re-layouts  2.82 us (2%)
  other arithmetic  1.64 us (1%)
    ppermute x3, waiting for transfers between devices, gather_tokens(): from_below = lax.ppermute(from_below, 'tensor', up)  29.7 us
    pallas_call x1, Pallas kernels, per_device(): pl.pallas_call(functools.partial(product_kernel, distances), grid=(SLOTS...  22.6 us
    ppermute x3, starting transfers between devices, gather_tokens(): from_above = lax.ppermute(from_above, 'tensor', down)  17.7 us
    all_to_all x1, waiting for transfers between devices, per_device(): lax.all_to_all(packed, 'dp', split_axis=0, concat_axis=0, tiled=True)  15.4 us
    all_to_all x1, starting transfers between devices, per_device(): lax.all_to_all(packed, 'dp', split_axis=0, concat_axis=0, tiled=True)  12.8 us
    all_gather x1, waiting for transfers between devices, per_device(): gathered = lax.all_gather(column, 'dp')  11.3 us
    ppermute x3, starting transfers between devices, gather_tokens(): from_below = lax.ppermute(from_below, 'tensor', up)  8.65 us
    ppermute x1, starting transfers between devices, gather_tokens(): arrays.append(lax.ppermute(from_above[half:], 'tensor', down))  4.49 us
  transfers between devices with their start and end apart: 10, of which 4 were waited for; matrix products, arithmetic and copies ran while one was open for 2% of the time, Pallas kernels for 3%

profile of v3, /device:TPU:1, one launch (start us, length us, event | category | flops | bytes accessed | tf_op | source)
XLA Modules:
  0.0 149.2 jit_solution(5837845817464523754)
XLA Ops:
  7.2 0.0 all-gather.2.cloned.1.call-start
  7.2 1.1 convert_element_type.9
  8.3 0.9 all_gather_reshape.3
  9.1 0.0 all-gather.2.cloned.1.call-update
  9.2 1.0 fusion.2.refs_0_
  10.2 4.8 %collective-permute-start = (bf16[512,768]{1,0:T(8,128)(2,1)S(1)}, bf16[512,768]{1,0:T(8,128)(2,1)S(1)}, u32[]{:S(2)}, u32[]{:S(2)}) collective-permute-start(bf16[512,768]{1,0:T(8,128)(2,1)S(1)} %fusion.2.refs_0_), channel_id=1, source_target_pairs={{0,1},{1,2},{2,3},{3,4},{4,5},{5,6},{6,7},{7,0},{8,9},{9,10},{10,1... | collective-permute-start | bytes 2359304 | tf_op jit(solution)/shard_map/ppermute | solution.py:154
  15.0 8.6 %collective-permute-start.1 = (bf16[512,768]{1,0:T(8,128)(2,1)S(1)}, bf16[512,768]{1,0:T(8,128)(2,1)S(1)}, u32[]{:S(2)}, u32[]{:S(2)}) collective-permute-start(bf16[512,768]{1,0:T(8,128)(2,1)S(1)} %fusion.2.refs_0_), channel_id=1, source_target_pairs={{0,7},{1,0},{2,1},{3,2},{4,3},{5,4},{6,5},{7,6},{8,15},{9,8},{10,9... | collective-permute-start | bytes 2359304 | tf_op jit(solution)/shard_map/ppermute | solution.py:155
  23.6 15.3 %collective-permute-done.refs_1_ = bf16[512,768]{1,0:T(8,128)(2,1)S(1)} collective-permute-done((bf16[512,768]{1,0:T(8,128)(2,1)S(1)}, bf16[512,768]{1,0:T(8,128)(2,1)S(1)}, u32[]{:S(2)}, u32[]{:S(2)}) %collective-permute-start) | collective-permute-done | bytes 786464 | tf_op jit(solution)/shard_map/ppermute | solution.py:154
  38.9 1.9 %collective-permute-start.2 = (bf16[512,768]{1,0:T(8,128)(2,1)S(1)}, bf16[512,768]{1,0:T(8,128)(2,1)S(1)}, u32[]{:S(2)}, u32[]{:S(2)}) collective-permute-start(bf16[512,768]{1,0:T(8,128)(2,1)S(1)} %collective-permute-done.refs_1_), channel_id=1, source_target_pairs={{0,1},{1,2},{2,3},{3,4},{4,5},{5,6},{6,7},{7,0},{8,9},{9,10},{10,1... | collective-permute-start | bytes 2359304 | tf_op jit(solution)/shard_map/ppermute | solution.py:154
  40.9 4.6 %collective-permute-start.3 = (bf16[512,768]{1,0:T(8,128)(2,1)S(1)}, bf16[512,768]{1,0:T(8,128)(2,1)}, u32[]{:S(2)}, u32[]{:S(2)}) collective-permute-start(bf16[512,768]{1,0:T(8,128)(2,1)S(1)} %collective-permute-done.1.refs_2_), channel_id=1, source_target_pairs={{0,7},{1,0},{2,1},{3,2},{4,3},{5,4},{6,5},{7,6},{8,15},{9,8},{10,9... | collective-permute-start | bytes 2359304 | tf_op jit(solution)/shard_map/ppermute | solution.py:155
  45.5 14.4 %collective-permute-done.2.refs_3_ = bf16[512,768]{1,0:T(8,128)(2,1)S(1)} collective-permute-done((bf16[512,768]{1,0:T(8,128)(2,1)S(1)}, bf16[512,768]{1,0:T(8,128)(2,1)S(1)}, u32[]{:S(2)}, u32[]{:S(2)}) %collective-permute-start.2) | collective-permute-done | bytes 786464 | tf_op jit(solution)/shard_map/ppermute | solution.py:154
  59.8 1.9 %collective-permute-start.4 = (bf16[512,768]{1,0:T(8,128)(2,1)S(1)}, bf16[512,768]{1,0:T(8,128)(2,1)S(1)}, u32[]{:S(2)}, u32[]{:S(2)}) collective-permute-start(bf16[512,768]{1,0:T(8,128)(2,1)S(1)} %collective-permute-done.2.refs_3_), channel_id=1, source_target_pairs={{0,1},{1,2},{2,3},{3,4},{4,5},{5,6},{6,7},{7,0},{8,9},{9,10},{10,1... | collective-permute-start | bytes 2359304 | tf_op jit(solution)/shard_map/ppermute | solution.py:154
  61.8 4.6 %collective-permute-start.5 = (bf16[512,768]{1,0:T(8,128)(2,1)}, bf16[512,768]{1,0:T(8,128)(2,1)}, u32[]{:S(2)}, u32[]{:S(2)}) collective-permute-start(bf16[512,768]{1,0:T(8,128)(2,1)} %collective-permute-done.3.refs_4_), channel_id=1, source_target_pairs={{0,7},{1,0},{2,1},{3,2},{4,3},{5,4},{6,5},{7,6},{8,15},{9,8},{10,9... | collective-permute-start | bytes 2359304 | tf_op jit(solution)/shard_map/ppermute | solution.py:155
  66.4 0.6 pad_add_fusion.own
  66.9 2.4 %pack.1 = bf16[64,16,256]{2,1,0:T(8,128)(2,1)} custom-call(s32[64]{0:T(128)} %lengths.5, s32[64]{0:T(128)} %shifts.5, s32[2]{0:T(128)} %pad_add_fusion.own, f32[96,896]{1,0:T(8,128)} %first.1, f32[96,896]{1,0:T(8,128)} %second.1), custom_call_target="tpu_custom_call" | custom-call | tf_op jit(solution)/shard_map/pack/pallas_call | solution.py:181
  69.3 12.8 %all-to-all-start = ((bf16[64,16,256]{2,1,0:T(8,128)(2,1)}), bf16[64,16,256]{2,1,0:T(8,128)(2,1)S(1)}, u32[]{:S(2)}, u32[]{:S(2)}) async-start(bf16[64,16,256]{2,1,0:T(8,128)(2,1)} %pack.1), calls=%async_computation | async-start | bytes 1048576 | tf_op jit(solution)/shard_map/all_to_all | solution.py:189
  82.2 1.9 %collective-permute-start.6 = (bf16[256,768]{1,0:T(8,128)(2,1)S(1)}, bf16[256,768]{1,0:T(8,128)(2,1)S(1)}, u32[]{:S(2)}, u32[]{:S(2)}) collective-permute-start(bf16[256,768]{1,0:T(8,128)(2,1)S(1)} %slice.8), channel_id=1, source_target_pairs={{0,1},{1,2},{2,3},{3,4},{4,5},{5,6},{6,7},{7,0},{8,9},{9,10},{10,1... | collective-permute-start | bytes 1179656 | tf_op jit(solution)/shard_map/ppermute | solution.py:159
  84.1 1.1 slice.9
  85.2 4.5 %collective-permute-start.7 = (bf16[256,768]{1,0:T(8,128)(2,1)S(1)}, bf16[256,768]{1,0:T(8,128)(2,1)}, u32[]{:S(2)}, u32[]{:S(2)}) collective-permute-start(bf16[256,768]{1,0:T(8,128)(2,1)S(1)} %slice.9), channel_id=1, source_target_pairs={{0,7},{1,0},{2,1},{3,2},{4,3},{5,4},{6,5},{7,6},{8,15},{9,8},{10,9... | collective-permute-start | bytes 1179656 | tf_op jit(solution)/shard_map/ppermute | solution.py:160
  89.7 15.4 %all-to-all-done.received = bf16[64,16,256]{2,1,0:T(8,128)(2,1)S(1)} async-done(((bf16[64,16,256]{2,1,0:T(8,128)(2,1)}), bf16[64,16,256]{2,1,0:T(8,128)(2,1)S(1)}, u32[]{:S(2)}, u32[]{:S(2)}) %all-to-all-start) | async-done | bytes 524320 | tf_op jit(solution)/shard_map/all_to_all | solution.py:189
  105.1 0.8 copy-done.1
  105.9 2.5 %unpack.1 = (f32[96,896]{1,0:T(8,128)}, f32[96,896]{1,0:T(8,128)}) custom-call(s32[64]{0:T(128)} %lengths.5, s32[64]{0:T(128)} %shifts.5, s32[2]{0:T(128)} %pad_add_fusion.own, bf16[64,16,256]{2,1,0:T(8,128)(2,1)} %copy-done.1), custom_call_target="tpu_custom_call" | custom-call | tf_op jit(solution)/shard_map/unpack/pallas_call | solution.py:190
  108.5 11.3 %all-gather.2.cloned.1.call-done.gathered = bf16[64,672,128]{2,1,0:T(8,128)(2,1)} async-done(((bf16[1,672,128]{2,1,0:T(8,128)(2,1)}), bf16[64,672,128]{2,1,0:T(8,128)(2,1)}) %all-gather.2.cloned.1.call-update) | async-done | bytes 11010064 | tf_op jit(solution)/shard_map/all_gather | solution.py:171
  119.7 22.6 %product.1 = (f32[96,896]{1,0:T(8,128)}, bf16[512,768]{1,0:T(8,128)(2,1)}, bf16[512,128]{1,0:T(8,128)(2,1)}) custom-call(s32[64]{0:T(128)} %lengths.5, s32[64]{0:T(128)} %shifts.5, s32[2]{0:T(128)} %pad_add_fusion.own, bf16[64,672,128]{2,1,0:T(8,128)(2,1)} %all-gather.2.cloned.1.call-done.gathered, bf16[512,768]{1,0:T(8,128)(2,1)} %copy-done.3, ...), custom_call_target="tpu_custom_call" | custom-call | flops 5637144576 | bytes 17301504 | tf_op jit(solution)/shard_map/product/pallas_call | solution.py:202
  (23 shorter events, 0.1 us)
Async XLA Ops:
  7.2 2.0 %copy-start = (bf16[512,768]{1,0:T(8,128)(2,1)S(1)}, bf16[512,768]{1,0:T(8,128)(2,1)}, u32[]{:S(2)}) copy-start(bf16[512,768]{1,0:T(8,128)(2,1)} %param.6) | copy-start | bytes 2359300
  7.2 112.5 %all-gather.2.cloned.1.call-start = ((), (), s32[]{:S(2)}) async-start(), calls=%async_computation.1 | async-start | bytes 11182080 | tf_op jit(solution)/shard_map/all_gather | solution.py:171
  10.2 35.3 %copy-start.3 = (bf16[512,768]{1,0:T(8,128)(2,1)}, bf16[512,768]{1,0:T(8,128)(2,1)S(1)}, u32[]{:S(2)}) copy-start(bf16[512,768]{1,0:T(8,128)(2,1)S(1)} %fusion.2.refs_0_) | copy-start | bytes 2359300
  10.2 28.8 %collective-permute-start = (bf16[512,768]{1,0:T(8,128)(2,1)S(1)}, bf16[512,768]{1,0:T(8,128)(2,1)S(1)}, u32[]{:S(2)}, u32[]{:S(2)}) collective-permute-start(bf16[512,768]{1,0:T(8,128)(2,1)S(1)} %fusion.2.refs_0_), channel_id=1, source_target_pairs={{0,1},{1,2},{2,3},{3,4},{4,5},{5,6},{6,7},{7,0},{8,9},{9,10},{10,1... | collective-permute-start | bytes 2359304 | tf_op jit(solution)/shard_map/ppermute | solution.py:154
  15.0 25.8 %collective-permute-start.1 = (bf16[512,768]{1,0:T(8,128)(2,1)S(1)}, bf16[512,768]{1,0:T(8,128)(2,1)S(1)}, u32[]{:S(2)}, u32[]{:S(2)}) collective-permute-start(bf16[512,768]{1,0:T(8,128)(2,1)S(1)} %fusion.2.refs_0_), channel_id=1, source_target_pairs={{0,7},{1,0},{2,1},{3,2},{4,3},{5,4},{6,5},{7,6},{8,15},{9,8},{10,9... | collective-permute-start | bytes 2359304 | tf_op jit(solution)/shard_map/ppermute | solution.py:155
  38.9 20.9 %copy-start.4 = (bf16[512,768]{1,0:T(8,128)(2,1)}, bf16[512,768]{1,0:T(8,128)(2,1)S(1)}, u32[]{:S(2)}) copy-start(bf16[512,768]{1,0:T(8,128)(2,1)S(1)} %collective-permute-done.refs_1_) | copy-start | bytes 2359300
  38.9 20.9 %collective-permute-start.2 = (bf16[512,768]{1,0:T(8,128)(2,1)S(1)}, bf16[512,768]{1,0:T(8,128)(2,1)S(1)}, u32[]{:S(2)}, u32[]{:S(2)}) collective-permute-start(bf16[512,768]{1,0:T(8,128)(2,1)S(1)} %collective-permute-done.refs_1_), channel_id=1, source_target_pairs={{0,1},{1,2},{2,3},{3,4},{4,5},{5,6},{6,7},{7,0},{8,9},{9,10},{10,1... | collective-permute-start | bytes 2359304 | tf_op jit(solution)/shard_map/ppermute | solution.py:154
  40.9 20.9 %copy-start.5 = (bf16[512,768]{1,0:T(8,128)(2,1)}, bf16[512,768]{1,0:T(8,128)(2,1)S(1)}, u32[]{:S(2)}) copy-start(bf16[512,768]{1,0:T(8,128)(2,1)S(1)} %collective-permute-done.1.refs_2_) | copy-start | bytes 2359300
  40.9 20.9 %collective-permute-start.3 = (bf16[512,768]{1,0:T(8,128)(2,1)S(1)}, bf16[512,768]{1,0:T(8,128)(2,1)}, u32[]{:S(2)}, u32[]{:S(2)}) collective-permute-start(bf16[512,768]{1,0:T(8,128)(2,1)S(1)} %collective-permute-done.1.refs_2_), channel_id=1, source_target_pairs={{0,7},{1,0},{2,1},{3,2},{4,3},{5,4},{6,5},{7,6},{8,15},{9,8},{10,9... | collective-permute-start | bytes 2359304 | tf_op jit(solution)/shard_map/ppermute | solution.py:155
  59.8 22.3 %copy-start.6 = (bf16[512,768]{1,0:T(8,128)(2,1)}, bf16[512,768]{1,0:T(8,128)(2,1)S(1)}, u32[]{:S(2)}) copy-start(bf16[512,768]{1,0:T(8,128)(2,1)S(1)} %collective-permute-done.2.refs_3_) | copy-start | bytes 2359300
  59.8 22.3 %collective-permute-start.4 = (bf16[512,768]{1,0:T(8,128)(2,1)S(1)}, bf16[512,768]{1,0:T(8,128)(2,1)S(1)}, u32[]{:S(2)}, u32[]{:S(2)}) collective-permute-start(bf16[512,768]{1,0:T(8,128)(2,1)S(1)} %collective-permute-done.2.refs_3_), channel_id=1, source_target_pairs={{0,1},{1,2},{2,3},{3,4},{4,5},{5,6},{6,7},{7,0},{8,9},{9,10},{10,1... | collective-permute-start | bytes 2359304 | tf_op jit(solution)/shard_map/ppermute | solution.py:154
  61.8 22.3 %collective-permute-start.5 = (bf16[512,768]{1,0:T(8,128)(2,1)}, bf16[512,768]{1,0:T(8,128)(2,1)}, u32[]{:S(2)}, u32[]{:S(2)}) collective-permute-start(bf16[512,768]{1,0:T(8,128)(2,1)} %collective-permute-done.3.refs_4_), channel_id=1, source_target_pairs={{0,7},{1,0},{2,1},{3,2},{4,3},{5,4},{6,5},{7,6},{8,15},{9,8},{10,9... | collective-permute-start | bytes 2359304 | tf_op jit(solution)/shard_map/ppermute | solution.py:155
  69.3 35.8 %all-to-all-start = ((bf16[64,16,256]{2,1,0:T(8,128)(2,1)}), bf16[64,16,256]{2,1,0:T(8,128)(2,1)S(1)}, u32[]{:S(2)}, u32[]{:S(2)}) async-start(bf16[64,16,256]{2,1,0:T(8,128)(2,1)} %pack.1), calls=%async_computation | async-start | bytes 1048576 | tf_op jit(solution)/shard_map/all_to_all | solution.py:189
  82.2 37.6 %copy-start.2 = (bf16[512,768]{1,0:T(8,128)(2,1)}, bf16[512,768]{1,0:T(8,128)(2,1)S(1)}, u32[]{:S(2)}) copy-start(bf16[512,768]{1,0:T(8,128)(2,1)S(1)} %collective-permute-done.4.refs_5_) | copy-start | bytes 2359300
  82.2 26.2 %collective-permute-start.6 = (bf16[256,768]{1,0:T(8,128)(2,1)S(1)}, bf16[256,768]{1,0:T(8,128)(2,1)S(1)}, u32[]{:S(2)}, u32[]{:S(2)}) collective-permute-start(bf16[256,768]{1,0:T(8,128)(2,1)S(1)} %slice.8), channel_id=1, source_target_pairs={{0,1},{1,2},{2,3},{3,4},{4,5},{5,6},{6,7},{7,0},{8,9},{9,10},{10,1... | collective-permute-start | bytes 1179656 | tf_op jit(solution)/shard_map/ppermute | solution.py:159
  85.2 23.2 %collective-permute-start.7 = (bf16[256,768]{1,0:T(8,128)(2,1)S(1)}, bf16[256,768]{1,0:T(8,128)(2,1)}, u32[]{:S(2)}, u32[]{:S(2)}) collective-permute-start(bf16[256,768]{1,0:T(8,128)(2,1)S(1)} %slice.9), channel_id=1, source_target_pairs={{0,7},{1,0},{2,1},{3,2},{4,3},{5,4},{6,5},{7,6},{8,15},{9,8},{10,9... | collective-permute-start | bytes 1179656 | tf_op jit(solution)/shard_map/ppermute | solution.py:160
  105.1 0.8 copy-start.1
  108.4 11.3 %copy-start.7 = (bf16[256,768]{1,0:T(8,128)(2,1)}, bf16[256,768]{1,0:T(8,128)(2,1)S(1)}, u32[]{:S(2)}) copy-start(bf16[256,768]{1,0:T(8,128)(2,1)S(1)} %collective-permute-done.6.refs_7_) | copy-start | bytes 1179652
Sparse Core Ops, SparseCore 0:
  11.9 107.7 all-gather.1

commit v4 on v2

--- a/solution.py
+++ b/solution.py
@@ -18,7 +18,9 @@
 BUCKET = 16
 N_DP = 64
 NY = N_DP // (NX * NC)
-GROUP = 16 * HEADS
+GROUP_ROWS = 32
+GROUP = GROUP_ROWS * HEADS
+GROUPS = SLOTS // GROUP
 CHUNK = 32
 N_Z = 8
 P_LOW = N_DP // N_Z
@@ -33,7 +35,7 @@
 Y_GROUPS = [[dp_index(y, x, c) for y in range(NY) for c in range(NC)] for x in range(NX)]
 
 
-def pack_kernel(lengths, shifts, own, first, second, out, first_rows, second_rows):
+def pack_kernel(lengths, shifts, own, first, second, after, out, first_rows, second_rows):
     for rows, state in ((first_rows, first), (second_rows, second)):
         for head in range(HEADS):
             rows[pl.ds(head, ROWS, stride=HEADS), :] = state[:, head * HS : (head + 1) * HS]
@@ -49,7 +51,7 @@
     lax.fori_loop(0, N_DP, piece, jnp.int32(0))
 
 
-def unpack_kernel(lengths, shifts, own, received, first, second, first_rows, second_rows):
+def unpack_kernel(lengths, shifts, own, received, after, first, second, first_rows, second_rows):
     me = own[0]
 
     def piece(j, start):
@@ -85,7 +87,7 @@
 
     @pl.when(group == 0)
     def _():
-        for g in range(SLOTS // GROUP):
+        for g in range(GROUPS):
             for copy in copies(g):
                 copy.start()
 
@@ -102,7 +104,7 @@
     sublane = lax.broadcasted_iota(jnp.int32, (16, HS), 0).astype(jnp.int16)
 
     def tile(t, carry):
-        whole = group * HEADS + t
+        whole = group * (GROUP // 16) + t
         offset = pl.multiple_of(whole * 16, 16)
         begin, end = firsts[whole], firsts[whole + 1]
 
@@ -122,21 +124,21 @@
 
         return lax.fori_loop(0, N_DP // CHUNK, chunk, carry)
 
-    lax.fori_loop(0, HEADS, tile, jnp.int32(0))
+    lax.fori_loop(0, GROUP // 16, tile, jnp.int32(0))
 
     def spread(low, carry):
         for i, distance in enumerate(places):
             p = ((my_z + distance) & (N_Z - 1)) * P_LOW + low
-            at = pl.ds(pl.multiple_of((i * P_LOW + low) * 16, 16), 16)
+            at = pl.ds(pl.multiple_of((i * P_LOW + low) * GROUP_ROWS, GROUP_ROWS), GROUP_ROWS)
             for head in range(HEADS):
-                weights[at, head * HS : (head + 1) * HS] = rows[p, pl.ds(head, 16, stride=HEADS), :].astype(
+                weights[at, head * HS : (head + 1) * HS] = rows[p, pl.ds(head, GROUP_ROWS, stride=HEADS), :].astype(
                     jnp.bfloat16
                 )
         return carry
 
     lax.fori_loop(0, P_LOW, spread, jnp.int32(0))
     for head in range(HEADS):
-        master[:, head * HS : (head + 1) * HS] = rows[me, pl.ds(head, 16, stride=HEADS), :]
+        master[:, head * HS : (head + 1) * HS] = rows[me, pl.ds(head, GROUP_ROWS, stride=HEADS), :]
 
     last = jnp.concatenate([tokens[-2][...], tokens[-1][...]], axis=0)
     columns = jnp.concatenate([block[...] for block in tokens[:-2]] + [last], axis=1)
@@ -158,6 +160,7 @@
 
 SMEM = pl.BlockSpec(memory_space=pltpu.SMEM)
 VMEM = pl.BlockSpec(memory_space=pltpu.VMEM)
+ANY = pl.BlockSpec(memory_space=pl.ANY)
 
 
 def gather_tokens(tokens):
@@ -191,7 +194,7 @@
     tokens_dev, width = tokens.shape
     old = jnp.arange(width, dtype=jnp.int32)
     low, depth = old // depth_dev, old % depth_dev
-    new = (depth // 16 * P_LOW + low) * 16 + depth % 16
+    new = (depth // GROUP_ROWS * P_LOW + low) * GROUP_ROWS + depth % GROUP_ROWS
     order = (new[:, None] == old[None, :]).astype(jnp.bfloat16)
     ordered = jnp.dot(tokens, order, preferred_element_type=jnp.float32).astype(jnp.bfloat16)
     distances, blocks = gather_tokens(ordered)
@@ -199,27 +202,18 @@
     packed = pl.pallas_call(
         pack_kernel,
         out_shape=jax.ShapeDtypeStruct((N_DP, BUCKET, 2 * HS), jnp.bfloat16),
-        in_specs=[SMEM] * 3 + [VMEM] * 2,
+        in_specs=[SMEM] * 3 + [VMEM] * 2 + [ANY],
         out_specs=VMEM,
         scratch_shapes=[slots, slots],
         name="pack",
-    )(piece_lengths, piece_shifts, own, old_first, old_second)
+    )(piece_lengths, piece_shifts, own, old_first, old_second, blocks[-1])
     received = lax.all_to_all(packed, "dp", split_axis=0, concat_axis=0, tiled=True)
-    new_first, new_second = pl.pallas_call(
-        unpack_kernel,
-        out_shape=[state, state],
-        in_specs=[SMEM] * 3 + [VMEM],
-        out_specs=[VMEM] * 2,
-        scratch_shapes=[slots, slots],
-        name="unpack",
-    )(piece_lengths, piece_shifts, own, received)
-
     query_cols = HQ // lax.axis_size("tensor") * HS
     key_cols = block_cols - query_cols
-    group_cols = P_LOW * 16
+    group_cols = P_LOW * GROUP_ROWS
     new_master, query, key = pl.pallas_call(
         functools.partial(product_kernel, distances),
-        grid=(SLOTS // GROUP,),
+        grid=(GROUPS,),
         out_shape=[
             state,
             jax.ShapeDtypeStruct((tokens_dev, query_cols), jnp.bfloat16),
@@ -229,7 +223,7 @@
         + [pl.BlockSpec(memory_space=pl.ANY)]
         + [pl.BlockSpec((block.shape[0], group_cols), lambda g: (0, g)) for block in blocks],
         out_specs=[
-            pl.BlockSpec((16, block_cols), lambda g: (g, 0)),
+            pl.BlockSpec((GROUP_ROWS, block_cols), lambda g: (g, 0)),
             pl.BlockSpec((tokens_dev, query_cols), lambda g: (0, 0)),
             pl.BlockSpec((tokens_dev, key_cols), lambda g: (0, 0)),
         ],
@@ -240,7 +234,7 @@
             pltpu.VMEM((tokens_dev, block_cols), jnp.float32),
             pltpu.SMEM((N_DP,), jnp.int32),
             pltpu.SMEM((SLOTS // 16 + 8,), jnp.int32),
-            pltpu.SemaphoreType.DMA((SLOTS // GROUP, 2 * NX * NC)),
+            pltpu.SemaphoreType.DMA((GROUPS, 2 * NX * NC)),
         ],
         compiler_params=pltpu.CompilerParams(vmem_limit_bytes=VMEM_LIMIT),
         cost_estimate=pl.CostEstimate(
@@ -250,6 +244,15 @@
         ),
         name="product",
     )(piece_lengths, piece_shifts, own, gathered, *blocks)
+    new_first, new_second = pl.pallas_call(
+        unpack_kernel,
+        out_shape=[state, state],
+        in_specs=[SMEM] * 3 + [VMEM, ANY],
+        out_specs=[VMEM] * 2,
+        scratch_shapes=[slots, slots],
+        name="unpack",
+    )(piece_lengths, piece_shifts, own, received, key)
+
     return (new_master, new_first, new_second, query, key)
 
 

time: 146 us -> 161 us (1.10)
  waiting for transfers between devices: 39.2 us -> 51.1 us
  starting transfers between devices: 45.4 us -> 49.3 us
    ppermute x3, waiting for transfers between devices: 0.01 us -> 34.5 us  [gather_tokens(): from_above = lax.ppermute(from_above, 'tensor', down)]
    ppermute x3, waiting for transfers between devices: 26.1 us -> 0.01 us  [gather_tokens(): from_below = lax.ppermute(from_below, 'tensor', up)]
    all_to_all x1, waiting for transfers between devices: 13 us -> 0.01 us  [per_device(): lax.all_to_all(packed, 'dp', split_axis=0, concat_axis=0, tiled=True)]
    ppermute x1, waiting for transfers between devices: 0.01 us -> 12.5 us  [gather_tokens(): arrays.append(lax.ppermute(from_below[:half], 'tensor', up))]
    ppermute x1, waiting for transfers between devices: 0.01 us -> 4.09 us  [gather_tokens(): arrays.append(lax.ppermute(from_above[half:], 'tensor', down))]
    ppermute x3, starting transfers between devices: 17.7 us -> 21.8 us  [gather_tokens(): from_above = lax.ppermute(from_above, 'tensor', down)]
    ppermute x3, starting transfers between devices: 8.13 us -> 5.76 us  [gather_tokens(): from_below = lax.ppermute(from_below, 'tensor', up)]
  transfers between devices with their start and end apart: 10 -> 10, of which waited for: 3 -> 5; matrix products, arithmetic and copies ran while one was open for 2% -> 1% of each run, Pallas kernels for 3% -> 16%
where the time goes in v4:
time: 161 us
  waiting for transfers between devices  51.1 us (32%)
  starting transfers between devices  49.3 us (31%)
  Pallas kernels  27.9 us (17%)
  between operations  14.3 us (9%)
  blocking collectives  12.9 us (8%)
  local copies, waits for them, and re-layouts  2.59 us (2%)
  other arithmetic  1.68 us (1%)
    ppermute x3, waiting for transfers between devices, gather_tokens(): from_above = lax.ppermute(from_above, 'tensor', down)  34.5 us
    pallas_call x1, Pallas kernels, per_device(): pl.pallas_call(functools.partial(product_kernel, distances), grid=(GROUPS...  23 us
    ppermute x3, starting transfers between devices, gather_tokens(): from_above = lax.ppermute(from_above, 'tensor', down)  21.8 us
    all_to_all x1, starting transfers between devices, per_device(): lax.all_to_all(packed, 'dp', split_axis=0, concat_axis=0, tiled=True)  14.4 us
    all_gather x1, blocking collectives, per_device(): lax.all_gather(column, 'dp', axis_index_groups=X_GROUPS, axis=0, tiled=True)  12.9 us
    ppermute x1, waiting for transfers between devices, gather_tokens(): arrays.append(lax.ppermute(from_below[:half], 'tensor', up))  12.5 us
    ppermute x3, starting transfers between devices, gather_tokens(): from_below = lax.ppermute(from_below, 'tensor', up)  5.76 us
    ppermute x1, starting transfers between devices, gather_tokens(): arrays.append(lax.ppermute(from_above[half:], 'tensor', down))  5.42 us
  transfers between devices with their start and end apart: 10, of which 5 were waited for; matrix products, arithmetic and copies ran while one was open for 1% of the time, Pallas kernels for 16%

profile of v4, /device:TPU:1, one launch (start us, length us, event | category | flops | bytes accessed | tf_op | source)
XLA Modules:
  0.0 160.7 jit_solution(17045650971388850715)
XLA Ops:
  7.2 1.1 convert_element_type.9
  8.5 12.9 %all_gather.6 = bf16[2688,128]{1,0:T(8,128)(2,1)} all-gather(bf16[672,128]{1,0:T(8,128)(2,1)S(1)} %reshape.63), channel_id=1, replica_groups={{0,16,32,48},{8,24,40,56},{64,80,96,112},{72,88,104,120},{128,144,160,1..., dimensions={0}, use_global_device_ids=true | all-gather | bytes 860160 | tf_op jit(solution)/shard_map/all_gather | solution.py:190
  21.4 1.0 fusion.2.refs_0_
  22.4 11.0 %collective-permute-start.1 = (bf16[512,768]{1,0:T(8,128)(2,1)S(1)}, bf16[512,768]{1,0:T(8,128)(2,1)S(1)}, u32[]{:S(2)}, u32[]{:S(2)}) collective-permute-start(bf16[512,768]{1,0:T(8,128)(2,1)S(1)} %fusion.2.refs_0_), channel_id=1, source_target_pairs={{0,7},{1,0},{2,1},{3,2},{4,3},{5,4},{6,5},{7,6},{8,15},{9,8},{10,9... | collective-permute-start | bytes 2359304 | tf_op jit(solution)/shard_map/ppermute | solution.py:174
  33.4 1.9 %collective-permute-start = (bf16[512,768]{1,0:T(8,128)(2,1)S(1)}, bf16[512,768]{1,0:T(8,128)(2,1)S(1)}, u32[]{:S(2)}, u32[]{:S(2)}) collective-permute-start(bf16[512,768]{1,0:T(8,128)(2,1)S(1)} %fusion.2.refs_0_), channel_id=1, source_target_pairs={{0,1},{1,2},{2,3},{3,4},{4,5},{5,6},{6,7},{7,0},{8,9},{9,10},{10,1... | collective-permute-start | bytes 2359304 | tf_op jit(solution)/shard_map/ppermute | solution.py:173
  35.3 12.3 %collective-permute-done.1.refs_2_ = bf16[512,768]{1,0:T(8,128)(2,1)S(1)} collective-permute-done((bf16[512,768]{1,0:T(8,128)(2,1)S(1)}, bf16[512,768]{1,0:T(8,128)(2,1)S(1)}, u32[]{:S(2)}, u32[]{:S(2)}) %collective-permute-start.1) | collective-permute-done | bytes 786464 | tf_op jit(solution)/shard_map/ppermute | solution.py:174
  47.7 5.4 %collective-permute-start.3 = (bf16[512,768]{1,0:T(8,128)(2,1)S(1)}, bf16[512,768]{1,0:T(8,128)(2,1)S(1)}, u32[]{:S(2)}, u32[]{:S(2)}) collective-permute-start(bf16[512,768]{1,0:T(8,128)(2,1)S(1)} %collective-permute-done.1.refs_2_), channel_id=1, source_target_pairs={{0,7},{1,0},{2,1},{3,2},{4,3},{5,4},{6,5},{7,6},{8,15},{9,8},{10,9... | collective-permute-start | bytes 2359304 | tf_op jit(solution)/shard_map/ppermute | solution.py:174
  53.1 1.9 %collective-permute-start.2 = (bf16[512,768]{1,0:T(8,128)(2,1)S(1)}, bf16[512,768]{1,0:T(8,128)(2,1)}, u32[]{:S(2)}, u32[]{:S(2)}) collective-permute-start(bf16[512,768]{1,0:T(8,128)(2,1)S(1)} %collective-permute-done.refs_1_), channel_id=1, source_target_pairs={{0,1},{1,2},{2,3},{3,4},{4,5},{5,6},{6,7},{7,0},{8,9},{9,10},{10,1... | collective-permute-start | bytes 2359304 | tf_op jit(solution)/shard_map/ppermute | solution.py:173
  55.0 11.5 %collective-permute-done.3.refs_4_ = bf16[512,768]{1,0:T(8,128)(2,1)S(1)} collective-permute-done((bf16[512,768]{1,0:T(8,128)(2,1)S(1)}, bf16[512,768]{1,0:T(8,128)(2,1)S(1)}, u32[]{:S(2)}, u32[]{:S(2)}) %collective-permute-start.3) | collective-permute-done | bytes 786464 | tf_op jit(solution)/shard_map/ppermute | solution.py:174
  66.5 5.4 %collective-permute-start.5 = (bf16[512,768]{1,0:T(8,128)(2,1)S(1)}, bf16[512,768]{1,0:T(8,128)(2,1)S(1)}, u32[]{:S(2)}, u32[]{:S(2)}) collective-permute-start(bf16[512,768]{1,0:T(8,128)(2,1)S(1)} %collective-permute-done.3.refs_4_), channel_id=1, source_target_pairs={{0,7},{1,0},{2,1},{3,2},{4,3},{5,4},{6,5},{7,6},{8,15},{9,8},{10,9... | collective-permute-start | bytes 2359304 | tf_op jit(solution)/shard_map/ppermute | solution.py:174
  72.0 1.9 %collective-permute-start.4 = (bf16[512,768]{1,0:T(8,128)(2,1)}, bf16[512,768]{1,0:T(8,128)(2,1)S(1)}, u32[]{:S(2)}, u32[]{:S(2)}) collective-permute-start(bf16[512,768]{1,0:T(8,128)(2,1)} %collective-permute-done.2.refs_3_), channel_id=1, source_target_pairs={{0,1},{1,2},{2,3},{3,4},{4,5},{5,6},{6,7},{7,0},{8,9},{9,10},{10,1... | collective-permute-start | bytes 2359304 | tf_op jit(solution)/shard_map/ppermute | solution.py:173
  73.9 10.7 %collective-permute-done.5.refs_6_ = bf16[512,768]{1,0:T(8,128)(2,1)S(1)} collective-permute-done((bf16[512,768]{1,0:T(8,128)(2,1)S(1)}, bf16[512,768]{1,0:T(8,128)(2,1)S(1)}, u32[]{:S(2)}, u32[]{:S(2)}) %collective-permute-start.5) | collective-permute-done | bytes 786464 | tf_op jit(solution)/shard_map/ppermute | solution.py:174
  84.6 5.4 %collective-permute-start.7 = (bf16[256,768]{1,0:T(8,128)(2,1)S(1)}, bf16[256,768]{1,0:T(8,128)(2,1)S(1)}, u32[]{:S(2)}, u32[]{:S(2)}) collective-permute-start(bf16[256,768]{1,0:T(8,128)(2,1)S(1)} %slice.9), channel_id=1, source_target_pairs={{0,7},{1,0},{2,1},{3,2},{4,3},{5,4},{6,5},{7,6},{8,15},{9,8},{10,9... | collective-permute-start | bytes 1179656 | tf_op jit(solution)/shard_map/ppermute | solution.py:179
  90.1 0.6 pad_add_fusion.own
  90.7 4.1 %collective-permute-done.7.refs_8_.after = bf16[256,768]{1,0:T(8,128)(2,1)S(1)} collective-permute-done((bf16[256,768]{1,0:T(8,128)(2,1)S(1)}, bf16[256,768]{1,0:T(8,128)(2,1)S(1)}, u32[]{:S(2)}, u32[]{:S(2)}) %collective-permute-start.7) | collective-permute-done | bytes 393248 | tf_op jit(solution)/shard_map/ppermute | solution.py:179
  94.8 0.8 copy-done.2
  95.5 2.4 %pack.1 = bf16[64,16,256]{2,1,0:T(8,128)(2,1)} custom-call(s32[64]{0:T(128)} %lengths.5, s32[64]{0:T(128)} %shifts.5, s32[2]{0:T(128)} %pad_add_fusion.own, f32[96,896]{1,0:T(8,128)} %first.1, f32[96,896]{1,0:T(8,128)} %second.1, bf16[256,768]{1,0:T(8,128)(2,1)} %copy-done.2), custom_call_target="tpu_custom_call" | custom-call | tf_op jit(solution)/shard_map/pack/pallas_call | solution.py:202
  97.9 14.4 %all-to-all-start = ((bf16[64,16,256]{2,1,0:T(8,128)(2,1)}), bf16[64,16,256]{2,1,0:T(8,128)(2,1)S(1)}, u32[]{:S(2)}, u32[]{:S(2)}) async-start(bf16[64,16,256]{2,1,0:T(8,128)(2,1)} %pack.1), calls=%async_computation | async-start | bytes 1048576 | tf_op jit(solution)/shard_map/all_to_all | solution.py:210
  112.4 1.9 %collective-permute-start.6 = (bf16[256,768]{1,0:T(8,128)(2,1)S(1)}, bf16[256,768]{1,0:T(8,128)(2,1)S(1)}, u32[]{:S(2)}, u32[]{:S(2)}) collective-permute-start(bf16[256,768]{1,0:T(8,128)(2,1)S(1)} %slice.8), channel_id=1, source_target_pairs={{0,1},{1,2},{2,3},{3,4},{4,5},{5,6},{6,7},{7,0},{8,9},{9,10},{10,1... | collective-permute-start | bytes 1179656 | tf_op jit(solution)/shard_map/ppermute | solution.py:178
  114.3 12.5 %collective-permute-done.6.refs_7_ = bf16[256,768]{1,0:T(8,128)(2,1)S(1)} collective-permute-done((bf16[256,768]{1,0:T(8,128)(2,1)S(1)}, bf16[256,768]{1,0:T(8,128)(2,1)S(1)}, u32[]{:S(2)}, u32[]{:S(2)}) %collective-permute-start.6) | collective-permute-done | bytes 393248 | tf_op jit(solution)/shard_map/ppermute | solution.py:178
  126.8 0.7 copy-done.9
  127.5 23.0 %product.1 = (f32[96,896]{1,0:T(8,128)}, bf16[512,768]{1,0:T(8,128)(2,1)}, bf16[512,128]{1,0:T(8,128)(2,1)}) custom-call(s32[64]{0:T(128)} %lengths.5, s32[64]{0:T(128)} %shifts.5, s32[2]{0:T(128)} %pad_add_fusion.own, bf16[8,2,4,672,128]{4,3,2,1,0:T(8,128)(2,1)} %bitcast.6, bf16[512,768]{1,0:T(8,128)(2,1)} %copy-done.5, bf16[512,768]{1,0:T(8,128)(2,1)} %copy-done.7, ...), custom_call_target="tpu_custom_call" | custom-call | flops 5637144576 | bytes 17301504 | tf_op jit(solution)/shard_map/product/pallas_call | solution.py:214
  150.6 0.8 copy-done.1
  151.4 2.5 %unpack.1 = (f32[96,896]{1,0:T(8,128)}, f32[96,896]{1,0:T(8,128)}) custom-call(s32[64]{0:T(128)} %lengths.5, s32[64]{0:T(128)} %shifts.5, s32[2]{0:T(128)} %pad_add_fusion.own, bf16[64,16,256]{2,1,0:T(8,128)(2,1)} %copy-done.1, bf16[512,128]{1,0:T(8,128)(2,1)} %get-tuple-element.9.after), custom_call_target="tpu_custom_call" | custom-call | tf_op jit(solution)/shard_map/unpack/pallas_call | solution.py:247
  (28 shorter events, 0.4 us)
Async XLA Ops:
  7.2 14.2 %copy-start = (bf16[512,768]{1,0:T(8,128)(2,1)S(1)}, bf16[512,768]{1,0:T(8,128)(2,1)}, u32[]{:S(2)}) copy-start(bf16[512,768]{1,0:T(8,128)(2,1)} %param.6) | copy-start | bytes 2359300
  7.2 119.6 %all-gather.2.cloned.1.call-start = ((), (), s32[]{:S(2)}) async-start(), calls=%async_computation.1 | async-start | bytes 11698176 | tf_op jit(solution)/shard_map/all_gather | solution.py:191
  22.4 67.7 %copy-start.5 = (bf16[512,768]{1,0:T(8,128)(2,1)}, bf16[512,768]{1,0:T(8,128)(2,1)S(1)}, u32[]{:S(2)}) copy-start(bf16[512,768]{1,0:T(8,128)(2,1)S(1)} %fusion.2.refs_0_) | copy-start | bytes 2359300
  22.4 25.3 %collective-permute-start.1 = (bf16[512,768]{1,0:T(8,128)(2,1)S(1)}, bf16[512,768]{1,0:T(8,128)(2,1)S(1)}, u32[]{:S(2)}, u32[]{:S(2)}) collective-permute-start(bf16[512,768]{1,0:T(8,128)(2,1)S(1)} %fusion.2.refs_0_), channel_id=1, source_target_pairs={{0,7},{1,0},{2,1},{3,2},{4,3},{5,4},{6,5},{7,6},{8,15},{9,8},{10,9... | collective-permute-start | bytes 2359304 | tf_op jit(solution)/shard_map/ppermute | solution.py:174
  33.4 19.7 %collective-permute-start = (bf16[512,768]{1,0:T(8,128)(2,1)S(1)}, bf16[512,768]{1,0:T(8,128)(2,1)S(1)}, u32[]{:S(2)}, u32[]{:S(2)}) collective-permute-start(bf16[512,768]{1,0:T(8,128)(2,1)S(1)} %fusion.2.refs_0_), channel_id=1, source_target_pairs={{0,1},{1,2},{2,3},{3,4},{4,5},{5,6},{6,7},{7,0},{8,9},{9,10},{10,1... | collective-permute-start | bytes 2359304 | tf_op jit(solution)/shard_map/ppermute | solution.py:173
  47.6 26.2 %copy-start.6 = (bf16[512,768]{1,0:T(8,128)(2,1)}, bf16[512,768]{1,0:T(8,128)(2,1)S(1)}, u32[]{:S(2)}) copy-start(bf16[512,768]{1,0:T(8,128)(2,1)S(1)} %collective-permute-done.1.refs_2_) | copy-start | bytes 2359300
  47.7 18.9 %collective-permute-start.3 = (bf16[512,768]{1,0:T(8,128)(2,1)S(1)}, bf16[512,768]{1,0:T(8,128)(2,1)S(1)}, u32[]{:S(2)}, u32[]{:S(2)}) collective-permute-start(bf16[512,768]{1,0:T(8,128)(2,1)S(1)} %collective-permute-done.1.refs_2_), channel_id=1, source_target_pairs={{0,7},{1,0},{2,1},{3,2},{4,3},{5,4},{6,5},{7,6},{8,15},{9,8},{10,9... | collective-permute-start | bytes 2359304 | tf_op jit(solution)/shard_map/ppermute | solution.py:174
  53.1 20.8 %copy-start.7 = (bf16[512,768]{1,0:T(8,128)(2,1)}, bf16[512,768]{1,0:T(8,128)(2,1)S(1)}, u32[]{:S(2)}) copy-start(bf16[512,768]{1,0:T(8,128)(2,1)S(1)} %collective-permute-done.refs_1_) | copy-start | bytes 2359300
  53.1 18.9 %collective-permute-start.2 = (bf16[512,768]{1,0:T(8,128)(2,1)S(1)}, bf16[512,768]{1,0:T(8,128)(2,1)}, u32[]{:S(2)}, u32[]{:S(2)}) collective-permute-start(bf16[512,768]{1,0:T(8,128)(2,1)S(1)} %collective-permute-done.refs_1_), channel_id=1, source_target_pairs={{0,1},{1,2},{2,3},{3,4},{4,5},{5,6},{6,7},{7,0},{8,9},{9,10},{10,1... | collective-permute-start | bytes 2359304 | tf_op jit(solution)/shard_map/ppermute | solution.py:173
  66.5 7.4 %copy-start.8 = (bf16[512,768]{1,0:T(8,128)(2,1)}, bf16[512,768]{1,0:T(8,128)(2,1)S(1)}, u32[]{:S(2)}) copy-start(bf16[512,768]{1,0:T(8,128)(2,1)S(1)} %collective-permute-done.3.refs_4_) | copy-start | bytes 2359300
  66.5 18.1 %collective-permute-start.5 = (bf16[512,768]{1,0:T(8,128)(2,1)S(1)}, bf16[512,768]{1,0:T(8,128)(2,1)S(1)}, u32[]{:S(2)}, u32[]{:S(2)}) collective-permute-start(bf16[512,768]{1,0:T(8,128)(2,1)S(1)} %collective-permute-done.3.refs_4_), channel_id=1, source_target_pairs={{0,7},{1,0},{2,1},{3,2},{4,3},{5,4},{6,5},{7,6},{8,15},{9,8},{10,9... | collective-permute-start | bytes 2359304 | tf_op jit(solution)/shard_map/ppermute | solution.py:174
  72.0 40.4 %collective-permute-start.4 = (bf16[512,768]{1,0:T(8,128)(2,1)}, bf16[512,768]{1,0:T(8,128)(2,1)S(1)}, u32[]{:S(2)}, u32[]{:S(2)}) collective-permute-start(bf16[512,768]{1,0:T(8,128)(2,1)} %collective-permute-done.2.refs_3_), channel_id=1, source_target_pairs={{0,1},{1,2},{2,3},{3,4},{4,5},{5,6},{6,7},{7,0},{8,9},{9,10},{10,1... | collective-permute-start | bytes 2359304 | tf_op jit(solution)/shard_map/ppermute | solution.py:173
  84.6 42.2 %copy-start.3 = (bf16[512,768]{1,0:T(8,128)(2,1)}, bf16[512,768]{1,0:T(8,128)(2,1)S(1)}, u32[]{:S(2)}) copy-start(bf16[512,768]{1,0:T(8,128)(2,1)S(1)} %collective-permute-done.5.refs_6_) | copy-start | bytes 2359300
  84.6 10.1 %collective-permute-start.7 = (bf16[256,768]{1,0:T(8,128)(2,1)S(1)}, bf16[256,768]{1,0:T(8,128)(2,1)S(1)}, u32[]{:S(2)}, u32[]{:S(2)}) collective-permute-start(bf16[256,768]{1,0:T(8,128)(2,1)S(1)} %slice.9), channel_id=1, source_target_pairs={{0,7},{1,0},{2,1},{3,2},{4,3},{5,4},{6,5},{7,6},{8,15},{9,8},{10,9... | collective-permute-start | bytes 1179656 | tf_op jit(solution)/shard_map/ppermute | solution.py:179
  94.8 0.8 copy-start.2
  97.9 52.6 %all-to-all-start = ((bf16[64,16,256]{2,1,0:T(8,128)(2,1)}), bf16[64,16,256]{2,1,0:T(8,128)(2,1)S(1)}, u32[]{:S(2)}, u32[]{:S(2)}) async-start(bf16[64,16,256]{2,1,0:T(8,128)(2,1)} %pack.1), calls=%async_computation | async-start | bytes 1048576 | tf_op jit(solution)/shard_map/all_to_all | solution.py:210
  112.3 14.5 %copy-start.4 = (bf16[512,768]{1,0:T(8,128)(2,1)}, bf16[512,768]{1,0:T(8,128)(2,1)S(1)}, u32[]{:S(2)}) copy-start(bf16[512,768]{1,0:T(8,128)(2,1)S(1)} %collective-permute-done.4.refs_5_) | copy-start | bytes 2359300
  112.4 14.4 %collective-permute-start.6 = (bf16[256,768]{1,0:T(8,128)(2,1)S(1)}, bf16[256,768]{1,0:T(8,128)(2,1)S(1)}, u32[]{:S(2)}, u32[]{:S(2)}) collective-permute-start(bf16[256,768]{1,0:T(8,128)(2,1)S(1)} %slice.8), channel_id=1, source_target_pairs={{0,1},{1,2},{2,3},{3,4},{4,5},{5,6},{6,7},{7,0},{8,9},{9,10},{10,1... | collective-permute-start | bytes 1179656 | tf_op jit(solution)/shard_map/ppermute | solution.py:178
  126.8 0.7 copy-start.9
  150.6 0.8 copy-start.1
Sparse Core Ops, SparseCore 0:
  21.5 77.9 all-gather.1

commit v5 on v4

--- a/solution.py
+++ b/solution.py
@@ -35,7 +35,7 @@
 Y_GROUPS = [[dp_index(y, x, c) for y in range(NY) for c in range(NC)] for x in range(NX)]
 
 
-def pack_kernel(lengths, shifts, own, first, second, after, out, first_rows, second_rows):
+def pack_kernel(lengths, shifts, own, first, second, out, first_rows, second_rows):
     for rows, state in ((first_rows, first), (second_rows, second)):
         for head in range(HEADS):
             rows[pl.ds(head, ROWS, stride=HEADS), :] = state[:, head * HS : (head + 1) * HS]
@@ -51,7 +51,7 @@
     lax.fori_loop(0, N_DP, piece, jnp.int32(0))
 
 
-def unpack_kernel(lengths, shifts, own, received, after, first, second, first_rows, second_rows):
+def unpack_kernel(lengths, shifts, own, received, first, second, first_rows, second_rows):
     me = own[0]
 
     def piece(j, start):
@@ -160,10 +160,9 @@
 
 SMEM = pl.BlockSpec(memory_space=pltpu.SMEM)
 VMEM = pl.BlockSpec(memory_space=pltpu.VMEM)
-ANY = pl.BlockSpec(memory_space=pl.ANY)
-
-
-def gather_tokens(tokens):
+
+
+def gather_tokens(tokens, moments):
     up = [(z, (z + 1) % N_Z) for z in range(N_Z)]
     down = [(z, (z - 1) % N_Z) for z in range(N_Z)]
     half = tokens.shape[0] // 2
@@ -173,11 +172,13 @@
         from_below = lax.ppermute(from_below, "tensor", up)
         from_above = lax.ppermute(from_above, "tensor", down)
         distances += [-distance, distance]
+        if distance == 2:
+            from_below, from_above, moments = lax.optimization_barrier((from_below, from_above, moments))
         arrays += [from_below, from_above]
     distances.append(N_Z // 2)
     arrays.append(lax.ppermute(from_below[:half], "tensor", up))
     arrays.append(lax.ppermute(from_above[half:], "tensor", down))
-    return tuple(distances), arrays
+    return tuple(distances), arrays, moments
 
 
 def per_device(tokens, old_master, old_first, old_second, piece_lengths, piece_shifts):
@@ -197,17 +198,26 @@
     new = (depth // GROUP_ROWS * P_LOW + low) * GROUP_ROWS + depth % GROUP_ROWS
     order = (new[:, None] == old[None, :]).astype(jnp.bfloat16)
     ordered = jnp.dot(tokens, order, preferred_element_type=jnp.float32).astype(jnp.bfloat16)
-    distances, blocks = gather_tokens(ordered)
-
     packed = pl.pallas_call(
         pack_kernel,
         out_shape=jax.ShapeDtypeStruct((N_DP, BUCKET, 2 * HS), jnp.bfloat16),
-        in_specs=[SMEM] * 3 + [VMEM] * 2 + [ANY],
+        in_specs=[SMEM] * 3 + [VMEM] * 2,
         out_specs=VMEM,
         scratch_shapes=[slots, slots],
         name="pack",
-    )(piece_lengths, piece_shifts, own, old_first, old_second, blocks[-1])
+    )(piece_lengths, piece_shifts, own, old_first, old_second)
     received = lax.all_to_all(packed, "dp", split_axis=0, concat_axis=0, tiled=True)
+    new_first, new_second = pl.pallas_call(
+        unpack_kernel,
+        out_shape=[state, state],
+        in_specs=[SMEM] * 3 + [VMEM],
+        out_specs=[VMEM] * 2,
+        scratch_shapes=[slots, slots],
+        name="unpack",
+    )(piece_lengths, piece_shifts, own, received)
+
+    distances, blocks, (new_first, new_second) = gather_tokens(ordered, (new_first, new_second))
+
     query_cols = HQ // lax.axis_size("tensor") * HS
     key_cols = block_cols - query_cols
     group_cols = P_LOW * GROUP_ROWS
@@ -244,15 +254,6 @@
         ),
         name="product",
     )(piece_lengths, piece_shifts, own, gathered, *blocks)
-    new_first, new_second = pl.pallas_call(
-        unpack_kernel,
-        out_shape=[state, state],
-        in_specs=[SMEM] * 3 + [VMEM, ANY],
-        out_specs=[VMEM] * 2,
-        scratch_shapes=[slots, slots],
-        name="unpack",
-    )(piece_lengths, piece_shifts, own, received, key)
-
     return (new_master, new_first, new_second, query, key)
 
 

time: 161 us -> 144 us (0.89); the launches traced: 161 us -> 141 us
  waiting for transfers between devices: 51.1 us -> 36.8 us
  starting transfers between devices: 49.3 us -> 45.9 us
    ppermute x3, waiting for transfers between devices: 34.5 us -> 0.01 us  [gather_tokens(): from_above = lax.ppermute(from_above, 'tensor', down)]
    all_to_all x1, waiting for transfers between devices: 0.01 us -> 16.3 us  [per_device(): lax.all_to_all(packed, 'dp', split_axis=0, concat_axis=0, tiled=True)]
    ppermute x3, waiting for transfers between devices: 0.01 us -> 14.6 us  [gather_tokens(): from_below = lax.ppermute(from_below, 'tensor', up)]
    ppermute x1, waiting for transfers between devices: 12.5 us -> 4.82 us  [gather_tokens(): arrays.append(lax.ppermute(from_below[:half], 'tensor', up))]
    ppermute x1, waiting for transfers between devices: 4.09 us -> 0.96 us  [gather_tokens(): arrays.append(lax.ppermute(from_above[half:], 'tensor', down))]
  transfers between devices with their start and end apart: 10 -> 10, of which waited for: 5 -> 5; matrix products, arithmetic and copies ran while one was open for 1% -> 1% of each run, Pallas kernels for 16% -> 3%
where the time goes in v5:
time: 144 us; the launch traced here: 141 us
  starting transfers between devices  45.9 us (32%)
  waiting for transfers between devices  36.8 us (26%)
  Pallas kernels  27.9 us (19%)
  between operations  14.2 us (10%)
  blocking collectives  12.9 us (9%)
  other arithmetic  1.74 us (1%)
    pallas_call x1, Pallas kernels, per_device(): pl.pallas_call(functools.partial(product_kernel, distances), grid=(GROUPS...  23 us
    ppermute x3, starting transfers between devices, gather_tokens(): from_above = lax.ppermute(from_above, 'tensor', down)  20.5 us
    all_to_all x1, waiting for transfers between devices, per_device(): lax.all_to_all(packed, 'dp', split_axis=0, concat_axis=0, tiled=True)  16.3 us
    ppermute x3, waiting for transfers between devices, gather_tokens(): from_below = lax.ppermute(from_below, 'tensor', up)  14.6 us
    all_to_all x1, starting transfers between devices, per_device(): lax.all_to_all(packed, 'dp', split_axis=0, concat_axis=0, tiled=True)  13.1 us
    all_gather x1, blocking collectives, per_device(): lax.all_gather(column, 'dp', axis_index_groups=X_GROUPS, axis=0, tiled=True)  12.9 us
    ppermute x3, starting transfers between devices, gather_tokens(): from_below = lax.ppermute(from_below, 'tensor', up)  5.75 us
    ppermute x1, waiting for transfers between devices, gather_tokens(): arrays.append(lax.ppermute(from_below[:half], 'tensor', up))  4.82 us
  transfers between devices with their start and end apart: 10, of which 5 were waited for; matrix products, arithmetic and copies ran while one was open for 1% of the time, Pallas kernels for 3%

profile of v5, /device:TPU:1, one launch (start us, length us, event | category | flops | bytes accessed | tf_op | source)
XLA Modules:
  0.0 141.4 jit_solution(2979479688013767066)
XLA Ops:
  7.2 0.0 all-gather.2.cloned.1.call-start
  7.2 1.1 convert_element_type.9
  8.3 0.2 reshape.63
  8.5 12.9 %all_gather.6 = bf16[2688,128]{1,0:T(8,128)(2,1)} all-gather(bf16[672,128]{1,0:T(8,128)(2,1)S(1)} %reshape.63), channel_id=1, replica_groups={{0,16,32,48},{8,24,40,56},{64,80,96,112},{72,88,104,120},{128,144,160,1..., dimensions={0}, use_global_device_ids=true | all-gather | bytes 860160 | tf_op jit(solution)/shard_map/all_gather | solution.py:191
  21.4 1.0 fusion.2.refs_0_
  22.4 11.0 %collective-permute-start.1 = (bf16[512,768]{1,0:T(8,128)(2,1)S(1)}, bf16[512,768]{1,0:T(8,128)(2,1)S(1)}, u32[]{:S(2)}, u32[]{:S(2)}) collective-permute-start(bf16[512,768]{1,0:T(8,128)(2,1)S(1)} %fusion.2.refs_0_), channel_id=1, source_target_pairs={{0,7},{1,0},{2,1},{3,2},{4,3},{5,4},{6,5},{7,6},{8,15},{9,8},{10,9... | collective-permute-start | bytes 2359304 | tf_op jit(solution)/shard_map/ppermute | solution.py:173
  33.4 1.9 %collective-permute-start = (bf16[512,768]{1,0:T(8,128)(2,1)S(1)}, bf16[512,768]{1,0:T(8,128)(2,1)}, u32[]{:S(2)}, u32[]{:S(2)}) collective-permute-start(bf16[512,768]{1,0:T(8,128)(2,1)S(1)} %fusion.2.refs_0_), channel_id=1, source_target_pairs={{0,1},{1,2},{2,3},{3,4},{4,5},{5,6},{6,7},{7,0},{8,9},{9,10},{10,1... | collective-permute-start | bytes 2359304 | tf_op jit(solution)/shard_map/ppermute | solution.py:172
  35.3 0.7 pad_add_fusion.own
  36.0 2.4 %pack.1 = bf16[64,16,256]{2,1,0:T(8,128)(2,1)} custom-call(s32[64]{0:T(128)} %lengths.5, s32[64]{0:T(128)} %shifts.5, s32[2]{0:T(128)} %pad_add_fusion.own, f32[96,896]{1,0:T(8,128)} %first.1, f32[96,896]{1,0:T(8,128)} %second.1), custom_call_target="tpu_custom_call" | custom-call | tf_op jit(solution)/shard_map/pack/pallas_call | solution.py:201
  38.3 13.1 %all-to-all-start = ((bf16[64,16,256]{2,1,0:T(8,128)(2,1)}), bf16[64,16,256]{2,1,0:T(8,128)(2,1)S(1)}, u32[]{:S(2)}, u32[]{:S(2)}) async-start(bf16[64,16,256]{2,1,0:T(8,128)(2,1)} %pack.1), calls=%async_computation | async-start | bytes 1048576 | tf_op jit(solution)/shard_map/all_to_all | solution.py:209
  51.4 4.9 %collective-permute-start.3 = (bf16[512,768]{1,0:T(8,128)(2,1)S(1)}, bf16[512,768]{1,0:T(8,128)(2,1)}, u32[]{:S(2)}, u32[]{:S(2)}) collective-permute-start(bf16[512,768]{1,0:T(8,128)(2,1)S(1)} %collective-permute-done.1.refs_2_), channel_id=1, source_target_pairs={{0,7},{1,0},{2,1},{3,2},{4,3},{5,4},{6,5},{7,6},{8,15},{9,8},{10,9... | collective-permute-start | bytes 2359304 | tf_op jit(solution)/shard_map/ppermute | solution.py:173
  56.3 1.9 %collective-permute-start.2 = (bf16[512,768]{1,0:T(8,128)(2,1)}, bf16[512,768]{1,0:T(8,128)(2,1)}, u32[]{:S(2)}, u32[]{:S(2)}) collective-permute-start(bf16[512,768]{1,0:T(8,128)(2,1)} %collective-permute-done.refs_1_), channel_id=1, source_target_pairs={{0,1},{1,2},{2,3},{3,4},{4,5},{5,6},{6,7},{7,0},{8,9},{9,10},{10,1... | collective-permute-start | bytes 2359304 | tf_op jit(solution)/shard_map/ppermute | solution.py:172
  58.2 16.3 %all-to-all-done.received = bf16[64,16,256]{2,1,0:T(8,128)(2,1)S(1)} async-done(((bf16[64,16,256]{2,1,0:T(8,128)(2,1)}), bf16[64,16,256]{2,1,0:T(8,128)(2,1)S(1)}, u32[]{:S(2)}, u32[]{:S(2)}) %all-to-all-start) | async-done | bytes 524320 | tf_op jit(solution)/shard_map/all_to_all | solution.py:209
  74.6 0.8 copy-done.1
  75.4 2.5 %unpack.1 = (f32[96,896]{1,0:T(8,128)}, f32[96,896]{1,0:T(8,128)}) custom-call(s32[64]{0:T(128)} %lengths.5, s32[64]{0:T(128)} %shifts.5, s32[2]{0:T(128)} %pad_add_fusion.own, bf16[64,16,256]{2,1,0:T(8,128)(2,1)} %copy-done.1), custom_call_target="tpu_custom_call" | custom-call | tf_op jit(solution)/shard_map/unpack/pallas_call | solution.py:210
  77.9 0.2 collective-permute-done.2.refs_3_
  78.1 1.9 %collective-permute-start.4 = (bf16[512,768]{1,0:T(8,128)(2,1)}, bf16[512,768]{1,0:T(8,128)(2,1)S(1)}, u32[]{:S(2)}, u32[]{:S(2)}) collective-permute-start(bf16[512,768]{1,0:T(8,128)(2,1)} %collective-permute-done.2.refs_3_), channel_id=1, source_target_pairs={{0,1},{1,2},{2,3},{3,4},{4,5},{5,6},{6,7},{7,0},{8,9},{9,10},{10,1... | collective-permute-start | bytes 2359304 | tf_op jit(solution)/shard_map/ppermute | solution.py:172
  80.0 4.7 %collective-permute-start.5 = (bf16[512,768]{1,0:T(8,128)(2,1)}, bf16[512,768]{1,0:T(8,128)(2,1)S(1)}, u32[]{:S(2)}, u32[]{:S(2)}) collective-permute-start(bf16[512,768]{1,0:T(8,128)(2,1)} %collective-permute-done.3.refs_4_), channel_id=1, source_target_pairs={{0,7},{1,0},{2,1},{3,2},{4,3},{5,4},{6,5},{7,6},{8,15},{9,8},{10,9... | collective-permute-start | bytes 2359304 | tf_op jit(solution)/shard_map/ppermute | solution.py:173
  84.7 14.4 %collective-permute-done.4.refs_5_ = bf16[512,768]{1,0:T(8,128)(2,1)S(1)} collective-permute-done((bf16[512,768]{1,0:T(8,128)(2,1)}, bf16[512,768]{1,0:T(8,128)(2,1)S(1)}, u32[]{:S(2)}, u32[]{:S(2)}) %collective-permute-start.4) | collective-permute-done | bytes 786464 | tf_op jit(solution)/shard_map/ppermute | solution.py:172
  99.2 1.9 %collective-permute-start.6 = (bf16[256,768]{1,0:T(8,128)(2,1)S(1)}, bf16[256,768]{1,0:T(8,128)(2,1)S(1)}, u32[]{:S(2)}, u32[]{:S(2)}) collective-permute-start(bf16[256,768]{1,0:T(8,128)(2,1)S(1)} %slice.8), channel_id=1, source_target_pairs={{0,1},{1,2},{2,3},{3,4},{4,5},{5,6},{6,7},{7,0},{8,9},{9,10},{10,1... | collective-permute-start | bytes 1179656 | tf_op jit(solution)/shard_map/ppermute | solution.py:179
  101.1 4.6 %collective-permute-start.7 = (bf16[256,768]{1,0:T(8,128)(2,1)S(1)}, bf16[256,768]{1,0:T(8,128)(2,1)}, u32[]{:S(2)}, u32[]{:S(2)}) collective-permute-start(bf16[256,768]{1,0:T(8,128)(2,1)S(1)} %slice.9), channel_id=1, source_target_pairs={{0,7},{1,0},{2,1},{3,2},{4,3},{5,4},{6,5},{7,6},{8,15},{9,8},{10,9... | collective-permute-start | bytes 1179656 | tf_op jit(solution)/shard_map/ppermute | solution.py:180
  105.7 4.8 %collective-permute-done.6.refs_7_ = bf16[256,768]{1,0:T(8,128)(2,1)S(1)} collective-permute-done((bf16[256,768]{1,0:T(8,128)(2,1)S(1)}, bf16[256,768]{1,0:T(8,128)(2,1)S(1)}, u32[]{:S(2)}, u32[]{:S(2)}) %collective-permute-start.6) | collective-permute-done | bytes 393248 | tf_op jit(solution)/shard_map/ppermute | solution.py:179
  110.5 1.0 collective-permute-done.7.refs_8_
  111.5 23.0 %product.1 = (f32[96,896]{1,0:T(8,128)}, bf16[512,768]{1,0:T(8,128)(2,1)}, bf16[512,128]{1,0:T(8,128)(2,1)}) custom-call(s32[64]{0:T(128)} %lengths.5, s32[64]{0:T(128)} %shifts.5, s32[2]{0:T(128)} %pad_add_fusion.own, bf16[8,2,4,672,128]{4,3,2,1,0:T(8,128)(2,1)} %bitcast.6, bf16[512,768]{1,0:T(8,128)(2,1)} %copy-done.4, ...), custom_call_target="tpu_custom_call" | custom-call | flops 5637144576 | bytes 17301504 | tf_op jit(solution)/shard_map/product/pallas_call | solution.py:224
  (22 shorter events, 0.1 us)
Async XLA Ops:
  7.2 14.2 %copy-start = (bf16[512,768]{1,0:T(8,128)(2,1)S(1)}, bf16[512,768]{1,0:T(8,128)(2,1)}, u32[]{:S(2)}) copy-start(bf16[512,768]{1,0:T(8,128)(2,1)} %param.6) | copy-start | bytes 2359300
  7.2 104.3 %all-gather.2.cloned.1.call-start = ((), (), s32[]{:S(2)}) async-start(), calls=%async_computation.1 | async-start | bytes 11698176 | tf_op jit(solution)/shard_map/all_gather | solution.py:192
  22.4 89.1 %copy-start.4 = (bf16[512,768]{1,0:T(8,128)(2,1)}, bf16[512,768]{1,0:T(8,128)(2,1)S(1)}, u32[]{:S(2)}) copy-start(bf16[512,768]{1,0:T(8,128)(2,1)S(1)} %fusion.2.refs_0_) | copy-start | bytes 2359300
  22.4 29.0 %collective-permute-start.1 = (bf16[512,768]{1,0:T(8,128)(2,1)S(1)}, bf16[512,768]{1,0:T(8,128)(2,1)S(1)}, u32[]{:S(2)}, u32[]{:S(2)}) collective-permute-start(bf16[512,768]{1,0:T(8,128)(2,1)S(1)} %fusion.2.refs_0_), channel_id=1, source_target_pairs={{0,7},{1,0},{2,1},{3,2},{4,3},{5,4},{6,5},{7,6},{8,15},{9,8},{10,9... | collective-permute-start | bytes 2359304 | tf_op jit(solution)/shard_map/ppermute | solution.py:173
  33.4 22.9 %collective-permute-start = (bf16[512,768]{1,0:T(8,128)(2,1)S(1)}, bf16[512,768]{1,0:T(8,128)(2,1)}, u32[]{:S(2)}, u32[]{:S(2)}) collective-permute-start(bf16[512,768]{1,0:T(8,128)(2,1)S(1)} %fusion.2.refs_0_), channel_id=1, source_target_pairs={{0,1},{1,2},{2,3},{3,4},{4,5},{5,6},{6,7},{7,0},{8,9},{9,10},{10,1... | collective-permute-start | bytes 2359304 | tf_op jit(solution)/shard_map/ppermute | solution.py:172
  38.3 36.2 %all-to-all-start = ((bf16[64,16,256]{2,1,0:T(8,128)(2,1)}), bf16[64,16,256]{2,1,0:T(8,128)(2,1)S(1)}, u32[]{:S(2)}, u32[]{:S(2)}) async-start(bf16[64,16,256]{2,1,0:T(8,128)(2,1)} %pack.1), calls=%async_computation | async-start | bytes 1048576 | tf_op jit(solution)/shard_map/all_to_all | solution.py:209
  51.4 26.6 %copy-start.5 = (bf16[512,768]{1,0:T(8,128)(2,1)}, bf16[512,768]{1,0:T(8,128)(2,1)S(1)}, u32[]{:S(2)}) copy-start(bf16[512,768]{1,0:T(8,128)(2,1)S(1)} %collective-permute-done.1.refs_2_) | copy-start | bytes 2359300
  51.4 26.4 %collective-permute-start.3 = (bf16[512,768]{1,0:T(8,128)(2,1)S(1)}, bf16[512,768]{1,0:T(8,128)(2,1)}, u32[]{:S(2)}, u32[]{:S(2)}) collective-permute-start(bf16[512,768]{1,0:T(8,128)(2,1)S(1)} %collective-permute-done.1.refs_2_), channel_id=1, source_target_pairs={{0,7},{1,0},{2,1},{3,2},{4,3},{5,4},{6,5},{7,6},{8,15},{9,8},{10,9... | collective-permute-start | bytes 2359304 | tf_op jit(solution)/shard_map/ppermute | solution.py:173
  56.3 21.8 %collective-permute-start.2 = (bf16[512,768]{1,0:T(8,128)(2,1)}, bf16[512,768]{1,0:T(8,128)(2,1)}, u32[]{:S(2)}, u32[]{:S(2)}) collective-permute-start(bf16[512,768]{1,0:T(8,128)(2,1)} %collective-permute-done.refs_1_), channel_id=1, source_target_pairs={{0,1},{1,2},{2,3},{3,4},{4,5},{5,6},{6,7},{7,0},{8,9},{9,10},{10,1... | collective-permute-start | bytes 2359304 | tf_op jit(solution)/shard_map/ppermute | solution.py:172
  74.6 0.8 copy-start.1
  78.1 21.0 %collective-permute-start.4 = (bf16[512,768]{1,0:T(8,128)(2,1)}, bf16[512,768]{1,0:T(8,128)(2,1)S(1)}, u32[]{:S(2)}, u32[]{:S(2)}) collective-permute-start(bf16[512,768]{1,0:T(8,128)(2,1)} %collective-permute-done.2.refs_3_), channel_id=1, source_target_pairs={{0,1},{1,2},{2,3},{3,4},{4,5},{5,6},{6,7},{7,0},{8,9},{9,10},{10,1... | collective-permute-start | bytes 2359304 | tf_op jit(solution)/shard_map/ppermute | solution.py:172
  80.0 21.1 %collective-permute-start.5 = (bf16[512,768]{1,0:T(8,128)(2,1)}, bf16[512,768]{1,0:T(8,128)(2,1)S(1)}, u32[]{:S(2)}, u32[]{:S(2)}) collective-permute-start(bf16[512,768]{1,0:T(8,128)(2,1)} %collective-permute-done.3.refs_4_), channel_id=1, source_target_pairs={{0,7},{1,0},{2,1},{3,2},{4,3},{5,4},{6,5},{7,6},{8,15},{9,8},{10,9... | collective-permute-start | bytes 2359304 | tf_op jit(solution)/shard_map/ppermute | solution.py:173
  99.1 12.4 %copy-start.2 = (bf16[512,768]{1,0:T(8,128)(2,1)}, bf16[512,768]{1,0:T(8,128)(2,1)S(1)}, u32[]{:S(2)}) copy-start(bf16[512,768]{1,0:T(8,128)(2,1)S(1)} %collective-permute-done.4.refs_5_) | copy-start | bytes 2359300
  99.2 11.4 %collective-permute-start.6 = (bf16[256,768]{1,0:T(8,128)(2,1)S(1)}, bf16[256,768]{1,0:T(8,128)(2,1)S(1)}, u32[]{:S(2)}, u32[]{:S(2)}) collective-permute-start(bf16[256,768]{1,0:T(8,128)(2,1)S(1)} %slice.8), channel_id=1, source_target_pairs={{0,1},{1,2},{2,3},{3,4},{4,5},{5,6},{6,7},{7,0},{8,9},{9,10},{10,1... | collective-permute-start | bytes 1179656 | tf_op jit(solution)/shard_map/ppermute | solution.py:179
  101.1 10.4 %copy-start.3 = (bf16[512,768]{1,0:T(8,128)(2,1)}, bf16[512,768]{1,0:T(8,128)(2,1)S(1)}, u32[]{:S(2)}) copy-start(bf16[512,768]{1,0:T(8,128)(2,1)S(1)} %collective-permute-done.5.refs_6_) | copy-start | bytes 2359300
  101.1 10.4 %collective-permute-start.7 = (bf16[256,768]{1,0:T(8,128)(2,1)S(1)}, bf16[256,768]{1,0:T(8,128)(2,1)}, u32[]{:S(2)}, u32[]{:S(2)}) collective-permute-start(bf16[256,768]{1,0:T(8,128)(2,1)S(1)} %slice.9), channel_id=1, source_target_pairs={{0,7},{1,0},{2,1},{3,2},{4,3},{5,4},{6,5},{7,6},{8,15},{9,8},{10,9... | collective-permute-start | bytes 1179656 | tf_op jit(solution)/shard_map/ppermute | solution.py:180
  110.5 1.0 copy-start.6
Sparse Core Ops, SparseCore 0:
  21.5 89.1 all-gather.1

commit v6 on v4

--- a/solution.py
+++ b/solution.py
@@ -35,7 +35,7 @@
 Y_GROUPS = [[dp_index(y, x, c) for y in range(NY) for c in range(NC)] for x in range(NX)]
 
 
-def pack_kernel(lengths, shifts, own, first, second, after, out, first_rows, second_rows):
+def pack_kernel(lengths, shifts, own, first, second, out, first_rows, second_rows):
     for rows, state in ((first_rows, first), (second_rows, second)):
         for head in range(HEADS):
             rows[pl.ds(head, ROWS, stride=HEADS), :] = state[:, head * HS : (head + 1) * HS]
@@ -51,7 +51,7 @@
     lax.fori_loop(0, N_DP, piece, jnp.int32(0))
 
 
-def unpack_kernel(lengths, shifts, own, received, after, first, second, first_rows, second_rows):
+def unpack_kernel(lengths, shifts, own, received, first, second, first_rows, second_rows):
     me = own[0]
 
     def piece(j, start):
@@ -160,7 +160,6 @@
 
 SMEM = pl.BlockSpec(memory_space=pltpu.SMEM)
 VMEM = pl.BlockSpec(memory_space=pltpu.VMEM)
-ANY = pl.BlockSpec(memory_space=pl.ANY)
 
 
 def gather_tokens(tokens):
@@ -197,17 +196,18 @@
     new = (depth // GROUP_ROWS * P_LOW + low) * GROUP_ROWS + depth % GROUP_ROWS
     order = (new[:, None] == old[None, :]).astype(jnp.bfloat16)
     ordered = jnp.dot(tokens, order, preferred_element_type=jnp.float32).astype(jnp.bfloat16)
-    distances, blocks = gather_tokens(ordered)
-
     packed = pl.pallas_call(
         pack_kernel,
         out_shape=jax.ShapeDtypeStruct((N_DP, BUCKET, 2 * HS), jnp.bfloat16),
-        in_specs=[SMEM] * 3 + [VMEM] * 2 + [ANY],
+        in_specs=[SMEM] * 3 + [VMEM] * 2,
         out_specs=VMEM,
         scratch_shapes=[slots, slots],
         name="pack",
-    )(piece_lengths, piece_shifts, own, old_first, old_second, blocks[-1])
+    )(piece_lengths, piece_shifts, own, old_first, old_second)
+    distances, blocks = gather_tokens(ordered)
+    packed, blocks = lax.optimization_barrier((packed, blocks))
     received = lax.all_to_all(packed, "dp", split_axis=0, concat_axis=0, tiled=True)
+
     query_cols = HQ // lax.axis_size("tensor") * HS
     key_cols = block_cols - query_cols
     group_cols = P_LOW * GROUP_ROWS
@@ -244,15 +244,15 @@
         ),
         name="product",
     )(piece_lengths, piece_shifts, own, gathered, *blocks)
+    received, key = lax.optimization_barrier((received, key))
     new_first, new_second = pl.pallas_call(
         unpack_kernel,
         out_shape=[state, state],
-        in_specs=[SMEM] * 3 + [VMEM, ANY],
+        in_specs=[SMEM] * 3 + [VMEM],
         out_specs=[VMEM] * 2,
         scratch_shapes=[slots, slots],
         name="unpack",
-    )(piece_lengths, piece_shifts, own, received, key)
-
+    )(piece_lengths, piece_shifts, own, received)
     return (new_master, new_first, new_second, query, key)
 
 

time: 161 us -> 149 us (0.925)
  waiting for transfers between devices: 51.1 us -> 39.5 us
    ppermute x1, waiting for transfers between devices: 12.5 us -> 4.91 us  [gather_tokens(): arrays.append(lax.ppermute(from_below[:half], 'tensor', up))]
    ppermute x1, waiting for transfers between devices: 4.09 us -> 0.01 us  [gather_tokens(): arrays.append(lax.ppermute(from_above[half:], 'tensor', down))]
  transfers between devices with their start and end apart: 10 -> 10, of which waited for: 5 -> 4; matrix products, arithmetic and copies ran while one was open for 1% -> 1% of each run, Pallas kernels for 16% -> 17%
where the time goes in v6:
time: 149 us; the launch traced here: 148 us
  starting transfers between devices  49.9 us (33%)
  waiting for transfers between devices  39.5 us (27%)
  Pallas kernels  27.9 us (19%)
  between operations  14.3 us (10%)
  blocking collectives  12.9 us (9%)
  other arithmetic  1.68 us (1%)
    ppermute x3, waiting for transfers between devices, gather_tokens(): from_above = lax.ppermute(from_above, 'tensor', down)  34.5 us
    pallas_call x1, Pallas kernels, per_device(): pl.pallas_call(functools.partial(product_kernel, distances), grid=(GROUPS...  23 us
    ppermute x3, starting transfers between devices, gather_tokens(): from_above = lax.ppermute(from_above, 'tensor', down)  21.8 us
    all_to_all x1, starting transfers between devices, per_device(): lax.all_to_all(packed, 'dp', split_axis=0, concat_axis=0, tiled=True)  15 us
    all_gather x1, blocking collectives, per_device(): lax.all_gather(column, 'dp', axis_index_groups=X_GROUPS, axis=0, tiled=True)  12.9 us
    ppermute x3, starting transfers between devices, gather_tokens(): from_below = lax.ppermute(from_below, 'tensor', up)  5.76 us
    ppermute x1, starting transfers between devices, gather_tokens(): arrays.append(lax.ppermute(from_above[half:], 'tensor', down))  5.42 us
    ppermute x1, waiting for transfers between devices, gather_tokens(): arrays.append(lax.ppermute(from_below[:half], 'tensor', up))  4.91 us
  transfers between devices with their start and end apart: 10, of which 4 were waited for; matrix products, arithmetic and copies ran while one was open for 1% of the time, Pallas kernels for 17%

profile of v6, /device:TPU:1, one launch (start us, length us, event | category | flops | bytes accessed | tf_op | source)
XLA Modules:
  0.0 148.2 jit_solution(9441853073457408112)
XLA Ops:
  7.2 0.0 all-gather.2.cloned.1.call-start
  7.2 1.1 convert_element_type.10
  8.3 0.2 reshape.63
  8.5 12.9 %all_gather.6 = bf16[2688,128]{1,0:T(8,128)(2,1)} all-gather(bf16[672,128]{1,0:T(8,128)(2,1)S(1)} %reshape.63), channel_id=1, replica_groups={{0,16,32,48},{8,24,40,56},{64,80,96,112},{72,88,104,120},{128,144,160,1..., dimensions={0}, use_global_device_ids=true | all-gather | bytes 860160 | tf_op jit(solution)/shard_map/all_gather | solution.py:189
  21.4 1.0 fusion.2.refs_0_
  22.4 11.0 %collective-permute-start.1 = (bf16[512,768]{1,0:T(8,128)(2,1)S(1)}, bf16[512,768]{1,0:T(8,128)(2,1)S(1)}, u32[]{:S(2)}, u32[]{:S(2)}) collective-permute-start(bf16[512,768]{1,0:T(8,128)(2,1)S(1)} %fusion.2.refs_0_), channel_id=1, source_target_pairs={{0,7},{1,0},{2,1},{3,2},{4,3},{5,4},{6,5},{7,6},{8,15},{9,8},{10,9... | collective-permute-start | bytes 2359304 | tf_op jit(solution)/shard_map/ppermute | solution.py:173
  33.4 1.9 %collective-permute-start = (bf16[512,768]{1,0:T(8,128)(2,1)S(1)}, bf16[512,768]{1,0:T(8,128)(2,1)S(1)}, u32[]{:S(2)}, u32[]{:S(2)}) collective-permute-start(bf16[512,768]{1,0:T(8,128)(2,1)S(1)} %fusion.2.refs_0_), channel_id=1, source_target_pairs={{0,1},{1,2},{2,3},{3,4},{4,5},{5,6},{6,7},{7,0},{8,9},{9,10},{10,1... | collective-permute-start | bytes 2359304 | tf_op jit(solution)/shard_map/ppermute | solution.py:172
  35.3 12.3 %collective-permute-done.1.refs_2_ = bf16[512,768]{1,0:T(8,128)(2,1)S(1)} collective-permute-done((bf16[512,768]{1,0:T(8,128)(2,1)S(1)}, bf16[512,768]{1,0:T(8,128)(2,1)S(1)}, u32[]{:S(2)}, u32[]{:S(2)}) %collective-permute-start.1) | collective-permute-done | bytes 786464 | tf_op jit(solution)/shard_map/ppermute | solution.py:173
  47.7 5.4 %collective-permute-start.3 = (bf16[512,768]{1,0:T(8,128)(2,1)S(1)}, bf16[512,768]{1,0:T(8,128)(2,1)S(1)}, u32[]{:S(2)}, u32[]{:S(2)}) collective-permute-start(bf16[512,768]{1,0:T(8,128)(2,1)S(1)} %collective-permute-done.1.refs_2_), channel_id=1, source_target_pairs={{0,7},{1,0},{2,1},{3,2},{4,3},{5,4},{6,5},{7,6},{8,15},{9,8},{10,9... | collective-permute-start | bytes 2359304 | tf_op jit(solution)/shard_map/ppermute | solution.py:173
  53.1 1.9 %collective-permute-start.2 = (bf16[512,768]{1,0:T(8,128)(2,1)S(1)}, bf16[512,768]{1,0:T(8,128)(2,1)S(1)}, u32[]{:S(2)}, u32[]{:S(2)}) collective-permute-start(bf16[512,768]{1,0:T(8,128)(2,1)S(1)} %collective-permute-done.refs_1_), channel_id=1, source_target_pairs={{0,1},{1,2},{2,3},{3,4},{4,5},{5,6},{6,7},{7,0},{8,9},{9,10},{10,1... | collective-permute-start | bytes 2359304 | tf_op jit(solution)/shard_map/ppermute | solution.py:172
  55.0 11.5 %collective-permute-done.3.refs_4_ = bf16[512,768]{1,0:T(8,128)(2,1)S(1)} collective-permute-done((bf16[512,768]{1,0:T(8,128)(2,1)S(1)}, bf16[512,768]{1,0:T(8,128)(2,1)S(1)}, u32[]{:S(2)}, u32[]{:S(2)}) %collective-permute-start.3) | collective-permute-done | bytes 786464 | tf_op jit(solution)/shard_map/ppermute | solution.py:173
  66.5 5.4 %collective-permute-start.5 = (bf16[512,768]{1,0:T(8,128)(2,1)S(1)}, bf16[512,768]{1,0:T(8,128)(2,1)S(1)}, u32[]{:S(2)}, u32[]{:S(2)}) collective-permute-start(bf16[512,768]{1,0:T(8,128)(2,1)S(1)} %collective-permute-done.3.refs_4_), channel_id=1, source_target_pairs={{0,7},{1,0},{2,1},{3,2},{4,3},{5,4},{6,5},{7,6},{8,15},{9,8},{10,9... | collective-permute-start | bytes 2359304 | tf_op jit(solution)/shard_map/ppermute | solution.py:173
  72.0 1.9 %collective-permute-start.4 = (bf16[512,768]{1,0:T(8,128)(2,1)S(1)}, bf16[512,768]{1,0:T(8,128)(2,1)S(1)}, u32[]{:S(2)}, u32[]{:S(2)}) collective-permute-start(bf16[512,768]{1,0:T(8,128)(2,1)S(1)} %collective-permute-done.2.refs_3_), channel_id=1, source_target_pairs={{0,1},{1,2},{2,3},{3,4},{4,5},{5,6},{6,7},{7,0},{8,9},{9,10},{10,1... | collective-permute-start | bytes 2359304 | tf_op jit(solution)/shard_map/ppermute | solution.py:172
  73.9 10.7 %collective-permute-done.5.refs_6_ = bf16[512,768]{1,0:T(8,128)(2,1)S(1)} collective-permute-done((bf16[512,768]{1,0:T(8,128)(2,1)S(1)}, bf16[512,768]{1,0:T(8,128)(2,1)S(1)}, u32[]{:S(2)}, u32[]{:S(2)}) %collective-permute-start.5) | collective-permute-done | bytes 786464 | tf_op jit(solution)/shard_map/ppermute | solution.py:173
  84.6 5.4 %collective-permute-start.7 = (bf16[256,768]{1,0:T(8,128)(2,1)S(1)}, bf16[256,768]{1,0:T(8,128)(2,1)S(1)}, u32[]{:S(2)}, u32[]{:S(2)}) collective-permute-start(bf16[256,768]{1,0:T(8,128)(2,1)S(1)} %slice.9), channel_id=1, source_target_pairs={{0,7},{1,0},{2,1},{3,2},{4,3},{5,4},{6,5},{7,6},{8,15},{9,8},{10,9... | collective-permute-start | bytes 1179656 | tf_op jit(solution)/shard_map/ppermute | solution.py:178
  90.1 1.9 %collective-permute-start.6 = (bf16[256,768]{1,0:T(8,128)(2,1)S(1)}, bf16[256,768]{1,0:T(8,128)(2,1)}, u32[]{:S(2)}, u32[]{:S(2)}) collective-permute-start(bf16[256,768]{1,0:T(8,128)(2,1)S(1)} %slice.8), channel_id=1, source_target_pairs={{0,1},{1,2},{2,3},{3,4},{4,5},{5,6},{6,7},{7,0},{8,9},{9,10},{10,1... | collective-permute-start | bytes 1179656 | tf_op jit(solution)/shard_map/ppermute | solution.py:177
  92.1 0.6 pad_add_fusion.own
  92.7 2.4 %pack.1 = bf16[64,16,256]{2,1,0:T(8,128)(2,1)} custom-call(s32[64]{0:T(128)} %lengths.5, s32[64]{0:T(128)} %shifts.5, s32[2]{0:T(128)} %pad_add_fusion.own, f32[96,896]{1,0:T(8,128)} %first.1, f32[96,896]{1,0:T(8,128)} %second.1), custom_call_target="tpu_custom_call" | custom-call | tf_op jit(solution)/shard_map/pack/pallas_call | solution.py:199
  95.0 4.9 %collective-permute-done.6.refs_7_ = bf16[256,768]{1,0:T(8,128)(2,1)} collective-permute-done((bf16[256,768]{1,0:T(8,128)(2,1)S(1)}, bf16[256,768]{1,0:T(8,128)(2,1)}, u32[]{:S(2)}, u32[]{:S(2)}) %collective-permute-start.6) | collective-permute-done | bytes 393248 | tf_op jit(solution)/shard_map/ppermute | solution.py:177
  100.0 15.0 %all-to-all-start = ((bf16[64,16,256]{2,1,0:T(8,128)(2,1)}), bf16[64,16,256]{2,1,0:T(8,128)(2,1)S(1)}, u32[]{:S(2)}, u32[]{:S(2)}) async-start(bf16[64,16,256]{2,1,0:T(8,128)(2,1)} %pack.1), calls=%async_computation | async-start | bytes 1048576 | tf_op jit(solution)/shard_map/all_to_all | solution.py:209
  114.9 0.0 all-gather.2.cloned.1.call-done
  115.0 23.0 %product.1 = (f32[96,896]{1,0:T(8,128)}, bf16[512,768]{1,0:T(8,128)(2,1)}, bf16[512,128]{1,0:T(8,128)(2,1)}) custom-call(s32[64]{0:T(128)} %lengths.5, s32[64]{0:T(128)} %shifts.5, s32[2]{0:T(128)} %pad_add_fusion.own, bf16[8,2,4,672,128]{4,3,2,1,0:T(8,128)(2,1)} %bitcast.6, bf16[512,768]{1,0:T(8,128)(2,1)} %copy-done.4, bf16[512,768]{1,0:T(8,128)(2,1)} %copy-done.6, ...), custom_call_target="tpu_custom_call" | custom-call | flops 5637144576 | bytes 17301504 | tf_op jit(solution)/shard_map/product/pallas_call | solution.py:214
  138.0 0.8 copy-done.1
  138.8 2.5 %unpack.1 = (f32[96,896]{1,0:T(8,128)}, f32[96,896]{1,0:T(8,128)}) custom-call(s32[64]{0:T(128)} %lengths.5, s32[64]{0:T(128)} %shifts.5, s32[2]{0:T(128)} %pad_add_fusion.own, bf16[64,16,256]{2,1,0:T(8,128)(2,1)} %copy-done.1), custom_call_target="tpu_custom_call" | custom-call | tf_op jit(solution)/shard_map/unpack/pallas_call | solution.py:248
  (28 shorter events, 0.1 us)
Async XLA Ops:
  7.2 14.2 %copy-start = (bf16[512,768]{1,0:T(8,128)(2,1)S(1)}, bf16[512,768]{1,0:T(8,128)(2,1)}, u32[]{:S(2)}) copy-start(bf16[512,768]{1,0:T(8,128)(2,1)} %param.6) | copy-start | bytes 2359300
  7.2 107.8 %all-gather.2.cloned.1.call-start = ((), (), s32[]{:S(2)}) async-start(), calls=%async_computation.1 | async-start | bytes 11698176 | tf_op jit(solution)/shard_map/all_gather | solution.py:190
  22.4 69.7 %copy-start.4 = (bf16[512,768]{1,0:T(8,128)(2,1)}, bf16[512,768]{1,0:T(8,128)(2,1)S(1)}, u32[]{:S(2)}) copy-start(bf16[512,768]{1,0:T(8,128)(2,1)S(1)} %fusion.2.refs_0_) | copy-start | bytes 2359300
  22.4 25.3 %collective-permute-start.1 = (bf16[512,768]{1,0:T(8,128)(2,1)S(1)}, bf16[512,768]{1,0:T(8,128)(2,1)S(1)}, u32[]{:S(2)}, u32[]{:S(2)}) collective-permute-start(bf16[512,768]{1,0:T(8,128)(2,1)S(1)} %fusion.2.refs_0_), channel_id=1, source_target_pairs={{0,7},{1,0},{2,1},{3,2},{4,3},{5,4},{6,5},{7,6},{8,15},{9,8},{10,9... | collective-permute-start | bytes 2359304 | tf_op jit(solution)/shard_map/ppermute | solution.py:173
  33.4 19.7 %collective-permute-start = (bf16[512,768]{1,0:T(8,128)(2,1)S(1)}, bf16[512,768]{1,0:T(8,128)(2,1)S(1)}, u32[]{:S(2)}, u32[]{:S(2)}) collective-permute-start(bf16[512,768]{1,0:T(8,128)(2,1)S(1)} %fusion.2.refs_0_), channel_id=1, source_target_pairs={{0,1},{1,2},{2,3},{3,4},{4,5},{5,6},{6,7},{7,0},{8,9},{9,10},{10,1... | collective-permute-start | bytes 2359304 | tf_op jit(solution)/shard_map/ppermute | solution.py:172
  47.6 26.3 %copy-start.5 = (bf16[512,768]{1,0:T(8,128)(2,1)}, bf16[512,768]{1,0:T(8,128)(2,1)S(1)}, u32[]{:S(2)}) copy-start(bf16[512,768]{1,0:T(8,128)(2,1)S(1)} %collective-permute-done.1.refs_2_) | copy-start | bytes 2359300
  47.7 18.9 %collective-permute-start.3 = (bf16[512,768]{1,0:T(8,128)(2,1)S(1)}, bf16[512,768]{1,0:T(8,128)(2,1)S(1)}, u32[]{:S(2)}, u32[]{:S(2)}) collective-permute-start(bf16[512,768]{1,0:T(8,128)(2,1)S(1)} %collective-permute-done.1.refs_2_), channel_id=1, source_target_pairs={{0,7},{1,0},{2,1},{3,2},{4,3},{5,4},{6,5},{7,6},{8,15},{9,8},{10,9... | collective-permute-start | bytes 2359304 | tf_op jit(solution)/shard_map/ppermute | solution.py:173
  53.1 20.8 %copy-start.6 = (bf16[512,768]{1,0:T(8,128)(2,1)}, bf16[512,768]{1,0:T(8,128)(2,1)S(1)}, u32[]{:S(2)}) copy-start(bf16[512,768]{1,0:T(8,128)(2,1)S(1)} %collective-permute-done.refs_1_) | copy-start | bytes 2359300
  53.1 18.9 %collective-permute-start.2 = (bf16[512,768]{1,0:T(8,128)(2,1)S(1)}, bf16[512,768]{1,0:T(8,128)(2,1)S(1)}, u32[]{:S(2)}, u32[]{:S(2)}) collective-permute-start(bf16[512,768]{1,0:T(8,128)(2,1)S(1)} %collective-permute-done.refs_1_), channel_id=1, source_target_pairs={{0,1},{1,2},{2,3},{3,4},{4,5},{5,6},{6,7},{7,0},{8,9},{9,10},{10,1... | collective-permute-start | bytes 2359304 | tf_op jit(solution)/shard_map/ppermute | solution.py:172
  66.5 7.4 %copy-start.7 = (bf16[512,768]{1,0:T(8,128)(2,1)}, bf16[512,768]{1,0:T(8,128)(2,1)S(1)}, u32[]{:S(2)}) copy-start(bf16[512,768]{1,0:T(8,128)(2,1)S(1)} %collective-permute-done.3.refs_4_) | copy-start | bytes 2359300
  66.5 18.1 %collective-permute-start.5 = (bf16[512,768]{1,0:T(8,128)(2,1)S(1)}, bf16[512,768]{1,0:T(8,128)(2,1)S(1)}, u32[]{:S(2)}, u32[]{:S(2)}) collective-permute-start(bf16[512,768]{1,0:T(8,128)(2,1)S(1)} %collective-permute-done.3.refs_4_), channel_id=1, source_target_pairs={{0,7},{1,0},{2,1},{3,2},{4,3},{5,4},{6,5},{7,6},{8,15},{9,8},{10,9... | collective-permute-start | bytes 2359304 | tf_op jit(solution)/shard_map/ppermute | solution.py:173
  72.0 20.1 %copy-start.8 = (bf16[512,768]{1,0:T(8,128)(2,1)}, bf16[512,768]{1,0:T(8,128)(2,1)S(1)}, u32[]{:S(2)}) copy-start(bf16[512,768]{1,0:T(8,128)(2,1)S(1)} %collective-permute-done.2.refs_3_) | copy-start | bytes 2359300
  72.0 18.1 %collective-permute-start.4 = (bf16[512,768]{1,0:T(8,128)(2,1)S(1)}, bf16[512,768]{1,0:T(8,128)(2,1)S(1)}, u32[]{:S(2)}, u32[]{:S(2)}) collective-permute-start(bf16[512,768]{1,0:T(8,128)(2,1)S(1)} %collective-permute-done.2.refs_3_), channel_id=1, source_target_pairs={{0,1},{1,2},{2,3},{3,4},{4,5},{5,6},{6,7},{7,0},{8,9},{9,10},{10,1... | collective-permute-start | bytes 2359304 | tf_op jit(solution)/shard_map/ppermute | solution.py:172
  84.6 30.4 %copy-start.2 = (bf16[512,768]{1,0:T(8,128)(2,1)}, bf16[512,768]{1,0:T(8,128)(2,1)S(1)}, u32[]{:S(2)}) copy-start(bf16[512,768]{1,0:T(8,128)(2,1)S(1)} %collective-permute-done.5.refs_6_) | copy-start | bytes 2359300
  84.6 10.4 %collective-permute-start.7 = (bf16[256,768]{1,0:T(8,128)(2,1)S(1)}, bf16[256,768]{1,0:T(8,128)(2,1)S(1)}, u32[]{:S(2)}, u32[]{:S(2)}) collective-permute-start(bf16[256,768]{1,0:T(8,128)(2,1)S(1)} %slice.9), channel_id=1, source_target_pairs={{0,7},{1,0},{2,1},{3,2},{4,3},{5,4},{6,5},{7,6},{8,15},{9,8},{10,9... | collective-permute-start | bytes 1179656 | tf_op jit(solution)/shard_map/ppermute | solution.py:178
  90.1 24.9 %copy-start.3 = (bf16[512,768]{1,0:T(8,128)(2,1)}, bf16[512,768]{1,0:T(8,128)(2,1)S(1)}, u32[]{:S(2)}) copy-start(bf16[512,768]{1,0:T(8,128)(2,1)S(1)} %collective-permute-done.4.refs_5_) | copy-start | bytes 2359300
  90.1 9.8 %collective-permute-start.6 = (bf16[256,768]{1,0:T(8,128)(2,1)S(1)}, bf16[256,768]{1,0:T(8,128)(2,1)}, u32[]{:S(2)}, u32[]{:S(2)}) collective-permute-start(bf16[256,768]{1,0:T(8,128)(2,1)S(1)} %slice.8), channel_id=1, source_target_pairs={{0,1},{1,2},{2,3},{3,4},{4,5},{5,6},{6,7},{7,0},{8,9},{9,10},{10,1... | collective-permute-start | bytes 1179656 | tf_op jit(solution)/shard_map/ppermute | solution.py:177
  95.0 19.9 %copy-start.9 = (bf16[256,768]{1,0:T(8,128)(2,1)}, bf16[256,768]{1,0:T(8,128)(2,1)S(1)}, u32[]{:S(2)}) copy-start(bf16[256,768]{1,0:T(8,128)(2,1)S(1)} %collective-permute-done.7.refs_8_) | copy-start | bytes 1179652
  100.0 38.1 %all-to-all-start = ((bf16[64,16,256]{2,1,0:T(8,128)(2,1)}), bf16[64,16,256]{2,1,0:T(8,128)(2,1)S(1)}, u32[]{:S(2)}, u32[]{:S(2)}) async-start(bf16[64,16,256]{2,1,0:T(8,128)(2,1)} %pack.1), calls=%async_computation | async-start | bytes 1048576 | tf_op jit(solution)/shard_map/all_to_all | solution.py:209
  138.0 0.8 copy-start.1
Sparse Core Ops, SparseCore 0:
  21.5 77.9 all-gather.1

commit v7 on v5

--- a/solution.py
+++ b/solution.py
@@ -27,12 +27,24 @@
 VMEM_LIMIT = 56 * 1024 * 1024
 
 
-def dp_index(y, x, c):
-    return (y * NX + x) * NC + c
-
-
-X_GROUPS = [[dp_index(y, x, c) for x in range(NX)] for y in range(NY) for c in range(NC)]
-Y_GROUPS = [[dp_index(y, x, c) for y in range(NY) for c in range(NC)] for x in range(NX)]
+def dp_moves(dy, dx, dc):
+    moves = []
+    for y in range(NY):
+        for x in range(NX):
+            for c in range(NC):
+                source = (y * NX + x) * NC + c
+                target = ((y + dy) % NY * NX + (x + dx) % NX) * NC + (c + dc) % NC
+                moves.append((source, target))
+    return moves
+
+
+X_UP, X_DOWN = dp_moves(0, 1, 0), dp_moves(0, -1, 0)
+Y_UP, Y_DOWN = dp_moves(1, 0, 0), dp_moves(-1, 0, 0)
+SIBLING = dp_moves(0, 0, 1)
+
+
+def move(array, moves):
+    return lax.ppermute(array, "dp", moves)
 
 
 def pack_kernel(lengths, shifts, own, first, second, out, first_rows, second_rows):
@@ -66,23 +78,24 @@
             state[:, head * HS : (head + 1) * HS] = rows[pl.ds(head, ROWS, stride=HEADS), :]
 
 
-def product_kernel(places, lengths, shifts, own, gathered, *refs):
-    tokens, (master, query, key), (held, rows, weights, total, starts, firsts, sems) = refs[:-10], refs[-10:-7], refs[-7:]
+def product_kernel(places, spans, lengths, shifts, own, *refs):
+    n = len(spans)
+    gathered, tokens, (master, query, key) = refs[:n], refs[n:-10], refs[-10:-7]
+    blocks, rows, weights, total, starts, firsts, sems = refs[-7:]
     group = pl.program_id(0)
     me, my_z = own[0], own[1]
-    blocks = held.reshape(2 * N_DP, SLOTS, HS)
+    my_y, my_x, my_c = me // (NX * NC), (me // NC) % NX, me % NC
 
     def copies(g):
         slots = pl.ds(pl.multiple_of(g * GROUP, GROUP), GROUP)
         return [
             pltpu.make_async_copy(
-                gathered.at[:, c, x, slots, :],
-                held.at[pl.ds(again * NY, NY), x, c, slots, :],
-                sems.at[g, (again * NX + x) * NC + c],
+                gathered[i].at[:, slots, :],
+                blocks.at[low, pl.ds(again * NY + at, count), slots, :],
+                sems.at[g, again * n + i],
             )
             for again in range(2)
-            for x in range(NX)
-            for c in range(NC)
+            for i, (low, at, count) in enumerate(spans)
         ]
 
     @pl.when(group == 0)
@@ -110,8 +123,15 @@
 
         def chunk(part, carry):
             def load(j):
-                base = N_DP - shifts[j] + part * CHUNK
-                return [blocks[base + i, pl.ds(offset, 16), :] for i in range(CHUNK)]
+                found = []
+                for u in range(CHUNK // NY):
+                    low = part * (CHUNK // NY) + u
+                    low_from = (low - shifts[j]) & (NX * NC - 1)
+                    borrow = jnp.where(low < (shifts[j] & (NX * NC - 1)), 1, 0)
+                    y_from = (0 - (shifts[j] >> 3) - borrow - my_y) & (NY - 1)
+                    place = (((low_from >> 1) - my_x) & (NX - 1)) * NC + ((low_from - my_c) & (NC - 1))
+                    found += [blocks[place, y_from + i, pl.ds(offset, 16), :] for i in range(NY)]
+                return found
 
             def later(j, kept):
                 take = sublane >= (starts[j] - offset).astype(jnp.int16)
@@ -119,7 +139,8 @@
 
             kept = lax.fori_loop(begin + 1, end + 1, later, load(begin))
             for i in range(CHUNK):
-                rows[part * CHUNK + i, pl.ds(pl.multiple_of(t * 16, 16), 16), :] = kept[i].astype(jnp.float32)
+                p = i % NY * (NX * NC) + part * (CHUNK // NY) + i // NY
+                rows[p, pl.ds(pl.multiple_of(t * 16, 16), 16), :] = kept[i].astype(jnp.float32)
             return carry
 
         return lax.fori_loop(0, N_DP // CHUNK, chunk, carry)
@@ -162,7 +183,28 @@
 VMEM = pl.BlockSpec(memory_space=pltpu.VMEM)
 
 
-def gather_tokens(tokens, moments):
+def gather_master(block):
+    ups, downs = [block], [block]
+    for _ in range(NY // 2 - 1):
+        ups.append(move(ups[-1], Y_UP))
+        downs.append(move(downs[-1], Y_DOWN))
+    column = jnp.concatenate(downs + [move(ups[-1], Y_UP)] + ups[:0:-1], axis=0)
+    from_below, from_above = move(column, X_UP), move(column, X_DOWN)
+    half = NY // 2
+    parts = [
+        (0, 0, column),
+        (3, 0, from_below),
+        (1, 0, from_above),
+        (2, 0, move(from_below[:half], X_UP)),
+        (2, half, move(from_above[half:], X_DOWN)),
+    ]
+    parts = [(dx * NC, at, part) for dx, at, part in parts] + [
+        (dx * NC + 1, at, move(part, SIBLING)) for dx, at, part in parts
+    ]
+    return tuple((low, at, part.shape[0]) for low, at, part in parts), [part for _, _, part in parts]
+
+
+def gather_tokens(tokens, packed, exchange):
     up = [(z, (z + 1) % N_Z) for z in range(N_Z)]
     down = [(z, (z - 1) % N_Z) for z in range(N_Z)]
     half = tokens.shape[0] // 2
@@ -173,6 +215,9 @@
         from_above = lax.ppermute(from_above, "tensor", down)
         distances += [-distance, distance]
         if distance == 2:
+            from_below, from_above, packed = lax.optimization_barrier((from_below, from_above, packed))
+            moments = exchange(packed)
+        if distance == 3:
             from_below, from_above, moments = lax.optimization_barrier((from_below, from_above, moments))
         arrays += [from_below, from_above]
     distances.append(N_Z // 2)
@@ -188,9 +233,7 @@
     slots = pltpu.VMEM((SLOTS + BUCKET, HS), jnp.float32)
 
     column = old_master.astype(jnp.bfloat16).reshape(SLOTS, HS)
-    row = lax.all_gather(column, "dp", axis_index_groups=X_GROUPS, axis=0, tiled=True)
-    gathered = lax.all_gather(row, "dp", axis_index_groups=Y_GROUPS, axis=0, tiled=True)
-    gathered = gathered.reshape(NY, NC, NX, SLOTS, HS)
+    spans, gathered = gather_master(column[None])
 
     tokens_dev, width = tokens.shape
     old = jnp.arange(width, dtype=jnp.int32)
@@ -206,23 +249,24 @@
         scratch_shapes=[slots, slots],
         name="pack",
     )(piece_lengths, piece_shifts, own, old_first, old_second)
-    received = lax.all_to_all(packed, "dp", split_axis=0, concat_axis=0, tiled=True)
-    new_first, new_second = pl.pallas_call(
-        unpack_kernel,
-        out_shape=[state, state],
-        in_specs=[SMEM] * 3 + [VMEM],
-        out_specs=[VMEM] * 2,
-        scratch_shapes=[slots, slots],
-        name="unpack",
-    )(piece_lengths, piece_shifts, own, received)
-
-    distances, blocks, (new_first, new_second) = gather_tokens(ordered, (new_first, new_second))
+    def exchange(packed):
+        received = lax.all_to_all(packed, "dp", split_axis=0, concat_axis=0, tiled=True)
+        return pl.pallas_call(
+            unpack_kernel,
+            out_shape=[state, state],
+            in_specs=[SMEM] * 3 + [VMEM],
+            out_specs=[VMEM] * 2,
+            scratch_shapes=[slots, slots],
+            name="unpack",
+        )(piece_lengths, piece_shifts, own, received)
+
+    distances, blocks, (new_first, new_second) = gather_tokens(ordered, packed, exchange)
 
     query_cols = HQ // lax.axis_size("tensor") * HS
     key_cols = block_cols - query_cols
     group_cols = P_LOW * GROUP_ROWS
     new_master, query, key = pl.pallas_call(
-        functools.partial(product_kernel, distances),
+        functools.partial(product_kernel, distances, spans),
         grid=(GROUPS,),
         out_shape=[
             state,
@@ -230,7 +274,7 @@
             jax.ShapeDtypeStruct((tokens_dev, key_cols), jnp.bfloat16),
         ],
         in_specs=[SMEM] * 3
-        + [pl.BlockSpec(memory_space=pl.ANY)]
+        + [pl.BlockSpec(memory_space=pl.ANY)] * len(gathered)
         + [pl.BlockSpec((block.shape[0], group_cols), lambda g: (0, g)) for block in blocks],
         out_specs=[
             pl.BlockSpec((GROUP_ROWS, block_cols), lambda g: (g, 0)),
@@ -238,13 +282,13 @@
             pl.BlockSpec((tokens_dev, key_cols), lambda g: (0, 0)),
         ],
         scratch_shapes=[
-            pltpu.VMEM((2 * NY, NX, NC, SLOTS, HS), jnp.bfloat16),
+            pltpu.VMEM((NX * NC, 2 * NY, SLOTS, HS), jnp.bfloat16),
             pltpu.VMEM((N_DP, GROUP, HS), jnp.float32),
             pltpu.VMEM((N_Z * group_cols, block_cols), jnp.bfloat16),
             pltpu.VMEM((tokens_dev, block_cols), jnp.float32),
             pltpu.SMEM((N_DP,), jnp.int32),
             pltpu.SMEM((SLOTS // 16 + 8,), jnp.int32),
-            pltpu.SemaphoreType.DMA((GROUPS, 2 * NX * NC)),
+            pltpu.SemaphoreType.DMA((GROUPS, 2 * len(gathered))),
         ],
         compiler_params=pltpu.CompilerParams(vmem_limit_bytes=VMEM_LIMIT),
         cost_estimate=pl.CostEstimate(
@@ -253,7 +297,7 @@
             transcendentals=0,
         ),
         name="product",
-    )(piece_lengths, piece_shifts, own, gathered, *blocks)
+    )(piece_lengths, piece_shifts, own, *gathered, *blocks)
     return (new_master, new_first, new_second, query, key)
 
 

time: 144 us -> 170 us (1.18)
  starting transfers between devices: 45.9 us -> 96.6 us
  between operations: 14.2 us -> 1.06 us
  blocking collectives: 12.9 us -> 0 us
  waiting for transfers between devices: 36.8 us -> 25.3 us
  local copies, waits for them, and re-layouts: 1.06 us -> 11 us
  Pallas kernels: 27.9 us -> 31.8 us
    ppermute x0 -> x16, starting transfers between devices: none -> 52.6 us  [move(): return lax.ppermute(array, 'dp', moves)]
    ppermute x3, waiting for transfers between devices: 14.6 us -> 0.01 us  [gather_tokens(): from_below = lax.ppermute(from_below, 'tensor', up)]
    all_gather x1 -> x0, blocking collectives: 12.9 us -> none  [per_device(): lax.all_gather(column, 'dp', axis_index_groups=X_GROUPS, axis=0, tiled=True)]
    all_to_all x1, waiting for transfers between devices: 16.3 us -> 4.54 us  [exchange(): lax.all_to_all(packed, 'dp', split_axis=0, concat_axis=0, tiled=True)]
    ppermute x0 -> x16, waiting for transfers between devices: none -> 7.5 us  [move(): return lax.ppermute(array, 'dp', moves)]
    unnamed x14 -> x27, local copies, waits for them, and re-layouts: 0.82 us -> 6.79 us
    ppermute x1, waiting for transfers between devices: 4.82 us -> 10.7 us  [gather_tokens(): arrays.append(lax.ppermute(from_below[:half], 'tensor', up))]
    pallas_call x2, Pallas kernels: 25.5 us -> 29.4 us  [the longest x1 26.9 us: per_device(): pl.pallas_call(functools.partial(product_kernel, distances, spans), grid=...]
  transfers between devices with their start and end apart: 10 -> 25, of which waited for: 5 -> 7; matrix products, arithmetic and copies ran while one was open for 1% -> 6% of each run, Pallas kernels for 3% -> 3%
where the time goes in v7:
time: 170 us; the launch traced here: 168 us
  starting transfers between devices  96.6 us (57%)
  Pallas kernels  31.8 us (19%)
  waiting for transfers between devices  25.3 us (15%)
  local copies, waits for them, and re-layouts  11 us (6%)
  other arithmetic  1.7 us (1%)
    ppermute x16, starting transfers between devices, move(): return lax.ppermute(array, 'dp', moves)  52.6 us
    pallas_call x1, Pallas kernels, per_device(): pl.pallas_call(functools.partial(product_kernel, distances, spans), grid=...  26.9 us
    ppermute x3, starting transfers between devices, gather_tokens(): from_above = lax.ppermute(from_above, 'tensor', down)  21.1 us
    all_to_all x1, starting transfers between devices, exchange(): lax.all_to_all(packed, 'dp', split_axis=0, concat_axis=0, tiled=True)  13.3 us
    ppermute x1, waiting for transfers between devices, gather_tokens(): arrays.append(lax.ppermute(from_below[:half], 'tensor', up))  10.7 us
    ppermute x16, waiting for transfers between devices, move(): return lax.ppermute(array, 'dp', moves)  7.5 us
    unnamed x27, local copies, waits for them, and re-layouts  6.79 us
    ppermute x3, starting transfers between devices, gather_tokens(): from_below = lax.ppermute(from_below, 'tensor', up)  5.76 us
  transfers between devices with their start and end apart: 25, of which 7 were waited for; matrix products, arithmetic and copies ran while one was open for 6% of the time, Pallas kernels for 3%

profile of v7, /device:TPU:1, one launch (start us, length us, event | category | flops | bytes accessed | tf_op | source)
XLA Modules:
  0.0 168.5 jit_solution(12790435320603887470)
XLA Ops:
  1.9 4.0 %collective-permute-start.3 = (bf16[1,672,128]{2,1,0:T(8,128)(2,1)S(1)}, bf16[1,672,128]{2,1,0:T(8,128)(2,1)S(1)}, u32[]{:S(2)}, u32[]{:S(2)}) collective-permute-start(bf16[1,672,128]{2,1,0:T(8,128)(2,1)S(1)} %broadcast_in_dim_reshape.3), channel_id=1, source_target_pairs={{0,64},{8,72},{16,80},{24,88},{32,96},{40,104},{48,112},{56,120},{... | collective-permute-start | bytes 516104 | tf_op jit(solution)/shard_map/ppermute | solution.py:47
  6.0 3.8 %collective-permute-start = (bf16[1,672,128]{2,1,0:T(8,128)(2,1)S(1)}, bf16[1,672,128]{2,1,0:T(8,128)(2,1)S(1)}, u32[]{:S(2)}, u32[]{:S(2)}) collective-permute-start(bf16[1,672,128]{2,1,0:T(8,128)(2,1)S(1)} %broadcast_in_dim_reshape.3), channel_id=1, source_target_pairs={{0,448},{8,456},{16,464},{24,472},{32,480},{40,488},{48,496},{56,5... | collective-permute-start | bytes 516104 | tf_op jit(solution)/shard_map/ppermute | solution.py:47
  13.5 12.0 %collective-permute-start.17 = (bf16[512,768]{1,0:T(8,128)(2,1)S(1)}, bf16[512,768]{1,0:T(8,128)(2,1)S(1)}, u32[]{:S(2)}, u32[]{:S(2)}) collective-permute-start(bf16[512,768]{1,0:T(8,128)(2,1)S(1)} %fusion.2.refs_10_), channel_id=1, source_target_pairs={{0,7},{1,0},{2,1},{3,2},{4,3},{5,4},{6,5},{7,6},{8,15},{9,8},{10,9... | collective-permute-start | bytes 2359304 | tf_op jit(solution)/shard_map/ppermute | solution.py:215
  27.5 4.6 %collective-permute-start.1 = (bf16[1,672,128]{2,1,0:T(8,128)(2,1)S(1)}, bf16[1,672,128]{2,1,0:T(8,128)(2,1)S(1)}, u32[]{:S(2)}, u32[]{:S(2)}) collective-permute-start(bf16[1,672,128]{2,1,0:T(8,128)(2,1)S(1)} %collective-permute-done), channel_id=1, source_target_pairs={{0,448},{8,456},{16,464},{24,472},{32,480},{40,488},{48,496},{56,5... | collective-permute-start | bytes 516104 | tf_op jit(solution)/shard_map/ppermute | solution.py:47
  34.7 5.0 %collective-permute-start.2 = (bf16[1,672,128]{2,1,0:T(8,128)(2,1)S(1)}, bf16[1,672,128]{2,1,0:T(8,128)(2,1)S(1)}, u32[]{:S(2)}, u32[]{:S(2)}) collective-permute-start(bf16[1,672,128]{2,1,0:T(8,128)(2,1)S(1)} %collective-permute-done.1), channel_id=1, source_target_pairs={{0,448},{8,456},{16,464},{24,472},{32,480},{40,488},{48,496},{56,5... | collective-permute-start | bytes 516104 | tf_op jit(solution)/shard_map/ppermute | solution.py:47
  43.6 4.4 %collective-permute-done.6 = bf16[1,672,128]{2,1,0:T(8,128)(2,1)S(1)} collective-permute-done((bf16[1,672,128]{2,1,0:T(8,128)(2,1)S(1)}, bf16[1,672,128]{2,1,0:T(8,128)(2,1)S(1)}, u32[]{:S(2)}, u32[]{:S(2)}) %collective-permute-start.6) | collective-permute-done | bytes 172064 | tf_op jit(solution)/shard_map/ppermute | solution.py:47
  49.4 4.3 %collective-permute-start.19 = (bf16[512,768]{1,0:T(8,128)(2,1)S(1)}, bf16[512,768]{1,0:T(8,128)(2,1)}, u32[]{:S(2)}, u32[]{:S(2)}) collective-permute-start(bf16[512,768]{1,0:T(8,128)(2,1)S(1)} %collective-permute-done.17.refs_12_), channel_id=1, source_target_pairs={{0,7},{1,0},{2,1},{3,2},{4,3},{5,4},{6,5},{7,6},{8,15},{9,8},{10,9... | collective-permute-start | bytes 2359304 | tf_op jit(solution)/shard_map/ppermute | solution.py:215
  53.7 1.9 %collective-permute-start.18 = (bf16[512,768]{1,0:T(8,128)(2,1)S(1)}, bf16[512,768]{1,0:T(8,128)(2,1)}, u32[]{:S(2)}, u32[]{:S(2)}) collective-permute-start(bf16[512,768]{1,0:T(8,128)(2,1)S(1)} %collective-permute-done.16.refs_11_), channel_id=1, source_target_pairs={{0,1},{1,2},{2,3},{3,4},{4,5},{5,6},{6,7},{7,0},{8,9},{9,10},{10,1... | collective-permute-start | bytes 2359304 | tf_op jit(solution)/shard_map/ppermute | solution.py:214
  57.0 4.4 %collective-permute-start.8 = (bf16[8,672,128]{2,1,0:T(8,128)(2,1)}, bf16[8,672,128]{2,1,0:T(8,128)(2,1)}, u32[]{:S(2)}, u32[]{:S(2)}) collective-permute-start(bf16[8,672,128]{2,1,0:T(8,128)(2,1)} %constant_dynamic-update-slice_fusion.refs_0_), channel_id=1, source_target_pairs={{0,48},{8,56},{16,0},{24,8},{32,16},{40,24},{48,32},{56,40},{64,11... | collective-permute-start | bytes 4128776 | tf_op jit(solution)/shard_map/ppermute | solution.py:47
  61.4 1.9 %collective-permute-start.7 = (bf16[8,672,128]{2,1,0:T(8,128)(2,1)}, bf16[8,672,128]{2,1,0:T(8,128)(2,1)}, u32[]{:S(2)}, u32[]{:S(2)}) collective-permute-start(bf16[8,672,128]{2,1,0:T(8,128)(2,1)} %constant_dynamic-update-slice_fusion.refs_0_), channel_id=1, source_target_pairs={{0,16},{8,24},{16,32},{24,40},{32,48},{40,56},{48,0},{56,8},{64,80... | collective-permute-start | bytes 4128776 | tf_op jit(solution)/shard_map/ppermute | solution.py:47
  63.9 2.4 %pack.1 = bf16[64,16,256]{2,1,0:T(8,128)(2,1)} custom-call(s32[64]{0:T(128)} %lengths.5, s32[64]{0:T(128)} %shifts.5, s32[2]{0:T(128)} %pad_add_fusion.own, f32[96,896]{1,0:T(8,128)} %first.1, f32[96,896]{1,0:T(8,128)} %second.1), custom_call_target="tpu_custom_call" | custom-call | tf_op jit(solution)/shard_map/pack/pallas_call | solution.py:244
  66.3 6.8 %collective-permute-start.11 = (bf16[8,672,128]{2,1,0:T(8,128)(2,1)}, bf16[8,672,128]{2,1,0:T(8,128)(2,1)}, u32[]{:S(2)}, u32[]{:S(2)}) collective-permute-start(bf16[8,672,128]{2,1,0:T(8,128)(2,1)} %constant_dynamic-update-slice_fusion.refs_0_), channel_id=1, source_target_pairs={{0,8},{8,0},{16,24},{24,16},{32,40},{40,32},{48,56},{56,48},{64,72... | collective-permute-start | bytes 4128776 | tf_op jit(solution)/shard_map/ppermute | solution.py:47
  75.1 4.9 %collective-permute-start.21 = (bf16[512,768]{1,0:T(8,128)(2,1)}, bf16[512,768]{1,0:T(8,128)(2,1)}, u32[]{:S(2)}, u32[]{:S(2)}) collective-permute-start(bf16[512,768]{1,0:T(8,128)(2,1)} %collective-permute-done.19.refs_14_), channel_id=1, source_target_pairs={{0,7},{1,0},{2,1},{3,2},{4,3},{5,4},{6,5},{7,6},{8,15},{9,8},{10,9... | collective-permute-start | bytes 2359304 | tf_op jit(solution)/shard_map/ppermute | solution.py:215
  79.9 13.3 %all-to-all-start = ((bf16[64,16,256]{2,1,0:T(8,128)(2,1)}), bf16[64,16,256]{2,1,0:T(8,128)(2,1)S(1)}, u32[]{:S(2)}, u32[]{:S(2)}) async-start(bf16[64,16,256]{2,1,0:T(8,128)(2,1)} %pack.1), calls=%async_computation | async-start | bytes 1048576 | tf_op jit(solution)/shard_map/all_to_all | solution.py:253
  94.4 4.5 %collective-permute-start.10 = (bf16[4,672,128]{2,1,0:T(8,128)(2,1)S(1)}, bf16[4,672,128]{2,1,0:T(8,128)(2,1)}, u32[]{:S(2)}, u32[]{:S(2)}) collective-permute-start(bf16[4,672,128]{2,1,0:T(8,128)(2,1)S(1)} %slice.17), channel_id=1, source_target_pairs={{0,48},{8,56},{16,0},{24,8},{32,16},{40,24},{48,32},{56,40},{64,11... | collective-permute-start | bytes 2064392 | tf_op jit(solution)/shard_map/ppermute | solution.py:47
  100.1 1.9 %collective-permute-start.9 = (bf16[4,672,128]{2,1,0:T(8,128)(2,1)S(1)}, bf16[4,672,128]{2,1,0:T(8,128)(2,1)}, u32[]{:S(2)}, u32[]{:S(2)}) collective-permute-start(bf16[4,672,128]{2,1,0:T(8,128)(2,1)S(1)} %slice.16), channel_id=1, source_target_pairs={{0,16},{8,24},{16,32},{24,40},{32,48},{40,56},{48,0},{56,8},{64,80... | collective-permute-start | bytes 2064392 | tf_op jit(solution)/shard_map/ppermute | solution.py:47
  102.0 2.6 %collective-permute-start.13 = (bf16[8,672,128]{2,1,0:T(8,128)(2,1)}, bf16[8,672,128]{2,1,0:T(8,128)(2,1)}, u32[]{:S(2)}, u32[]{:S(2)}) collective-permute-start(bf16[8,672,128]{2,1,0:T(8,128)(2,1)} %collective-permute-done.8.refs_2_), channel_id=1, source_target_pairs={{0,8},{8,0},{16,24},{24,16},{32,40},{40,32},{48,56},{56,48},{64,72... | collective-permute-start | bytes 4128776 | tf_op jit(solution)/shard_map/ppermute | solution.py:47
  106.5 4.5 %all-to-all-done.received = bf16[64,16,256]{2,1,0:T(8,128)(2,1)S(1)} async-done(((bf16[64,16,256]{2,1,0:T(8,128)(2,1)}), bf16[64,16,256]{2,1,0:T(8,128)(2,1)S(1)}, u32[]{:S(2)}, u32[]{:S(2)}) %all-to-all-start) | async-done | bytes 524320 | tf_op jit(solution)/shard_map/all_to_all | solution.py:253
  111.9 2.5 %unpack.1 = (f32[96,896]{1,0:T(8,128)}, f32[96,896]{1,0:T(8,128)}) custom-call(s32[64]{0:T(128)} %lengths.5, s32[64]{0:T(128)} %shifts.5, s32[2]{0:T(128)} %pad_add_fusion.own, bf16[64,16,256]{2,1,0:T(8,128)(2,1)} %copy-done.1), custom_call_target="tpu_custom_call" | custom-call | tf_op jit(solution)/shard_map/unpack/pallas_call | solution.py:254
  117.8 2.7 %collective-permute-start.15 = (bf16[4,672,128]{2,1,0:T(8,128)(2,1)}, bf16[4,672,128]{2,1,0:T(8,128)(2,1)S(1)}, u32[]{:S(2)}, u32[]{:S(2)}) collective-permute-start(bf16[4,672,128]{2,1,0:T(8,128)(2,1)} %collective-permute-done.10.refs_4_), channel_id=1, source_target_pairs={{0,8},{8,0},{16,24},{24,16},{32,40},{40,32},{48,56},{56,48},{64,72... | collective-permute-start | bytes 2064392 | tf_op jit(solution)/shard_map/ppermute | solution.py:47
  122.3 2.7 %collective-permute-start.14 = (bf16[4,672,128]{2,1,0:T(8,128)(2,1)}, bf16[4,672,128]{2,1,0:T(8,128)(2,1)S(1)}, u32[]{:S(2)}, u32[]{:S(2)}) collective-permute-start(bf16[4,672,128]{2,1,0:T(8,128)(2,1)} %collective-permute-done.9.refs_3_), channel_id=1, source_target_pairs={{0,8},{8,0},{16,24},{24,16},{32,40},{40,32},{48,56},{56,48},{64,72... | collective-permute-start | bytes 2064392 | tf_op jit(solution)/shard_map/ppermute | solution.py:47
  125.1 2.6 %collective-permute-done.23.refs_18_ = bf16[256,768]{1,0:T(8,128)(2,1)S(1)} collective-permute-done((bf16[256,768]{1,0:T(8,128)(2,1)S(1)}, bf16[256,768]{1,0:T(8,128)(2,1)S(1)}, u32[]{:S(2)}, u32[]{:S(2)}) %collective-permute-start.23) | collective-permute-done | bytes 393248 | tf_op jit(solution)/shard_map/ppermute | solution.py:225
  129.6 10.7 %collective-permute-done.22.refs_17_ = bf16[256,768]{1,0:T(8,128)(2,1)S(1)} collective-permute-done((bf16[256,768]{1,0:T(8,128)(2,1)S(1)}, bf16[256,768]{1,0:T(8,128)(2,1)S(1)}, u32[]{:S(2)}, u32[]{:S(2)}) %collective-permute-start.22) | collective-permute-done | bytes 393248 | tf_op jit(solution)/shard_map/ppermute | solution.py:224
  141.5 26.9 %product.1 = (f32[96,896]{1,0:T(8,128)}, bf16[512,768]{1,0:T(8,128)(2,1)}, bf16[512,128]{1,0:T(8,128)(2,1)}) custom-call(s32[64]{0:T(128)} %lengths.5, s32[64]{0:T(128)} %shifts.5, s32[2]{0:T(128)} %pad_add_fusion.own, bf16[8,672,128]{2,1,0:T(8,128)(2,1)} %constant_dynamic-update-slice_fusion.refs_0_, bf16[8,672,128]{2,1,0:T(8,128)(2,1)} %collective-permute-done.7.refs_1_, ...), custom_call_target="tpu_custom_call" | custom-call | flops 5637144576 | bytes 17301504 | tf_op jit(solution)/shard_map/product/pallas_call | solution.py:268
  (66 shorter events, 32.1 us)
Async XLA Ops:
  1.9 8.7 %collective-permute-start.3 = (bf16[1,672,128]{2,1,0:T(8,128)(2,1)S(1)}, bf16[1,672,128]{2,1,0:T(8,128)(2,1)S(1)}, u32[]{:S(2)}, u32[]{:S(2)}) collective-permute-start(bf16[1,672,128]{2,1,0:T(8,128)(2,1)S(1)} %broadcast_in_dim_reshape.3), channel_id=1, source_target_pairs={{0,64},{8,72},{16,80},{24,88},{32,96},{40,104},{48,112},{56,120},{... | collective-permute-start | bytes 516104 | tf_op jit(solution)/shard_map/ppermute | solution.py:47
  6.0 21.5 %collective-permute-start = (bf16[1,672,128]{2,1,0:T(8,128)(2,1)S(1)}, bf16[1,672,128]{2,1,0:T(8,128)(2,1)S(1)}, u32[]{:S(2)}, u32[]{:S(2)}) collective-permute-start(bf16[1,672,128]{2,1,0:T(8,128)(2,1)S(1)} %broadcast_in_dim_reshape.3), channel_id=1, source_target_pairs={{0,448},{8,456},{16,464},{24,472},{32,480},{40,488},{48,496},{56,5... | collective-permute-start | bytes 516104 | tf_op jit(solution)/shard_map/ppermute | solution.py:47
  10.6 21.4 %collective-permute-start.4 = (bf16[1,672,128]{2,1,0:T(8,128)(2,1)S(1)}, bf16[1,672,128]{2,1,0:T(8,128)(2,1)S(1)}, u32[]{:S(2)}, u32[]{:S(2)}) collective-permute-start(bf16[1,672,128]{2,1,0:T(8,128)(2,1)S(1)} %collective-permute-done.3), channel_id=1, source_target_pairs={{0,64},{8,72},{16,80},{24,88},{32,96},{40,104},{48,112},{56,120},{... | collective-permute-start | bytes 516104 | tf_op jit(solution)/shard_map/ppermute | solution.py:47
  13.5 35.9 %collective-permute-start.17 = (bf16[512,768]{1,0:T(8,128)(2,1)S(1)}, bf16[512,768]{1,0:T(8,128)(2,1)S(1)}, u32[]{:S(2)}, u32[]{:S(2)}) collective-permute-start(bf16[512,768]{1,0:T(8,128)(2,1)S(1)} %fusion.2.refs_10_), channel_id=1, source_target_pairs={{0,7},{1,0},{2,1},{3,2},{4,3},{5,4},{6,5},{7,6},{8,15},{9,8},{10,9... | collective-permute-start | bytes 2359304 | tf_op jit(solution)/shard_map/ppermute | solution.py:215
  25.5 28.2 %collective-permute-start.16 = (bf16[512,768]{1,0:T(8,128)(2,1)S(1)}, bf16[512,768]{1,0:T(8,128)(2,1)S(1)}, u32[]{:S(2)}, u32[]{:S(2)}) collective-permute-start(bf16[512,768]{1,0:T(8,128)(2,1)S(1)} %fusion.2.refs_10_), channel_id=1, source_target_pairs={{0,1},{1,2},{2,3},{3,4},{4,5},{5,6},{6,7},{7,0},{8,9},{9,10},{10,1... | collective-permute-start | bytes 2359304 | tf_op jit(solution)/shard_map/ppermute | solution.py:214
  32.0 8.3 %collective-permute-start.5 = (bf16[1,672,128]{2,1,0:T(8,128)(2,1)S(1)}, bf16[1,672,128]{2,1,0:T(8,128)(2,1)S(1)}, u32[]{:S(2)}, u32[]{:S(2)}) collective-permute-start(bf16[1,672,128]{2,1,0:T(8,128)(2,1)S(1)} %collective-permute-done.4), channel_id=1, source_target_pairs={{0,64},{8,72},{16,80},{24,88},{32,96},{40,104},{48,112},{56,120},{... | collective-permute-start | bytes 516104 | tf_op jit(solution)/shard_map/ppermute | solution.py:47
  34.7 8.3 %collective-permute-start.2 = (bf16[1,672,128]{2,1,0:T(8,128)(2,1)S(1)}, bf16[1,672,128]{2,1,0:T(8,128)(2,1)S(1)}, u32[]{:S(2)}, u32[]{:S(2)}) collective-permute-start(bf16[1,672,128]{2,1,0:T(8,128)(2,1)S(1)} %collective-permute-done.1), channel_id=1, source_target_pairs={{0,448},{8,456},{16,464},{24,472},{32,480},{40,488},{48,496},{56,5... | collective-permute-start | bytes 516104 | tf_op jit(solution)/shard_map/ppermute | solution.py:47
  40.4 7.6 %collective-permute-start.6 = (bf16[1,672,128]{2,1,0:T(8,128)(2,1)S(1)}, bf16[1,672,128]{2,1,0:T(8,128)(2,1)S(1)}, u32[]{:S(2)}, u32[]{:S(2)}) collective-permute-start(bf16[1,672,128]{2,1,0:T(8,128)(2,1)S(1)} %collective-permute-done.5), channel_id=1, source_target_pairs={{0,64},{8,72},{16,80},{24,88},{32,96},{40,104},{48,112},{56,120},{... | collective-permute-start | bytes 516104 | tf_op jit(solution)/shard_map/ppermute | solution.py:47
  49.4 23.7 %collective-permute-start.19 = (bf16[512,768]{1,0:T(8,128)(2,1)S(1)}, bf16[512,768]{1,0:T(8,128)(2,1)}, u32[]{:S(2)}, u32[]{:S(2)}) collective-permute-start(bf16[512,768]{1,0:T(8,128)(2,1)S(1)} %collective-permute-done.17.refs_12_), channel_id=1, source_target_pairs={{0,7},{1,0},{2,1},{3,2},{4,3},{5,4},{6,5},{7,6},{8,15},{9,8},{10,9... | collective-permute-start | bytes 2359304 | tf_op jit(solution)/shard_map/ppermute | solution.py:215
  53.7 19.4 %collective-permute-start.18 = (bf16[512,768]{1,0:T(8,128)(2,1)S(1)}, bf16[512,768]{1,0:T(8,128)(2,1)}, u32[]{:S(2)}, u32[]{:S(2)}) collective-permute-start(bf16[512,768]{1,0:T(8,128)(2,1)S(1)} %collective-permute-done.16.refs_11_), channel_id=1, source_target_pairs={{0,1},{1,2},{2,3},{3,4},{4,5},{5,6},{6,7},{7,0},{8,9},{9,10},{10,1... | collective-permute-start | bytes 2359304 | tf_op jit(solution)/shard_map/ppermute | solution.py:214
  57.0 36.2 %collective-permute-start.8 = (bf16[8,672,128]{2,1,0:T(8,128)(2,1)}, bf16[8,672,128]{2,1,0:T(8,128)(2,1)}, u32[]{:S(2)}, u32[]{:S(2)}) collective-permute-start(bf16[8,672,128]{2,1,0:T(8,128)(2,1)} %constant_dynamic-update-slice_fusion.refs_0_), channel_id=1, source_target_pairs={{0,48},{8,56},{16,0},{24,8},{32,16},{40,24},{48,32},{56,40},{64,11... | collective-permute-start | bytes 4128776 | tf_op jit(solution)/shard_map/ppermute | solution.py:47
  61.4 37.5 %collective-permute-start.7 = (bf16[8,672,128]{2,1,0:T(8,128)(2,1)}, bf16[8,672,128]{2,1,0:T(8,128)(2,1)}, u32[]{:S(2)}, u32[]{:S(2)}) collective-permute-start(bf16[8,672,128]{2,1,0:T(8,128)(2,1)} %constant_dynamic-update-slice_fusion.refs_0_), channel_id=1, source_target_pairs={{0,16},{8,24},{16,32},{24,40},{32,48},{40,56},{48,0},{56,8},{64,80... | collective-permute-start | bytes 4128776 | tf_op jit(solution)/shard_map/ppermute | solution.py:47
  66.3 49.1 %collective-permute-start.11 = (bf16[8,672,128]{2,1,0:T(8,128)(2,1)}, bf16[8,672,128]{2,1,0:T(8,128)(2,1)}, u32[]{:S(2)}, u32[]{:S(2)}) collective-permute-start(bf16[8,672,128]{2,1,0:T(8,128)(2,1)} %constant_dynamic-update-slice_fusion.refs_0_), channel_id=1, source_target_pairs={{0,8},{8,0},{16,24},{24,16},{32,40},{40,32},{48,56},{56,48},{64,72... | collective-permute-start | bytes 4128776 | tf_op jit(solution)/shard_map/ppermute | solution.py:47
  73.1 28.9 %collective-permute-start.20 = (bf16[512,768]{1,0:T(8,128)(2,1)}, bf16[512,768]{1,0:T(8,128)(2,1)S(1)}, u32[]{:S(2)}, u32[]{:S(2)}) collective-permute-start(bf16[512,768]{1,0:T(8,128)(2,1)} %collective-permute-done.18.refs_13_), channel_id=1, source_target_pairs={{0,1},{1,2},{2,3},{3,4},{4,5},{5,6},{6,7},{7,0},{8,9},{9,10},{10,1... | collective-permute-start | bytes 2359304 | tf_op jit(solution)/shard_map/ppermute | solution.py:214
  75.1 29.5 %collective-permute-start.21 = (bf16[512,768]{1,0:T(8,128)(2,1)}, bf16[512,768]{1,0:T(8,128)(2,1)}, u32[]{:S(2)}, u32[]{:S(2)}) collective-permute-start(bf16[512,768]{1,0:T(8,128)(2,1)} %collective-permute-done.19.refs_14_), channel_id=1, source_target_pairs={{0,7},{1,0},{2,1},{3,2},{4,3},{5,4},{6,5},{7,6},{8,15},{9,8},{10,9... | collective-permute-start | bytes 2359304 | tf_op jit(solution)/shard_map/ppermute | solution.py:215
  79.9 31.1 %all-to-all-start = ((bf16[64,16,256]{2,1,0:T(8,128)(2,1)}), bf16[64,16,256]{2,1,0:T(8,128)(2,1)S(1)}, u32[]{:S(2)}, u32[]{:S(2)}) async-start(bf16[64,16,256]{2,1,0:T(8,128)(2,1)} %pack.1), calls=%async_computation | async-start | bytes 1048576 | tf_op jit(solution)/shard_map/all_to_all | solution.py:253
  94.4 23.4 %collective-permute-start.10 = (bf16[4,672,128]{2,1,0:T(8,128)(2,1)S(1)}, bf16[4,672,128]{2,1,0:T(8,128)(2,1)}, u32[]{:S(2)}, u32[]{:S(2)}) collective-permute-start(bf16[4,672,128]{2,1,0:T(8,128)(2,1)S(1)} %slice.17), channel_id=1, source_target_pairs={{0,48},{8,56},{16,0},{24,8},{32,16},{40,24},{48,32},{56,40},{64,11... | collective-permute-start | bytes 2064392 | tf_op jit(solution)/shard_map/ppermute | solution.py:47
  100.1 22.2 %collective-permute-start.9 = (bf16[4,672,128]{2,1,0:T(8,128)(2,1)S(1)}, bf16[4,672,128]{2,1,0:T(8,128)(2,1)}, u32[]{:S(2)}, u32[]{:S(2)}) collective-permute-start(bf16[4,672,128]{2,1,0:T(8,128)(2,1)S(1)} %slice.16), channel_id=1, source_target_pairs={{0,16},{8,24},{16,32},{24,40},{32,48},{40,56},{48,0},{56,8},{64,80... | collective-permute-start | bytes 2064392 | tf_op jit(solution)/shard_map/ppermute | solution.py:47
  102.0 38.3 %collective-permute-start.13 = (bf16[8,672,128]{2,1,0:T(8,128)(2,1)}, bf16[8,672,128]{2,1,0:T(8,128)(2,1)}, u32[]{:S(2)}, u32[]{:S(2)}) collective-permute-start(bf16[8,672,128]{2,1,0:T(8,128)(2,1)} %collective-permute-done.8.refs_2_), channel_id=1, source_target_pairs={{0,8},{8,0},{16,24},{24,16},{32,40},{40,32},{48,56},{56,48},{64,72... | collective-permute-start | bytes 4128776 | tf_op jit(solution)/shard_map/ppermute | solution.py:47
  104.6 35.8 %collective-permute-start.12 = (bf16[8,672,128]{2,1,0:T(8,128)(2,1)}, bf16[8,672,128]{2,1,0:T(8,128)(2,1)}, u32[]{:S(2)}, u32[]{:S(2)}) collective-permute-start(bf16[8,672,128]{2,1,0:T(8,128)(2,1)} %collective-permute-done.7.refs_1_), channel_id=1, source_target_pairs={{0,8},{8,0},{16,24},{24,16},{32,40},{40,32},{48,56},{56,48},{64,72... | collective-permute-start | bytes 4128776 | tf_op jit(solution)/shard_map/ppermute | solution.py:47
  115.4 12.3 %collective-permute-start.23 = (bf16[256,768]{1,0:T(8,128)(2,1)S(1)}, bf16[256,768]{1,0:T(8,128)(2,1)S(1)}, u32[]{:S(2)}, u32[]{:S(2)}) collective-permute-start(bf16[256,768]{1,0:T(8,128)(2,1)S(1)} %slice.15), channel_id=1, source_target_pairs={{0,7},{1,0},{2,1},{3,2},{4,3},{5,4},{6,5},{7,6},{8,15},{9,8},{10,9... | collective-permute-start | bytes 1179656 | tf_op jit(solution)/shard_map/ppermute | solution.py:225
  117.8 22.5 %collective-permute-start.15 = (bf16[4,672,128]{2,1,0:T(8,128)(2,1)}, bf16[4,672,128]{2,1,0:T(8,128)(2,1)S(1)}, u32[]{:S(2)}, u32[]{:S(2)}) collective-permute-start(bf16[4,672,128]{2,1,0:T(8,128)(2,1)} %collective-permute-done.10.refs_4_), channel_id=1, source_target_pairs={{0,8},{8,0},{16,24},{24,16},{32,40},{40,32},{48,56},{56,48},{64,72... | collective-permute-start | bytes 2064392 | tf_op jit(solution)/shard_map/ppermute | solution.py:47
  122.3 18.0 %collective-permute-start.14 = (bf16[4,672,128]{2,1,0:T(8,128)(2,1)}, bf16[4,672,128]{2,1,0:T(8,128)(2,1)S(1)}, u32[]{:S(2)}, u32[]{:S(2)}) collective-permute-start(bf16[4,672,128]{2,1,0:T(8,128)(2,1)} %collective-permute-done.9.refs_3_), channel_id=1, source_target_pairs={{0,8},{8,0},{16,24},{24,16},{32,40},{40,32},{48,56},{56,48},{64,72... | collective-permute-start | bytes 2064392 | tf_op jit(solution)/shard_map/ppermute | solution.py:47
  127.7 12.6 %collective-permute-start.22 = (bf16[256,768]{1,0:T(8,128)(2,1)S(1)}, bf16[256,768]{1,0:T(8,128)(2,1)S(1)}, u32[]{:S(2)}, u32[]{:S(2)}) collective-permute-start(bf16[256,768]{1,0:T(8,128)(2,1)S(1)} %slice.14), channel_id=1, source_target_pairs={{0,1},{1,2},{2,3},{3,4},{4,5},{5,6},{6,7},{7,0},{8,9},{9,10},{10,1... | collective-permute-start | bytes 1179656 | tf_op jit(solution)/shard_map/ppermute | solution.py:224
  (11 other events, 174.1 us)

commit v8 on v5

--- a/solution.py
+++ b/solution.py
@@ -21,6 +21,7 @@
 GROUP_ROWS = 32
 GROUP = GROUP_ROWS * HEADS
 GROUPS = SLOTS // GROUP
+STEP = 112
 CHUNK = 32
 N_Z = 8
 P_LOW = N_DP // N_Z
@@ -67,95 +68,125 @@
 
 
 def product_kernel(places, lengths, shifts, own, gathered, *refs):
-    tokens, (master, query, key), (held, rows, weights, total, starts, firsts, sems) = refs[:-10], refs[-10:-7], refs[-7:]
-    group = pl.program_id(0)
+    tokens, (master, query, key), (held, columns, rows, weights, total, starts, firsts, sems, token_sems) = (
+        refs[:-12],
+        refs[-12:-9],
+        refs[-9:],
+    )
     me, my_z = own[0], own[1]
-    blocks = held.reshape(2 * N_DP, SLOTS, HS)
-
-    def copies(g):
-        slots = pl.ds(pl.multiple_of(g * GROUP, GROUP), GROUP)
+    blocks = held.reshape(N_DP + CHUNK, SLOTS, HS)
+    half = tokens[-1].shape[0]
+
+    def copies(step):
+        slots = pl.ds(step * STEP, STEP)
         return [
             pltpu.make_async_copy(
-                gathered.at[:, c, x, slots, :],
-                held.at[pl.ds(again * NY, NY), x, c, slots, :],
-                sems.at[g, (again * NX + x) * NC + c],
+                gathered.at[pl.ds(0, count), c, :, slots, :],
+                held.at[pl.ds(at, count), :, c, slots, :],
+                sems.at[step, again * NC + c],
             )
-            for again in range(2)
-            for x in range(NX)
+            for again, (at, count) in enumerate(((0, NY), (NY, CHUNK // (NX * NC))))
             for c in range(NC)
         ]
 
-    @pl.when(group == 0)
-    def _():
-        for g in range(GROUPS):
-            for copy in copies(g):
+    def token_copies(group):
+        wide = P_LOW * GROUP_ROWS
+        found = []
+        for i, block in enumerate(tokens):
+            last = i == len(tokens) - 1
+            found.append(
+                pltpu.make_async_copy(
+                    block.at[:, pl.ds(group * wide, wide)],
+                    columns.at[
+                        group, pl.ds(half if last else 0, block.shape[0]), pl.ds((i - 1 if last else i) * wide, wide)
+                    ],
+                    token_sems.at[group, i],
+                )
+            )
+        return found
+
+    per_group = GROUP // STEP
+    for group in range(GROUPS):
+        for step in range(group * per_group, (group + 1) * per_group):
+            for copy in copies(step):
                 copy.start()
-
-        def piece(j, start):
-            starts[j] = start
-            firsts[(start + 15) >> 4] = j
-            return start + lengths[j]
-
-        lax.fori_loop(0, N_DP, piece, jnp.int32(0))
-
-    for copy in copies(group):
-        copy.wait()
-
+        for copy in token_copies(group):
+            copy.start()
+
+    def piece(j, start):
+        starts[j] = start
+        firsts[(start + 15) >> 4] = j
+        return start + lengths[j]
+
+    lax.fori_loop(0, N_DP, piece, jnp.int32(0))
     sublane = lax.broadcasted_iota(jnp.int32, (16, HS), 0).astype(jnp.int16)
 
-    def tile(t, carry):
-        whole = group * (GROUP // 16) + t
-        offset = pl.multiple_of(whole * 16, 16)
-        begin, end = firsts[whole], firsts[whole + 1]
-
-        def chunk(part, carry):
-            def load(j):
-                base = N_DP - shifts[j] + part * CHUNK
-                return [blocks[base + i, pl.ds(offset, 16), :] for i in range(CHUNK)]
-
-            def later(j, kept):
-                take = sublane >= (starts[j] - offset).astype(jnp.int16)
-                return [jnp.where(take, new, old) for new, old in zip(load(j), kept)]
-
-            kept = lax.fori_loop(begin + 1, end + 1, later, load(begin))
-            for i in range(CHUNK):
-                rows[part * CHUNK + i, pl.ds(pl.multiple_of(t * 16, 16), 16), :] = kept[i].astype(jnp.float32)
-            return carry
-
-        return lax.fori_loop(0, N_DP // CHUNK, chunk, carry)
-
-    lax.fori_loop(0, GROUP // 16, tile, jnp.int32(0))
+    def select(group, step):
+        def tile(t, carry):
+            whole = step * (STEP // 16) + t
+            offset = pl.multiple_of(whole * 16, 16)
+            at = pl.ds(pl.multiple_of(offset - group * GROUP, 16), 16)
+            begin, end = firsts[whole], firsts[whole + 1]
+
+            def chunk(part, carry):
+                def load(j):
+                    base = (part * CHUNK - shifts[j]) & (N_DP - 1)
+                    return [blocks[base + i, pl.ds(offset, 16), :] for i in range(CHUNK)]
+
+                def later(j, kept):
+                    take = sublane >= (starts[j] - offset).astype(jnp.int16)
+                    return [jnp.where(take, new, old) for new, old in zip(load(j), kept)]
+
+                kept = lax.fori_loop(begin + 1, end + 1, later, load(begin))
+                for i in range(CHUNK):
+                    rows[part * CHUNK + i, at, :] = kept[i].astype(jnp.float32)
+                return carry
+
+            return lax.fori_loop(0, N_DP // CHUNK, chunk, carry)
+
+        lax.fori_loop(0, STEP // 16, tile, jnp.int32(0))
 
     def spread(low, carry):
         for i, distance in enumerate(places):
             p = ((my_z + distance) & (N_Z - 1)) * P_LOW + low
             at = pl.ds(pl.multiple_of((i * P_LOW + low) * GROUP_ROWS, GROUP_ROWS), GROUP_ROWS)
             for head in range(HEADS):
-                weights[at, head * HS : (head + 1) * HS] = rows[p, pl.ds(head, GROUP_ROWS, stride=HEADS), :].astype(
-                    jnp.bfloat16
-                )
+                weights[at, head * HS : (head + 1) * HS] = rows[
+                    p, pl.ds(head, GROUP_ROWS, stride=HEADS), :
+                ].astype(jnp.bfloat16)
         return carry
 
-    lax.fori_loop(0, P_LOW, spread, jnp.int32(0))
-    for head in range(HEADS):
-        master[:, head * HS : (head + 1) * HS] = rows[me, pl.ds(head, GROUP_ROWS, stride=HEADS), :]
-
-    last = jnp.concatenate([tokens[-2][...], tokens[-1][...]], axis=0)
-    columns = jnp.concatenate([block[...] for block in tokens[:-2]] + [last], axis=1)
-    part = jnp.dot(columns, weights[...], preferred_element_type=jnp.float32)
-
-    @pl.when(group == 0)
-    def _():
-        total[...] = part
-
-    @pl.when(group > 0)
-    def _():
-        total[...] += part
-
-    @pl.when(group == pl.num_programs(0) - 1)
-    def _():
-        query[...] = total[:, : query.shape[1]].astype(query.dtype)
-        key[...] = total[:, query.shape[1] :].astype(key.dtype)
+    def one_group(group, carry):
+        def one_step(step, carry):
+            for copy in copies(group * per_group + step):
+                copy.wait()
+            select(group, group * per_group + step)
+            return carry
+
+        lax.fori_loop(0, per_group, one_step, jnp.int32(0))
+        lax.fori_loop(0, P_LOW, spread, jnp.int32(0))
+        for head in range(HEADS):
+            master[pl.ds(pl.multiple_of(group * GROUP_ROWS, GROUP_ROWS), GROUP_ROWS), head * HS : (head + 1) * HS] = rows[
+                me, pl.ds(head, GROUP_ROWS, stride=HEADS), :
+            ]
+        for copy in token_copies(group):
+            copy.wait()
+        part = jnp.dot(columns[group], weights[...], preferred_element_type=jnp.float32)
+
+        @pl.when(group == 0)
+        def _():
+            total[...] = part
+
+        @pl.when(group > 0)
+        def _():
+            total[...] += part
+
+        return carry
+
+    lax.fori_loop(0, GROUPS, one_group, jnp.int32(0))
+    cols = query.shape[1]
+    query[...] = total[:, :cols].astype(query.dtype)
+    key[...] = total[:, cols:].astype(key.dtype)
 
 
 SMEM = pl.BlockSpec(memory_space=pltpu.SMEM)
@@ -223,28 +254,23 @@
     group_cols = P_LOW * GROUP_ROWS
     new_master, query, key = pl.pallas_call(
         functools.partial(product_kernel, distances),
-        grid=(GROUPS,),
         out_shape=[
             state,
             jax.ShapeDtypeStruct((tokens_dev, query_cols), jnp.bfloat16),
             jax.ShapeDtypeStruct((tokens_dev, key_cols), jnp.bfloat16),
         ],
-        in_specs=[SMEM] * 3
-        + [pl.BlockSpec(memory_space=pl.ANY)]
-        + [pl.BlockSpec((block.shape[0], group_cols), lambda g: (0, g)) for block in blocks],
-        out_specs=[
-            pl.BlockSpec((GROUP_ROWS, block_cols), lambda g: (g, 0)),
-            pl.BlockSpec((tokens_dev, query_cols), lambda g: (0, 0)),
-            pl.BlockSpec((tokens_dev, key_cols), lambda g: (0, 0)),
-        ],
+        in_specs=[SMEM] * 3 + [pl.BlockSpec(memory_space=pl.ANY)] * (1 + len(blocks)),
+        out_specs=[VMEM] * 3,
         scratch_shapes=[
-            pltpu.VMEM((2 * NY, NX, NC, SLOTS, HS), jnp.bfloat16),
+            pltpu.VMEM((NY + CHUNK // (NX * NC), NX, NC, SLOTS, HS), jnp.bfloat16),
+            pltpu.VMEM((GROUPS, tokens_dev, N_Z * group_cols), jnp.bfloat16),
             pltpu.VMEM((N_DP, GROUP, HS), jnp.float32),
             pltpu.VMEM((N_Z * group_cols, block_cols), jnp.bfloat16),
             pltpu.VMEM((tokens_dev, block_cols), jnp.float32),
             pltpu.SMEM((N_DP,), jnp.int32),
             pltpu.SMEM((SLOTS // 16 + 8,), jnp.int32),
-            pltpu.SemaphoreType.DMA((GROUPS, 2 * NX * NC)),
+            pltpu.SemaphoreType.DMA((SLOTS // STEP, 2 * NC)),
+            pltpu.SemaphoreType.DMA((GROUPS, len(blocks))),
         ],
         compiler_params=pltpu.CompilerParams(vmem_limit_bytes=VMEM_LIMIT),
         cost_estimate=pl.CostEstimate(

time: 144 us -> 141 us (0.979)
  Pallas kernels: 27.9 us -> 25 us
    pallas_call x1, Pallas kernels: 23 us -> 20.1 us  [per_device(): pl.pallas_call(functools.partial(product_kernel, distances), out_shape=[s...]
  transfers between devices with their start and end apart: 10 -> 10, of which waited for: 5 -> 5; matrix products, arithmetic and copies ran while one was open for 1% -> 1% of each run, Pallas kernels for 3% -> 4%
where the time goes in v8:
time: 141 us; the launch traced here: 139 us
  starting transfers between devices  45.9 us (33%)
  waiting for transfers between devices  36.8 us (26%)
  Pallas kernels  25 us (18%)
  between operations  14.2 us (10%)
  blocking collectives  12.9 us (9%)
  other arithmetic  1.74 us (1%)
    ppermute x3, starting transfers between devices, gather_tokens(): from_above = lax.ppermute(from_above, 'tensor', down)  20.5 us
    pallas_call x1, Pallas kernels, per_device(): pl.pallas_call(functools.partial(product_kernel, distances), out_shape=[s...  20.1 us
    all_to_all x1, waiting for transfers between devices, per_device(): lax.all_to_all(packed, 'dp', split_axis=0, concat_axis=0, tiled=True)  16.3 us
    ppermute x3, waiting for transfers between devices, gather_tokens(): from_below = lax.ppermute(from_below, 'tensor', up)  14.6 us
    all_to_all x1, starting transfers between devices, per_device(): lax.all_to_all(packed, 'dp', split_axis=0, concat_axis=0, tiled=True)  13.1 us
    all_gather x1, blocking collectives, per_device(): lax.all_gather(column, 'dp', axis_index_groups=X_GROUPS, axis=0, tiled=True)  12.9 us
    ppermute x3, starting transfers between devices, gather_tokens(): from_below = lax.ppermute(from_below, 'tensor', up)  5.75 us
    ppermute x1, waiting for transfers between devices, gather_tokens(): arrays.append(lax.ppermute(from_below[:half], 'tensor', up))  4.82 us
  transfers between devices with their start and end apart: 10, of which 5 were waited for; matrix products, arithmetic and copies ran while one was open for 1% of the time, Pallas kernels for 4%

profile of v8, /device:TPU:1, one launch (start us, length us, event | category | flops | bytes accessed | tf_op | source)
XLA Modules:
  0.0 138.5 jit_solution(16778737541729006619)
XLA Ops:
  7.2 0.0 all-gather.2.cloned.1.call-start
  7.2 1.1 convert_element_type.9
  8.3 0.2 reshape.63
  8.5 12.9 %all_gather.6 = bf16[2688,128]{1,0:T(8,128)(2,1)} all-gather(bf16[672,128]{1,0:T(8,128)(2,1)S(1)} %reshape.63), channel_id=1, replica_groups={{0,16,32,48},{8,24,40,56},{64,80,96,112},{72,88,104,120},{128,144,160,1..., dimensions={0}, use_global_device_ids=true | all-gather | bytes 860160 | tf_op jit(solution)/shard_map/all_gather | solution.py:222
  21.4 1.0 fusion.2.refs_0_
  22.4 11.0 %collective-permute-start.1 = (bf16[512,768]{1,0:T(8,128)(2,1)S(1)}, bf16[512,768]{1,0:T(8,128)(2,1)S(1)}, u32[]{:S(2)}, u32[]{:S(2)}) collective-permute-start(bf16[512,768]{1,0:T(8,128)(2,1)S(1)} %fusion.2.refs_0_), channel_id=1, source_target_pairs={{0,7},{1,0},{2,1},{3,2},{4,3},{5,4},{6,5},{7,6},{8,15},{9,8},{10,9... | collective-permute-start | bytes 2359304 | tf_op jit(solution)/shard_map/ppermute | solution.py:204
  33.4 1.9 %collective-permute-start = (bf16[512,768]{1,0:T(8,128)(2,1)S(1)}, bf16[512,768]{1,0:T(8,128)(2,1)}, u32[]{:S(2)}, u32[]{:S(2)}) collective-permute-start(bf16[512,768]{1,0:T(8,128)(2,1)S(1)} %fusion.2.refs_0_), channel_id=1, source_target_pairs={{0,1},{1,2},{2,3},{3,4},{4,5},{5,6},{6,7},{7,0},{8,9},{9,10},{10,1... | collective-permute-start | bytes 2359304 | tf_op jit(solution)/shard_map/ppermute | solution.py:203
  35.3 0.7 pad_add_fusion.own
  36.0 2.4 %pack.1 = bf16[64,16,256]{2,1,0:T(8,128)(2,1)} custom-call(s32[64]{0:T(128)} %lengths.5, s32[64]{0:T(128)} %shifts.5, s32[2]{0:T(128)} %pad_add_fusion.own, f32[96,896]{1,0:T(8,128)} %first.1, f32[96,896]{1,0:T(8,128)} %second.1), custom_call_target="tpu_custom_call" | custom-call | tf_op jit(solution)/shard_map/pack/pallas_call | solution.py:232
  38.3 13.1 %all-to-all-start = ((bf16[64,16,256]{2,1,0:T(8,128)(2,1)}), bf16[64,16,256]{2,1,0:T(8,128)(2,1)S(1)}, u32[]{:S(2)}, u32[]{:S(2)}) async-start(bf16[64,16,256]{2,1,0:T(8,128)(2,1)} %pack.1), calls=%async_computation | async-start | bytes 1048576 | tf_op jit(solution)/shard_map/all_to_all | solution.py:240
  51.4 4.9 %collective-permute-start.3 = (bf16[512,768]{1,0:T(8,128)(2,1)S(1)}, bf16[512,768]{1,0:T(8,128)(2,1)}, u32[]{:S(2)}, u32[]{:S(2)}) collective-permute-start(bf16[512,768]{1,0:T(8,128)(2,1)S(1)} %collective-permute-done.1.refs_2_), channel_id=1, source_target_pairs={{0,7},{1,0},{2,1},{3,2},{4,3},{5,4},{6,5},{7,6},{8,15},{9,8},{10,9... | collective-permute-start | bytes 2359304 | tf_op jit(solution)/shard_map/ppermute | solution.py:204
  56.3 1.9 %collective-permute-start.2 = (bf16[512,768]{1,0:T(8,128)(2,1)}, bf16[512,768]{1,0:T(8,128)(2,1)}, u32[]{:S(2)}, u32[]{:S(2)}) collective-permute-start(bf16[512,768]{1,0:T(8,128)(2,1)} %collective-permute-done.refs_1_), channel_id=1, source_target_pairs={{0,1},{1,2},{2,3},{3,4},{4,5},{5,6},{6,7},{7,0},{8,9},{9,10},{10,1... | collective-permute-start | bytes 2359304 | tf_op jit(solution)/shard_map/ppermute | solution.py:203
  58.2 16.3 %all-to-all-done.received = bf16[64,16,256]{2,1,0:T(8,128)(2,1)S(1)} async-done(((bf16[64,16,256]{2,1,0:T(8,128)(2,1)}), bf16[64,16,256]{2,1,0:T(8,128)(2,1)S(1)}, u32[]{:S(2)}, u32[]{:S(2)}) %all-to-all-start) | async-done | bytes 524320 | tf_op jit(solution)/shard_map/all_to_all | solution.py:240
  74.6 0.8 copy-done.1
  75.4 2.5 %unpack.1 = (f32[96,896]{1,0:T(8,128)}, f32[96,896]{1,0:T(8,128)}) custom-call(s32[64]{0:T(128)} %lengths.5, s32[64]{0:T(128)} %shifts.5, s32[2]{0:T(128)} %pad_add_fusion.own, bf16[64,16,256]{2,1,0:T(8,128)(2,1)} %copy-done.1), custom_call_target="tpu_custom_call" | custom-call | tf_op jit(solution)/shard_map/unpack/pallas_call | solution.py:241
  77.9 0.2 collective-permute-done.2.refs_3_
  78.1 1.9 %collective-permute-start.4 = (bf16[512,768]{1,0:T(8,128)(2,1)}, bf16[512,768]{1,0:T(8,128)(2,1)S(1)}, u32[]{:S(2)}, u32[]{:S(2)}) collective-permute-start(bf16[512,768]{1,0:T(8,128)(2,1)} %collective-permute-done.2.refs_3_), channel_id=1, source_target_pairs={{0,1},{1,2},{2,3},{3,4},{4,5},{5,6},{6,7},{7,0},{8,9},{9,10},{10,1... | collective-permute-start | bytes 2359304 | tf_op jit(solution)/shard_map/ppermute | solution.py:203
  80.0 4.7 %collective-permute-start.5 = (bf16[512,768]{1,0:T(8,128)(2,1)}, bf16[512,768]{1,0:T(8,128)(2,1)S(1)}, u32[]{:S(2)}, u32[]{:S(2)}) collective-permute-start(bf16[512,768]{1,0:T(8,128)(2,1)} %collective-permute-done.3.refs_4_), channel_id=1, source_target_pairs={{0,7},{1,0},{2,1},{3,2},{4,3},{5,4},{6,5},{7,6},{8,15},{9,8},{10,9... | collective-permute-start | bytes 2359304 | tf_op jit(solution)/shard_map/ppermute | solution.py:204
  84.7 14.4 %collective-permute-done.4.refs_5_ = bf16[512,768]{1,0:T(8,128)(2,1)S(1)} collective-permute-done((bf16[512,768]{1,0:T(8,128)(2,1)}, bf16[512,768]{1,0:T(8,128)(2,1)S(1)}, u32[]{:S(2)}, u32[]{:S(2)}) %collective-permute-start.4) | collective-permute-done | bytes 786464 | tf_op jit(solution)/shard_map/ppermute | solution.py:203
  99.2 1.9 %collective-permute-start.6 = (bf16[256,768]{1,0:T(8,128)(2,1)S(1)}, bf16[256,768]{1,0:T(8,128)(2,1)S(1)}, u32[]{:S(2)}, u32[]{:S(2)}) collective-permute-start(bf16[256,768]{1,0:T(8,128)(2,1)S(1)} %slice.8), channel_id=1, source_target_pairs={{0,1},{1,2},{2,3},{3,4},{4,5},{5,6},{6,7},{7,0},{8,9},{9,10},{10,1... | collective-permute-start | bytes 1179656 | tf_op jit(solution)/shard_map/ppermute | solution.py:210
  101.1 4.6 %collective-permute-start.7 = (bf16[256,768]{1,0:T(8,128)(2,1)S(1)}, bf16[256,768]{1,0:T(8,128)(2,1)}, u32[]{:S(2)}, u32[]{:S(2)}) collective-permute-start(bf16[256,768]{1,0:T(8,128)(2,1)S(1)} %slice.9), channel_id=1, source_target_pairs={{0,7},{1,0},{2,1},{3,2},{4,3},{5,4},{6,5},{7,6},{8,15},{9,8},{10,9... | collective-permute-start | bytes 1179656 | tf_op jit(solution)/shard_map/ppermute | solution.py:211
  105.7 4.8 %collective-permute-done.6.refs_7_ = bf16[256,768]{1,0:T(8,128)(2,1)S(1)} collective-permute-done((bf16[256,768]{1,0:T(8,128)(2,1)S(1)}, bf16[256,768]{1,0:T(8,128)(2,1)S(1)}, u32[]{:S(2)}, u32[]{:S(2)}) %collective-permute-start.6) | collective-permute-done | bytes 393248 | tf_op jit(solution)/shard_map/ppermute | solution.py:210
  110.5 1.0 collective-permute-done.7.refs_8_
  111.5 20.1 %product.1 = (f32[96,896]{1,0:T(8,128)}, bf16[512,768]{1,0:T(8,128)(2,1)}, bf16[512,128]{1,0:T(8,128)(2,1)}) custom-call(s32[64]{0:T(128)} %lengths.5, s32[64]{0:T(128)} %shifts.5, s32[2]{0:T(128)} %pad_add_fusion.own, bf16[8,2,4,672,128]{4,3,2,1,0:T(8,128)(2,1)} %bitcast.6, bf16[512,768]{1,0:T(8,128)(2,1)} %copy-done.4, ...), custom_call_target="tpu_custom_call" | custom-call | flops 5637144576 | bytes 17301504 | tf_op jit(solution)/shard_map/product/pallas_call | solution.py:255
  (22 shorter events, 0.1 us)
Async XLA Ops:
  7.2 14.2 %copy-start = (bf16[512,768]{1,0:T(8,128)(2,1)S(1)}, bf16[512,768]{1,0:T(8,128)(2,1)}, u32[]{:S(2)}) copy-start(bf16[512,768]{1,0:T(8,128)(2,1)} %param.6) | copy-start | bytes 2359300
  7.2 104.3 %all-gather.2.cloned.1.call-start = ((), (), s32[]{:S(2)}) async-start(), calls=%async_computation.1 | async-start | bytes 11698176 | tf_op jit(solution)/shard_map/all_gather | solution.py:223
  22.4 89.1 %copy-start.4 = (bf16[512,768]{1,0:T(8,128)(2,1)}, bf16[512,768]{1,0:T(8,128)(2,1)S(1)}, u32[]{:S(2)}) copy-start(bf16[512,768]{1,0:T(8,128)(2,1)S(1)} %fusion.2.refs_0_) | copy-start | bytes 2359300
  22.4 29.0 %collective-permute-start.1 = (bf16[512,768]{1,0:T(8,128)(2,1)S(1)}, bf16[512,768]{1,0:T(8,128)(2,1)S(1)}, u32[]{:S(2)}, u32[]{:S(2)}) collective-permute-start(bf16[512,768]{1,0:T(8,128)(2,1)S(1)} %fusion.2.refs_0_), channel_id=1, source_target_pairs={{0,7},{1,0},{2,1},{3,2},{4,3},{5,4},{6,5},{7,6},{8,15},{9,8},{10,9... | collective-permute-start | bytes 2359304 | tf_op jit(solution)/shard_map/ppermute | solution.py:204
  33.4 22.9 %collective-permute-start = (bf16[512,768]{1,0:T(8,128)(2,1)S(1)}, bf16[512,768]{1,0:T(8,128)(2,1)}, u32[]{:S(2)}, u32[]{:S(2)}) collective-permute-start(bf16[512,768]{1,0:T(8,128)(2,1)S(1)} %fusion.2.refs_0_), channel_id=1, source_target_pairs={{0,1},{1,2},{2,3},{3,4},{4,5},{5,6},{6,7},{7,0},{8,9},{9,10},{10,1... | collective-permute-start | bytes 2359304 | tf_op jit(solution)/shard_map/ppermute | solution.py:203
  38.3 36.2 %all-to-all-start = ((bf16[64,16,256]{2,1,0:T(8,128)(2,1)}), bf16[64,16,256]{2,1,0:T(8,128)(2,1)S(1)}, u32[]{:S(2)}, u32[]{:S(2)}) async-start(bf16[64,16,256]{2,1,0:T(8,128)(2,1)} %pack.1), calls=%async_computation | async-start | bytes 1048576 | tf_op jit(solution)/shard_map/all_to_all | solution.py:240
  51.4 26.6 %copy-start.5 = (bf16[512,768]{1,0:T(8,128)(2,1)}, bf16[512,768]{1,0:T(8,128)(2,1)S(1)}, u32[]{:S(2)}) copy-start(bf16[512,768]{1,0:T(8,128)(2,1)S(1)} %collective-permute-done.1.refs_2_) | copy-start | bytes 2359300
  51.4 26.4 %collective-permute-start.3 = (bf16[512,768]{1,0:T(8,128)(2,1)S(1)}, bf16[512,768]{1,0:T(8,128)(2,1)}, u32[]{:S(2)}, u32[]{:S(2)}) collective-permute-start(bf16[512,768]{1,0:T(8,128)(2,1)S(1)} %collective-permute-done.1.refs_2_), channel_id=1, source_target_pairs={{0,7},{1,0},{2,1},{3,2},{4,3},{5,4},{6,5},{7,6},{8,15},{9,8},{10,9... | collective-permute-start | bytes 2359304 | tf_op jit(solution)/shard_map/ppermute | solution.py:204
  56.3 21.8 %collective-permute-start.2 = (bf16[512,768]{1,0:T(8,128)(2,1)}, bf16[512,768]{1,0:T(8,128)(2,1)}, u32[]{:S(2)}, u32[]{:S(2)}) collective-permute-start(bf16[512,768]{1,0:T(8,128)(2,1)} %collective-permute-done.refs_1_), channel_id=1, source_target_pairs={{0,1},{1,2},{2,3},{3,4},{4,5},{5,6},{6,7},{7,0},{8,9},{9,10},{10,1... | collective-permute-start | bytes 2359304 | tf_op jit(solution)/shard_map/ppermute | solution.py:203
  74.6 0.8 copy-start.1
  78.1 21.0 %collective-permute-start.4 = (bf16[512,768]{1,0:T(8,128)(2,1)}, bf16[512,768]{1,0:T(8,128)(2,1)S(1)}, u32[]{:S(2)}, u32[]{:S(2)}) collective-permute-start(bf16[512,768]{1,0:T(8,128)(2,1)} %collective-permute-done.2.refs_3_), channel_id=1, source_target_pairs={{0,1},{1,2},{2,3},{3,4},{4,5},{5,6},{6,7},{7,0},{8,9},{9,10},{10,1... | collective-permute-start | bytes 2359304 | tf_op jit(solution)/shard_map/ppermute | solution.py:203
  80.0 21.1 %collective-permute-start.5 = (bf16[512,768]{1,0:T(8,128)(2,1)}, bf16[512,768]{1,0:T(8,128)(2,1)S(1)}, u32[]{:S(2)}, u32[]{:S(2)}) collective-permute-start(bf16[512,768]{1,0:T(8,128)(2,1)} %collective-permute-done.3.refs_4_), channel_id=1, source_target_pairs={{0,7},{1,0},{2,1},{3,2},{4,3},{5,4},{6,5},{7,6},{8,15},{9,8},{10,9... | collective-permute-start | bytes 2359304 | tf_op jit(solution)/shard_map/ppermute | solution.py:204
  99.1 12.4 %copy-start.2 = (bf16[512,768]{1,0:T(8,128)(2,1)}, bf16[512,768]{1,0:T(8,128)(2,1)S(1)}, u32[]{:S(2)}) copy-start(bf16[512,768]{1,0:T(8,128)(2,1)S(1)} %collective-permute-done.4.refs_5_) | copy-start | bytes 2359300
  99.2 11.4 %collective-permute-start.6 = (bf16[256,768]{1,0:T(8,128)(2,1)S(1)}, bf16[256,768]{1,0:T(8,128)(2,1)S(1)}, u32[]{:S(2)}, u32[]{:S(2)}) collective-permute-start(bf16[256,768]{1,0:T(8,128)(2,1)S(1)} %slice.8), channel_id=1, source_target_pairs={{0,1},{1,2},{2,3},{3,4},{4,5},{5,6},{6,7},{7,0},{8,9},{9,10},{10,1... | collective-permute-start | bytes 1179656 | tf_op jit(solution)/shard_map/ppermute | solution.py:210
  101.1 10.4 %copy-start.3 = (bf16[512,768]{1,0:T(8,128)(2,1)}, bf16[512,768]{1,0:T(8,128)(2,1)S(1)}, u32[]{:S(2)}) copy-start(bf16[512,768]{1,0:T(8,128)(2,1)S(1)} %collective-permute-done.5.refs_6_) | copy-start | bytes 2359300
  101.1 10.4 %collective-permute-start.7 = (bf16[256,768]{1,0:T(8,128)(2,1)S(1)}, bf16[256,768]{1,0:T(8,128)(2,1)}, u32[]{:S(2)}, u32[]{:S(2)}) collective-permute-start(bf16[256,768]{1,0:T(8,128)(2,1)S(1)} %slice.9), channel_id=1, source_target_pairs={{0,7},{1,0},{2,1},{3,2},{4,3},{5,4},{6,5},{7,6},{8,15},{9,8},{10,9... | collective-permute-start | bytes 1179656 | tf_op jit(solution)/shard_map/ppermute | solution.py:211
  110.5 1.0 copy-start.6
Sparse Core Ops, SparseCore 0:
  21.5 89.1 all-gather.1

commit v9 on v8

--- a/solution.py
+++ b/solution.py
@@ -203,7 +203,7 @@
         from_below = lax.ppermute(from_below, "tensor", up)
         from_above = lax.ppermute(from_above, "tensor", down)
         distances += [-distance, distance]
-        if distance == 2:
+        if distance == 3:
             from_below, from_above, moments = lax.optimization_barrier((from_below, from_above, moments))
         arrays += [from_below, from_above]
     distances.append(N_Z // 2)

time: 141 us -> 143 us (1.014)
  waiting for transfers between devices: 36.8 us -> 39.3 us
    ppermute x3, waiting for transfers between devices: 14.6 us -> 0.01 us  [gather_tokens(): from_below = lax.ppermute(from_below, 'tensor', up)]
    ppermute x3, waiting for transfers between devices: 0.01 us -> 12.3 us  [gather_tokens(): from_above = lax.ppermute(from_above, 'tensor', down)]
    ppermute x1, waiting for transfers between devices: 0.96 us -> 5.61 us  [gather_tokens(): arrays.append(lax.ppermute(from_above[half:], 'tensor', down))]
  transfers between devices with their start and end apart: 10 -> 10, of which waited for: 5 -> 4; matrix products, arithmetic and copies ran while one was open for 1% -> 1% of each run, Pallas kernels for 4% -> 3%
where the time goes in v9:
time: 143 us; the launch traced here: 142 us
  starting transfers between devices  45.9 us (32%)
  waiting for transfers between devices  39.3 us (27%)
  Pallas kernels  25 us (17%)
  between operations  14.3 us (10%)
  blocking collectives  12.9 us (9%)
  local copies, waits for them, and re-layouts  1.78 us (1%)
  other arithmetic  1.74 us (1%)
    ppermute x3, starting transfers between devices, gather_tokens(): from_above = lax.ppermute(from_above, 'tensor', down)  21.2 us
    pallas_call x1, Pallas kernels, per_device(): pl.pallas_call(functools.partial(product_kernel, distances), out_shape=[s...  20.1 us
    all_to_all x1, waiting for transfers between devices, per_device(): lax.all_to_all(packed, 'dp', split_axis=0, concat_axis=0, tiled=True)  16.3 us
    all_gather x1, blocking collectives, per_device(): lax.all_gather(column, 'dp', axis_index_groups=X_GROUPS, axis=0, tiled=True)  12.9 us
    ppermute x3, waiting for transfers between devices, gather_tokens(): from_above = lax.ppermute(from_above, 'tensor', down)  12.3 us
    all_to_all x1, starting transfers between devices, per_device(): lax.all_to_all(packed, 'dp', split_axis=0, concat_axis=0, tiled=True)  12.2 us
    ppermute x3, starting transfers between devices, gather_tokens(): from_below = lax.ppermute(from_below, 'tensor', up)  5.76 us
    ppermute x1, waiting for transfers between devices, gather_tokens(): arrays.append(lax.ppermute(from_above[half:], 'tensor', down))  5.61 us
  transfers between devices with their start and end apart: 10, of which 4 were waited for; matrix products, arithmetic and copies ran while one was open for 1% of the time, Pallas kernels for 3%

profile of v9, /device:TPU:1, one launch (start us, length us, event | category | flops | bytes accessed | tf_op | source)
XLA Modules:
  0.0 141.9 jit_solution(6317710480663359653)
XLA Ops:
  7.2 0.0 all-gather.2.cloned.1.call-start
  7.2 1.1 convert_element_type.9
  8.3 0.2 reshape.63
  8.5 12.9 %all_gather.6 = bf16[2688,128]{1,0:T(8,128)(2,1)} all-gather(bf16[672,128]{1,0:T(8,128)(2,1)S(1)} %reshape.63), channel_id=1, replica_groups={{0,16,32,48},{8,24,40,56},{64,80,96,112},{72,88,104,120},{128,144,160,1..., dimensions={0}, use_global_device_ids=true | all-gather | bytes 860160 | tf_op jit(solution)/shard_map/all_gather | solution.py:222
  21.4 1.0 fusion.2.refs_0_
  22.4 11.0 %collective-permute-start.1 = (bf16[512,768]{1,0:T(8,128)(2,1)S(1)}, bf16[512,768]{1,0:T(8,128)(2,1)S(1)}, u32[]{:S(2)}, u32[]{:S(2)}) collective-permute-start(bf16[512,768]{1,0:T(8,128)(2,1)S(1)} %fusion.2.refs_0_), channel_id=1, source_target_pairs={{0,7},{1,0},{2,1},{3,2},{4,3},{5,4},{6,5},{7,6},{8,15},{9,8},{10,9... | collective-permute-start | bytes 2359304 | tf_op jit(solution)/shard_map/ppermute | solution.py:204
  33.4 1.9 %collective-permute-start = (bf16[512,768]{1,0:T(8,128)(2,1)S(1)}, bf16[512,768]{1,0:T(8,128)(2,1)S(1)}, u32[]{:S(2)}, u32[]{:S(2)}) collective-permute-start(bf16[512,768]{1,0:T(8,128)(2,1)S(1)} %fusion.2.refs_0_), channel_id=1, source_target_pairs={{0,1},{1,2},{2,3},{3,4},{4,5},{5,6},{6,7},{7,0},{8,9},{9,10},{10,1... | collective-permute-start | bytes 2359304 | tf_op jit(solution)/shard_map/ppermute | solution.py:203
  35.3 12.3 %collective-permute-done.1.refs_2_ = bf16[512,768]{1,0:T(8,128)(2,1)S(1)} collective-permute-done((bf16[512,768]{1,0:T(8,128)(2,1)S(1)}, bf16[512,768]{1,0:T(8,128)(2,1)S(1)}, u32[]{:S(2)}, u32[]{:S(2)}) %collective-permute-start.1) | collective-permute-done | bytes 786464 | tf_op jit(solution)/shard_map/ppermute | solution.py:204
  47.7 5.4 %collective-permute-start.3 = (bf16[512,768]{1,0:T(8,128)(2,1)S(1)}, bf16[512,768]{1,0:T(8,128)(2,1)}, u32[]{:S(2)}, u32[]{:S(2)}) collective-permute-start(bf16[512,768]{1,0:T(8,128)(2,1)S(1)} %collective-permute-done.1.refs_2_), channel_id=1, source_target_pairs={{0,7},{1,0},{2,1},{3,2},{4,3},{5,4},{6,5},{7,6},{8,15},{9,8},{10,9... | collective-permute-start | bytes 2359304 | tf_op jit(solution)/shard_map/ppermute | solution.py:204
  53.1 1.9 %collective-permute-start.2 = (bf16[512,768]{1,0:T(8,128)(2,1)S(1)}, bf16[512,768]{1,0:T(8,128)(2,1)}, u32[]{:S(2)}, u32[]{:S(2)}) collective-permute-start(bf16[512,768]{1,0:T(8,128)(2,1)S(1)} %collective-permute-done.refs_1_), channel_id=1, source_target_pairs={{0,1},{1,2},{2,3},{3,4},{4,5},{5,6},{6,7},{7,0},{8,9},{9,10},{10,1... | collective-permute-start | bytes 2359304 | tf_op jit(solution)/shard_map/ppermute | solution.py:203
  55.0 0.6 pad_add_fusion.own
  55.7 2.4 %pack.1 = bf16[64,16,256]{2,1,0:T(8,128)(2,1)} custom-call(s32[64]{0:T(128)} %lengths.5, s32[64]{0:T(128)} %shifts.5, s32[2]{0:T(128)} %pad_add_fusion.own, f32[96,896]{1,0:T(8,128)} %first.1, f32[96,896]{1,0:T(8,128)} %second.1), custom_call_target="tpu_custom_call" | custom-call | tf_op jit(solution)/shard_map/pack/pallas_call | solution.py:232
  58.1 12.2 %all-to-all-start = ((bf16[64,16,256]{2,1,0:T(8,128)(2,1)}), bf16[64,16,256]{2,1,0:T(8,128)(2,1)S(1)}, u32[]{:S(2)}, u32[]{:S(2)}) async-start(bf16[64,16,256]{2,1,0:T(8,128)(2,1)} %pack.1), calls=%async_computation | async-start | bytes 1048576 | tf_op jit(solution)/shard_map/all_to_all | solution.py:240
  70.3 4.8 %collective-permute-start.5 = (bf16[512,768]{1,0:T(8,128)(2,1)}, bf16[512,768]{1,0:T(8,128)(2,1)S(1)}, u32[]{:S(2)}, u32[]{:S(2)}) collective-permute-start(bf16[512,768]{1,0:T(8,128)(2,1)} %collective-permute-done.3.refs_4_), channel_id=1, source_target_pairs={{0,7},{1,0},{2,1},{3,2},{4,3},{5,4},{6,5},{7,6},{8,15},{9,8},{10,9... | collective-permute-start | bytes 2359304 | tf_op jit(solution)/shard_map/ppermute | solution.py:204
  75.1 1.9 %collective-permute-start.4 = (bf16[512,768]{1,0:T(8,128)(2,1)}, bf16[512,768]{1,0:T(8,128)(2,1)S(1)}, u32[]{:S(2)}, u32[]{:S(2)}) collective-permute-start(bf16[512,768]{1,0:T(8,128)(2,1)} %collective-permute-done.2.refs_3_), channel_id=1, source_target_pairs={{0,1},{1,2},{2,3},{3,4},{4,5},{5,6},{6,7},{7,0},{8,9},{9,10},{10,1... | collective-permute-start | bytes 2359304 | tf_op jit(solution)/shard_map/ppermute | solution.py:203
  77.1 16.3 %all-to-all-done.received = bf16[64,16,256]{2,1,0:T(8,128)(2,1)S(1)} async-done(((bf16[64,16,256]{2,1,0:T(8,128)(2,1)}), bf16[64,16,256]{2,1,0:T(8,128)(2,1)S(1)}, u32[]{:S(2)}, u32[]{:S(2)}) %all-to-all-start) | async-done | bytes 524320 | tf_op jit(solution)/shard_map/all_to_all | solution.py:240
  93.4 0.8 copy-done.1
  94.2 2.6 %unpack.1 = (f32[96,896]{1,0:T(8,128)}, f32[96,896]{1,0:T(8,128)}) custom-call(s32[64]{0:T(128)} %lengths.5, s32[64]{0:T(128)} %shifts.5, s32[2]{0:T(128)} %pad_add_fusion.own, bf16[64,16,256]{2,1,0:T(8,128)(2,1)} %copy-done.1), custom_call_target="tpu_custom_call" | custom-call | tf_op jit(solution)/shard_map/unpack/pallas_call | solution.py:241
  96.9 4.8 %collective-permute-start.7 = (bf16[256,768]{1,0:T(8,128)(2,1)S(1)}, bf16[256,768]{1,0:T(8,128)(2,1)S(1)}, u32[]{:S(2)}, u32[]{:S(2)}) collective-permute-start(bf16[256,768]{1,0:T(8,128)(2,1)S(1)} %slice.7), channel_id=1, source_target_pairs={{0,7},{1,0},{2,1},{3,2},{4,3},{5,4},{6,5},{7,6},{8,15},{9,8},{10,9... | collective-permute-start | bytes 1179656 | tf_op jit(solution)/shard_map/ppermute | solution.py:211
  101.6 1.9 %collective-permute-start.6 = (bf16[256,768]{1,0:T(8,128)(2,1)S(1)}, bf16[256,768]{1,0:T(8,128)(2,1)S(1)}, u32[]{:S(2)}, u32[]{:S(2)}) collective-permute-start(bf16[256,768]{1,0:T(8,128)(2,1)S(1)} %slice.6), channel_id=1, source_target_pairs={{0,1},{1,2},{2,3},{3,4},{4,5},{5,6},{6,7},{7,0},{8,9},{9,10},{10,1... | collective-permute-start | bytes 1179656 | tf_op jit(solution)/shard_map/ppermute | solution.py:210
  103.6 5.6 %collective-permute-done.7.refs_8_ = bf16[256,768]{1,0:T(8,128)(2,1)S(1)} collective-permute-done((bf16[256,768]{1,0:T(8,128)(2,1)S(1)}, bf16[256,768]{1,0:T(8,128)(2,1)S(1)}, u32[]{:S(2)}, u32[]{:S(2)}) %collective-permute-start.7) | collective-permute-done | bytes 393248 | tf_op jit(solution)/shard_map/ppermute | solution.py:211
  109.2 5.0 %collective-permute-done.6.refs_7_ = bf16[256,768]{1,0:T(8,128)(2,1)S(1)} collective-permute-done((bf16[256,768]{1,0:T(8,128)(2,1)S(1)}, bf16[256,768]{1,0:T(8,128)(2,1)S(1)}, u32[]{:S(2)}, u32[]{:S(2)}) %collective-permute-start.6) | collective-permute-done | bytes 393248 | tf_op jit(solution)/shard_map/ppermute | solution.py:210
  114.2 0.7 copy-done.8
  114.9 20.1 %product.1 = (f32[96,896]{1,0:T(8,128)}, bf16[512,768]{1,0:T(8,128)(2,1)}, bf16[512,128]{1,0:T(8,128)(2,1)}) custom-call(s32[64]{0:T(128)} %lengths.5, s32[64]{0:T(128)} %shifts.5, s32[2]{0:T(128)} %pad_add_fusion.own, bf16[8,2,4,672,128]{4,3,2,1,0:T(8,128)(2,1)} %bitcast.6, bf16[512,768]{1,0:T(8,128)(2,1)} %copy-done.4, bf16[512,768]{1,0:T(8,128)(2,1)} %copy-done.6, ...), custom_call_target="tpu_custom_call" | custom-call | flops 5637144576 | bytes 17301504 | tf_op jit(solution)/shard_map/product/pallas_call | solution.py:255
  (26 shorter events, 0.1 us)
Async XLA Ops:
  7.2 14.2 %copy-start = (bf16[512,768]{1,0:T(8,128)(2,1)S(1)}, bf16[512,768]{1,0:T(8,128)(2,1)}, u32[]{:S(2)}) copy-start(bf16[512,768]{1,0:T(8,128)(2,1)} %param.6) | copy-start | bytes 2359300
  7.2 107.0 %all-gather.2.cloned.1.call-start = ((), (), s32[]{:S(2)}) async-start(), calls=%async_computation.1 | async-start | bytes 11698176 | tf_op jit(solution)/shard_map/all_gather | solution.py:223
  22.4 11.0 %copy-start.4 = (bf16[512,768]{1,0:T(8,128)(2,1)}, bf16[512,768]{1,0:T(8,128)(2,1)S(1)}, u32[]{:S(2)}) copy-start(bf16[512,768]{1,0:T(8,128)(2,1)S(1)} %fusion.2.refs_0_) | copy-start | bytes 2359300
  22.4 25.3 %collective-permute-start.1 = (bf16[512,768]{1,0:T(8,128)(2,1)S(1)}, bf16[512,768]{1,0:T(8,128)(2,1)S(1)}, u32[]{:S(2)}, u32[]{:S(2)}) collective-permute-start(bf16[512,768]{1,0:T(8,128)(2,1)S(1)} %fusion.2.refs_0_), channel_id=1, source_target_pairs={{0,7},{1,0},{2,1},{3,2},{4,3},{5,4},{6,5},{7,6},{8,15},{9,8},{10,9... | collective-permute-start | bytes 2359304 | tf_op jit(solution)/shard_map/ppermute | solution.py:204
  33.4 19.7 %collective-permute-start = (bf16[512,768]{1,0:T(8,128)(2,1)S(1)}, bf16[512,768]{1,0:T(8,128)(2,1)S(1)}, u32[]{:S(2)}, u32[]{:S(2)}) collective-permute-start(bf16[512,768]{1,0:T(8,128)(2,1)S(1)} %fusion.2.refs_0_), channel_id=1, source_target_pairs={{0,1},{1,2},{2,3},{3,4},{4,5},{5,6},{6,7},{7,0},{8,9},{9,10},{10,1... | collective-permute-start | bytes 2359304 | tf_op jit(solution)/shard_map/ppermute | solution.py:203
  47.6 22.6 %copy-start.5 = (bf16[512,768]{1,0:T(8,128)(2,1)}, bf16[512,768]{1,0:T(8,128)(2,1)S(1)}, u32[]{:S(2)}) copy-start(bf16[512,768]{1,0:T(8,128)(2,1)S(1)} %collective-permute-done.1.refs_2_) | copy-start | bytes 2359300
  47.7 22.6 %collective-permute-start.3 = (bf16[512,768]{1,0:T(8,128)(2,1)S(1)}, bf16[512,768]{1,0:T(8,128)(2,1)}, u32[]{:S(2)}, u32[]{:S(2)}) collective-permute-start(bf16[512,768]{1,0:T(8,128)(2,1)S(1)} %collective-permute-done.1.refs_2_), channel_id=1, source_target_pairs={{0,7},{1,0},{2,1},{3,2},{4,3},{5,4},{6,5},{7,6},{8,15},{9,8},{10,9... | collective-permute-start | bytes 2359304 | tf_op jit(solution)/shard_map/ppermute | solution.py:204
  53.1 22.0 %copy-start.6 = (bf16[512,768]{1,0:T(8,128)(2,1)}, bf16[512,768]{1,0:T(8,128)(2,1)S(1)}, u32[]{:S(2)}) copy-start(bf16[512,768]{1,0:T(8,128)(2,1)S(1)} %collective-permute-done.refs_1_) | copy-start | bytes 2359300
  53.1 22.0 %collective-permute-start.2 = (bf16[512,768]{1,0:T(8,128)(2,1)S(1)}, bf16[512,768]{1,0:T(8,128)(2,1)}, u32[]{:S(2)}, u32[]{:S(2)}) collective-permute-start(bf16[512,768]{1,0:T(8,128)(2,1)S(1)} %collective-permute-done.refs_1_), channel_id=1, source_target_pairs={{0,1},{1,2},{2,3},{3,4},{4,5},{5,6},{6,7},{7,0},{8,9},{9,10},{10,1... | collective-permute-start | bytes 2359304 | tf_op jit(solution)/shard_map/ppermute | solution.py:203
  58.1 35.3 %all-to-all-start = ((bf16[64,16,256]{2,1,0:T(8,128)(2,1)}), bf16[64,16,256]{2,1,0:T(8,128)(2,1)S(1)}, u32[]{:S(2)}, u32[]{:S(2)}) async-start(bf16[64,16,256]{2,1,0:T(8,128)(2,1)} %pack.1), calls=%async_computation | async-start | bytes 1048576 | tf_op jit(solution)/shard_map/all_to_all | solution.py:240
  70.3 26.5 %collective-permute-start.5 = (bf16[512,768]{1,0:T(8,128)(2,1)}, bf16[512,768]{1,0:T(8,128)(2,1)S(1)}, u32[]{:S(2)}, u32[]{:S(2)}) collective-permute-start(bf16[512,768]{1,0:T(8,128)(2,1)} %collective-permute-done.3.refs_4_), channel_id=1, source_target_pairs={{0,7},{1,0},{2,1},{3,2},{4,3},{5,4},{6,5},{7,6},{8,15},{9,8},{10,9... | collective-permute-start | bytes 2359304 | tf_op jit(solution)/shard_map/ppermute | solution.py:204
  75.1 21.6 %collective-permute-start.4 = (bf16[512,768]{1,0:T(8,128)(2,1)}, bf16[512,768]{1,0:T(8,128)(2,1)S(1)}, u32[]{:S(2)}, u32[]{:S(2)}) collective-permute-start(bf16[512,768]{1,0:T(8,128)(2,1)} %collective-permute-done.2.refs_3_), channel_id=1, source_target_pairs={{0,1},{1,2},{2,3},{3,4},{4,5},{5,6},{6,7},{7,0},{8,9},{9,10},{10,1... | collective-permute-start | bytes 2359304 | tf_op jit(solution)/shard_map/ppermute | solution.py:203
  93.4 0.8 copy-start.1
  96.8 17.4 %copy-start.2 = (bf16[512,768]{1,0:T(8,128)(2,1)}, bf16[512,768]{1,0:T(8,128)(2,1)S(1)}, u32[]{:S(2)}) copy-start(bf16[512,768]{1,0:T(8,128)(2,1)S(1)} %collective-permute-done.5.refs_6_) | copy-start | bytes 2359300
  96.8 17.4 %copy-start.3 = (bf16[512,768]{1,0:T(8,128)(2,1)}, bf16[512,768]{1,0:T(8,128)(2,1)S(1)}, u32[]{:S(2)}) copy-start(bf16[512,768]{1,0:T(8,128)(2,1)S(1)} %collective-permute-done.4.refs_5_) | copy-start | bytes 2359300
  96.9 12.3 %collective-permute-start.7 = (bf16[256,768]{1,0:T(8,128)(2,1)S(1)}, bf16[256,768]{1,0:T(8,128)(2,1)S(1)}, u32[]{:S(2)}, u32[]{:S(2)}) collective-permute-start(bf16[256,768]{1,0:T(8,128)(2,1)S(1)} %slice.7), channel_id=1, source_target_pairs={{0,7},{1,0},{2,1},{3,2},{4,3},{5,4},{6,5},{7,6},{8,15},{9,8},{10,9... | collective-permute-start | bytes 1179656 | tf_op jit(solution)/shard_map/ppermute | solution.py:211
  101.6 12.6 %collective-permute-start.6 = (bf16[256,768]{1,0:T(8,128)(2,1)S(1)}, bf16[256,768]{1,0:T(8,128)(2,1)S(1)}, u32[]{:S(2)}, u32[]{:S(2)}) collective-permute-start(bf16[256,768]{1,0:T(8,128)(2,1)S(1)} %slice.6), channel_id=1, source_target_pairs={{0,1},{1,2},{2,3},{3,4},{4,5},{5,6},{6,7},{7,0},{8,9},{9,10},{10,1... | collective-permute-start | bytes 1179656 | tf_op jit(solution)/shard_map/ppermute | solution.py:210
  109.2 5.0 %copy-start.7 = (bf16[256,768]{1,0:T(8,128)(2,1)}, bf16[256,768]{1,0:T(8,128)(2,1)S(1)}, u32[]{:S(2)}) copy-start(bf16[256,768]{1,0:T(8,128)(2,1)S(1)} %collective-permute-done.7.refs_8_) | copy-start | bytes 1179652
  114.2 0.7 copy-start.8
Sparse Core Ops, SparseCore 0:
  21.5 89.1 all-gather.1

commit v10 on v9

--- a/solution.py
+++ b/solution.py
@@ -22,6 +22,7 @@
 GROUP = GROUP_ROWS * HEADS
 GROUPS = SLOTS // GROUP
 STEP = 112
+CHAINS = 2
 CHUNK = 32
 N_Z = 8
 P_LOW = N_DP // N_Z
@@ -67,7 +68,7 @@
             state[:, head * HS : (head + 1) * HS] = rows[pl.ds(head, ROWS, stride=HEADS), :]
 
 
-def product_kernel(places, lengths, shifts, own, gathered, *refs):
+def product_kernel(places, spans, lengths, shifts, own, gathered, *refs):
     tokens, (master, query, key), (held, columns, rows, weights, total, starts, firsts, sems, token_sems) = (
         refs[:-12],
         refs[-12:-9],
@@ -75,7 +76,6 @@
     )
     me, my_z = own[0], own[1]
     blocks = held.reshape(N_DP + CHUNK, SLOTS, HS)
-    half = tokens[-1].shape[0]
 
     def copies(step):
         slots = pl.ds(step * STEP, STEP)
@@ -91,19 +91,14 @@
 
     def token_copies(group):
         wide = P_LOW * GROUP_ROWS
-        found = []
-        for i, block in enumerate(tokens):
-            last = i == len(tokens) - 1
-            found.append(
-                pltpu.make_async_copy(
-                    block.at[:, pl.ds(group * wide, wide)],
-                    columns.at[
-                        group, pl.ds(half if last else 0, block.shape[0]), pl.ds((i - 1 if last else i) * wide, wide)
-                    ],
-                    token_sems.at[group, i],
-                )
+        return [
+            pltpu.make_async_copy(
+                block.at[:, pl.ds(group * wide, wide)],
+                columns.at[group, pl.ds(row, block.shape[0]), pl.ds(column * wide, wide)],
+                token_sems.at[group, i],
             )
-        return found
+            for i, (block, (column, row)) in enumerate(zip(tokens, spans))
+        ]
 
     per_group = GROUP // STEP
     for group in range(GROUPS):
@@ -193,23 +188,26 @@
 VMEM = pl.BlockSpec(memory_space=pltpu.VMEM)
 
 
-def gather_tokens(tokens, moments):
+def gather_tokens(tokens):
     up = [(z, (z + 1) % N_Z) for z in range(N_Z)]
     down = [(z, (z - 1) % N_Z) for z in range(N_Z)]
-    half = tokens.shape[0] // 2
-    from_below, from_above = tokens, tokens
-    distances, arrays = [0], [tokens]
+    rows = tokens.shape[0] // CHAINS
+    half = rows // 2
+    distances, spans, arrays = [0], [(0, 0)], [tokens]
     for distance in range(1, N_Z // 2):
-        from_below = lax.ppermute(from_below, "tensor", up)
-        from_above = lax.ppermute(from_above, "tensor", down)
         distances += [-distance, distance]
-        if distance == 3:
-            from_below, from_above, moments = lax.optimization_barrier((from_below, from_above, moments))
-        arrays += [from_below, from_above]
     distances.append(N_Z // 2)
-    arrays.append(lax.ppermute(from_below[:half], "tensor", up))
-    arrays.append(lax.ppermute(from_above[half:], "tensor", down))
-    return tuple(distances), arrays, moments
+    for first in range(0, tokens.shape[0], rows):
+        from_below = from_above = tokens[first : first + rows]
+        for distance in range(1, N_Z // 2):
+            from_below = lax.ppermute(from_below, "tensor", up)
+            from_above = lax.ppermute(from_above, "tensor", down)
+            spans += [(2 * distance - 1, first), (2 * distance, first)]
+            arrays += [from_below, from_above]
+        spans += [(N_Z - 1, first), (N_Z - 1, first + half)]
+        arrays.append(lax.ppermute(from_below[:half], "tensor", up))
+        arrays.append(lax.ppermute(from_above[half:], "tensor", down))
+    return tuple(distances), tuple(spans), arrays
 
 
 def per_device(tokens, old_master, old_first, old_second, piece_lengths, piece_shifts):
@@ -237,23 +235,16 @@
         scratch_shapes=[slots, slots],
         name="pack",
     )(piece_lengths, piece_shifts, own, old_first, old_second)
+    distances, spans, blocks = gather_tokens(ordered)
+    ends = slice(N_Z - 1, N_Z + 1)
+    packed, blocks[ends] = lax.optimization_barrier((packed, blocks[ends]))
     received = lax.all_to_all(packed, "dp", split_axis=0, concat_axis=0, tiled=True)
-    new_first, new_second = pl.pallas_call(
-        unpack_kernel,
-        out_shape=[state, state],
-        in_specs=[SMEM] * 3 + [VMEM],
-        out_specs=[VMEM] * 2,
-        scratch_shapes=[slots, slots],
-        name="unpack",
-    )(piece_lengths, piece_shifts, own, received)
-
-    distances, blocks, (new_first, new_second) = gather_tokens(ordered, (new_first, new_second))
 
     query_cols = HQ // lax.axis_size("tensor") * HS
     key_cols = block_cols - query_cols
     group_cols = P_LOW * GROUP_ROWS
     new_master, query, key = pl.pallas_call(
-        functools.partial(product_kernel, distances),
+        functools.partial(product_kernel, distances, spans),
         out_shape=[
             state,
             jax.ShapeDtypeStruct((tokens_dev, query_cols), jnp.bfloat16),
@@ -280,6 +271,15 @@
         ),
         name="product",
     )(piece_lengths, piece_shifts, own, gathered, *blocks)
+    received, key = lax.optimization_barrier((received, key))
+    new_first, new_second = pl.pallas_call(
+        unpack_kernel,
+        out_shape=[state, state],
+        in_specs=[SMEM] * 3 + [VMEM],
+        out_specs=[VMEM] * 2,
+        scratch_shapes=[slots, slots],
+        name="unpack",
+    )(piece_lengths, piece_shifts, own, received)
     return (new_master, new_first, new_second, query, key)
 
 

time: 143 us -> 148 us (1.035)
  starting transfers between devices: 45.9 us -> 76.2 us
  waiting for transfers between devices: 39.3 us -> 12.2 us
  local copies, waits for them, and re-layouts: 1.78 us -> 3.37 us
    all_to_all x1, waiting for transfers between devices: 16.3 us -> 0.01 us  [per_device(): lax.all_to_all(packed, 'dp', split_axis=0, concat_axis=0, tiled=True)]
    ppermute x3 -> x6, starting transfers between devices: 21.2 us -> 35.9 us  [gather_tokens(): from_above = lax.ppermute(from_above, 'tensor', down)]
    ppermute x3 -> x6, waiting for transfers between devices: 12.3 us -> 5.94 us  [gather_tokens(): from_above = lax.ppermute(from_above, 'tensor', down)]
    ppermute x3 -> x6, starting transfers between devices: 5.76 us -> 11.5 us  [gather_tokens(): from_below = lax.ppermute(from_below, 'tensor', up)]
    ppermute x1 -> x2, starting transfers between devices: 4.78 us -> 10.3 us  [gather_tokens(): arrays.append(lax.ppermute(from_above[half:], 'tensor', down))]
    ppermute x1 -> x2, waiting for transfers between devices: 5.61 us -> 0.92 us  [gather_tokens(): arrays.append(lax.ppermute(from_above[half:], 'tensor', down))]
    all_to_all x1, starting transfers between devices: 12.2 us -> 14.7 us  [per_device(): lax.all_to_all(packed, 'dp', split_axis=0, concat_axis=0, tiled=True)]
    ppermute x1 -> x2, starting transfers between devices: 1.92 us -> 3.84 us  [gather_tokens(): arrays.append(lax.ppermute(from_below[:half], 'tensor', up))]
  transfers between devices with their start and end apart: 10 -> 18, of which waited for: 4 -> 5; matrix products, arithmetic and copies ran while one was open for 1% -> 2% of each run, Pallas kernels for 3% -> 15%
where the time goes in v10:
time: 148 us; the launch traced here: 147 us
  starting transfers between devices  76.2 us (51%)
  Pallas kernels  25.3 us (17%)
  between operations  14.5 us (10%)
  blocking collectives  12.9 us (9%)
  waiting for transfers between devices  12.2 us (8%)
  local copies, waits for them, and re-layouts  3.37 us (2%)
  other arithmetic  1.72 us (1%)
    ppermute x6, starting transfers between devices, gather_tokens(): from_above = lax.ppermute(from_above, 'tensor', down)  35.9 us
    pallas_call x1, Pallas kernels, per_device(): pl.pallas_call(functools.partial(product_kernel, distances, spans), out_s...  20.3 us
    all_to_all x1, starting transfers between devices, per_device(): lax.all_to_all(packed, 'dp', split_axis=0, concat_axis=0, tiled=True)  14.7 us
    all_gather x1, blocking collectives, per_device(): lax.all_gather(column, 'dp', axis_index_groups=X_GROUPS, axis=0, tiled=True)  12.9 us
    ppermute x6, starting transfers between devices, gather_tokens(): from_below = lax.ppermute(from_below, 'tensor', up)  11.5 us
    ppermute x2, starting transfers between devices, gather_tokens(): arrays.append(lax.ppermute(from_above[half:], 'tensor', down))  10.3 us
    ppermute x6, waiting for transfers between devices, gather_tokens(): from_above = lax.ppermute(from_above, 'tensor', down)  5.94 us
    ppermute x2, waiting for transfers between devices, gather_tokens(): arrays.append(lax.ppermute(from_below[:half], 'tensor', up))  5.29 us
  transfers between devices with their start and end apart: 18, of which 5 were waited for; matrix products, arithmetic and copies ran while one was open for 2% of the time, Pallas kernels for 15%

profile of v10, /device:TPU:1, one launch (start us, length us, event | category | flops | bytes accessed | tf_op | source)
XLA Modules:
  0.0 147.1 jit_solution(9564105998496954664)
XLA Ops:
  7.2 1.1 convert_element_type.9
  8.5 12.9 %all_gather.6 = bf16[2688,128]{1,0:T(8,128)(2,1)} all-gather(bf16[672,128]{1,0:T(8,128)(2,1)S(1)} %reshape.63), channel_id=1, replica_groups={{0,16,32,48},{8,24,40,56},{64,80,96,112},{72,88,104,120},{128,144,160,1..., dimensions={0}, use_global_device_ids=true | all-gather | bytes 860160 | tf_op jit(solution)/shard_map/all_gather | solution.py:220
  22.4 11.0 %collective-permute-start.1 = (bf16[256,768]{1,0:T(8,128)(2,1)S(1)}, bf16[256,768]{1,0:T(8,128)(2,1)S(1)}, u32[]{:S(2)}, u32[]{:S(2)}) collective-permute-start(bf16[256,768]{1,0:T(8,128)(2,1)S(1)} %get-tuple-element.26), channel_id=1, source_target_pairs={{0,7},{1,0},{2,1},{3,2},{4,3},{5,4},{6,5},{7,6},{8,15},{9,8},{10,9... | collective-permute-start | bytes 1179656 | tf_op jit(solution)/shard_map/ppermute | solution.py:204
  33.4 1.9 %collective-permute-start = (bf16[256,768]{1,0:T(8,128)(2,1)S(1)}, bf16[256,768]{1,0:T(8,128)(2,1)S(1)}, u32[]{:S(2)}, u32[]{:S(2)}) collective-permute-start(bf16[256,768]{1,0:T(8,128)(2,1)S(1)} %get-tuple-element.26), channel_id=1, source_target_pairs={{0,1},{1,2},{2,3},{3,4},{4,5},{5,6},{6,7},{7,0},{8,9},{9,10},{10,1... | collective-permute-start | bytes 1179656 | tf_op jit(solution)/shard_map/ppermute | solution.py:203
  35.4 3.9 %collective-permute-done.1.refs_2_ = bf16[256,768]{1,0:T(8,128)(2,1)S(1)} collective-permute-done((bf16[256,768]{1,0:T(8,128)(2,1)S(1)}, bf16[256,768]{1,0:T(8,128)(2,1)S(1)}, u32[]{:S(2)}, u32[]{:S(2)}) %collective-permute-start.1) | collective-permute-done | bytes 393248 | tf_op jit(solution)/shard_map/ppermute | solution.py:204
  39.3 5.3 %collective-permute-start.3 = (bf16[256,768]{1,0:T(8,128)(2,1)S(1)}, bf16[256,768]{1,0:T(8,128)(2,1)S(1)}, u32[]{:S(2)}, u32[]{:S(2)}) collective-permute-start(bf16[256,768]{1,0:T(8,128)(2,1)S(1)} %collective-permute-done.1.refs_2_), channel_id=1, source_target_pairs={{0,7},{1,0},{2,1},{3,2},{4,3},{5,4},{6,5},{7,6},{8,15},{9,8},{10,9... | collective-permute-start | bytes 1179656 | tf_op jit(solution)/shard_map/ppermute | solution.py:204
  44.6 1.9 %collective-permute-start.2 = (bf16[256,768]{1,0:T(8,128)(2,1)S(1)}, bf16[256,768]{1,0:T(8,128)(2,1)S(1)}, u32[]{:S(2)}, u32[]{:S(2)}) collective-permute-start(bf16[256,768]{1,0:T(8,128)(2,1)S(1)} %collective-permute-done.refs_1_), channel_id=1, source_target_pairs={{0,1},{1,2},{2,3},{3,4},{4,5},{5,6},{6,7},{7,0},{8,9},{9,10},{10,1... | collective-permute-start | bytes 1179656 | tf_op jit(solution)/shard_map/ppermute | solution.py:203
  46.5 4.6 %collective-permute-start.9 = (bf16[256,768]{1,0:T(8,128)(2,1)S(1)}, bf16[256,768]{1,0:T(8,128)(2,1)S(1)}, u32[]{:S(2)}, u32[]{:S(2)}) collective-permute-start(bf16[256,768]{1,0:T(8,128)(2,1)S(1)} %get-tuple-element.25), channel_id=1, source_target_pairs={{0,7},{1,0},{2,1},{3,2},{4,3},{5,4},{6,5},{7,6},{8,15},{9,8},{10,9... | collective-permute-start | bytes 1179656 | tf_op jit(solution)/shard_map/ppermute | solution.py:204
  51.1 1.9 %collective-permute-start.8 = (bf16[256,768]{1,0:T(8,128)(2,1)S(1)}, bf16[256,768]{1,0:T(8,128)(2,1)}, u32[]{:S(2)}, u32[]{:S(2)}) collective-permute-start(bf16[256,768]{1,0:T(8,128)(2,1)S(1)} %get-tuple-element.25), channel_id=1, source_target_pairs={{0,1},{1,2},{2,3},{3,4},{4,5},{5,6},{6,7},{7,0},{8,9},{9,10},{10,1... | collective-permute-start | bytes 1179656 | tf_op jit(solution)/shard_map/ppermute | solution.py:203
  53.1 4.6 %collective-permute-start.5 = (bf16[256,768]{1,0:T(8,128)(2,1)S(1)}, bf16[256,768]{1,0:T(8,128)(2,1)S(1)}, u32[]{:S(2)}, u32[]{:S(2)}) collective-permute-start(bf16[256,768]{1,0:T(8,128)(2,1)S(1)} %collective-permute-done.3.refs_4_), channel_id=1, source_target_pairs={{0,7},{1,0},{2,1},{3,2},{4,3},{5,4},{6,5},{7,6},{8,15},{9,8},{10,9... | collective-permute-start | bytes 1179656 | tf_op jit(solution)/shard_map/ppermute | solution.py:204
  57.7 1.9 %collective-permute-start.4 = (bf16[256,768]{1,0:T(8,128)(2,1)S(1)}, bf16[256,768]{1,0:T(8,128)(2,1)S(1)}, u32[]{:S(2)}, u32[]{:S(2)}) collective-permute-start(bf16[256,768]{1,0:T(8,128)(2,1)S(1)} %collective-permute-done.2.refs_3_), channel_id=1, source_target_pairs={{0,1},{1,2},{2,3},{3,4},{4,5},{5,6},{6,7},{7,0},{8,9},{9,10},{10,1... | collective-permute-start | bytes 1179656 | tf_op jit(solution)/shard_map/ppermute | solution.py:203
  59.6 5.1 %collective-permute-start.11 = (bf16[256,768]{1,0:T(8,128)(2,1)S(1)}, bf16[256,768]{1,0:T(8,128)(2,1)}, u32[]{:S(2)}, u32[]{:S(2)}) collective-permute-start(bf16[256,768]{1,0:T(8,128)(2,1)S(1)} %collective-permute-done.9.refs_10_), channel_id=1, source_target_pairs={{0,7},{1,0},{2,1},{3,2},{4,3},{5,4},{6,5},{7,6},{8,15},{9,8},{10,9... | collective-permute-start | bytes 1179656 | tf_op jit(solution)/shard_map/ppermute | solution.py:204
  64.7 1.9 %collective-permute-start.10 = (bf16[256,768]{1,0:T(8,128)(2,1)}, bf16[256,768]{1,0:T(8,128)(2,1)}, u32[]{:S(2)}, u32[]{:S(2)}) collective-permute-start(bf16[256,768]{1,0:T(8,128)(2,1)} %collective-permute-done.8.refs_9_), channel_id=1, source_target_pairs={{0,1},{1,2},{2,3},{3,4},{4,5},{5,6},{6,7},{7,0},{8,9},{9,10},{10,1... | collective-permute-start | bytes 1179656 | tf_op jit(solution)/shard_map/ppermute | solution.py:203
  67.7 5.4 %collective-permute-start.7 = (bf16[128,768]{1,0:T(8,128)(2,1)S(1)}, bf16[128,768]{1,0:T(8,128)(2,1)S(1)}, u32[]{:S(2)}, u32[]{:S(2)}) collective-permute-start(bf16[128,768]{1,0:T(8,128)(2,1)S(1)} %slice.26), channel_id=1, source_target_pairs={{0,7},{1,0},{2,1},{3,2},{4,3},{5,4},{6,5},{7,6},{8,15},{9,8},{10,9... | collective-permute-start | bytes 589832 | tf_op jit(solution)/shard_map/ppermute | solution.py:209
  73.2 1.9 %collective-permute-start.6 = (bf16[128,768]{1,0:T(8,128)(2,1)S(1)}, bf16[128,768]{1,0:T(8,128)(2,1)}, u32[]{:S(2)}, u32[]{:S(2)}) collective-permute-start(bf16[128,768]{1,0:T(8,128)(2,1)S(1)} %slice.25), channel_id=1, source_target_pairs={{0,1},{1,2},{2,3},{3,4},{4,5},{5,6},{6,7},{7,0},{8,9},{9,10},{10,1... | collective-permute-start | bytes 589832 | tf_op jit(solution)/shard_map/ppermute | solution.py:208
  76.1 5.4 %collective-permute-start.13 = (bf16[256,768]{1,0:T(8,128)(2,1)}, bf16[256,768]{1,0:T(8,128)(2,1)S(1)}, u32[]{:S(2)}, u32[]{:S(2)}) collective-permute-start(bf16[256,768]{1,0:T(8,128)(2,1)} %collective-permute-done.11.refs_12_), channel_id=1, source_target_pairs={{0,7},{1,0},{2,1},{3,2},{4,3},{5,4},{6,5},{7,6},{8,15},{9,8},{10,9... | collective-permute-start | bytes 1179656 | tf_op jit(solution)/shard_map/ppermute | solution.py:204
  81.6 1.9 %collective-permute-start.12 = (bf16[256,768]{1,0:T(8,128)(2,1)}, bf16[256,768]{1,0:T(8,128)(2,1)}, u32[]{:S(2)}, u32[]{:S(2)}) collective-permute-start(bf16[256,768]{1,0:T(8,128)(2,1)} %collective-permute-done.10.refs_11_), channel_id=1, source_target_pairs={{0,1},{1,2},{2,3},{3,4},{4,5},{5,6},{6,7},{7,0},{8,9},{9,10},{10,1... | collective-permute-start | bytes 1179656 | tf_op jit(solution)/shard_map/ppermute | solution.py:203
  84.1 2.4 %pack.1 = bf16[64,16,256]{2,1,0:T(8,128)(2,1)} custom-call(s32[64]{0:T(128)} %lengths.5, s32[64]{0:T(128)} %shifts.5, s32[2]{0:T(128)} %pad_add_fusion.own, f32[96,896]{1,0:T(8,128)} %first.1, f32[96,896]{1,0:T(8,128)} %second.1), custom_call_target="tpu_custom_call" | custom-call | tf_op jit(solution)/shard_map/pack/pallas_call | solution.py:230
  86.6 14.7 %all-to-all-start = ((bf16[64,16,256]{2,1,0:T(8,128)(2,1)}), bf16[64,16,256]{2,1,0:T(8,128)(2,1)S(1)}, u32[]{:S(2)}, u32[]{:S(2)}) async-start(bf16[64,16,256]{2,1,0:T(8,128)(2,1)} %pack.1), calls=%async_computation | async-start | bytes 1048576 | tf_op jit(solution)/shard_map/all_to_all | solution.py:241
  101.3 4.8 %collective-permute-start.15 = (bf16[128,768]{1,0:T(8,128)(2,1)S(1)}, bf16[128,768]{1,0:T(8,128)(2,1)S(1)}, u32[]{:S(2)}, u32[]{:S(2)}) collective-permute-start(bf16[128,768]{1,0:T(8,128)(2,1)S(1)} %slice.29), channel_id=1, source_target_pairs={{0,7},{1,0},{2,1},{3,2},{4,3},{5,4},{6,5},{7,6},{8,15},{9,8},{10,9... | collective-permute-start | bytes 589832 | tf_op jit(solution)/shard_map/ppermute | solution.py:209
  107.1 1.9 %collective-permute-start.14 = (bf16[128,768]{1,0:T(8,128)(2,1)S(1)}, bf16[128,768]{1,0:T(8,128)(2,1)S(1)}, u32[]{:S(2)}, u32[]{:S(2)}) collective-permute-start(bf16[128,768]{1,0:T(8,128)(2,1)S(1)} %slice.28), channel_id=1, source_target_pairs={{0,1},{1,2},{2,3},{3,4},{4,5},{5,6},{6,7},{7,0},{8,9},{9,10},{10,1... | collective-permute-start | bytes 589832 | tf_op jit(solution)/shard_map/ppermute | solution.py:208
  110.6 5.3 %collective-permute-done.14.refs_15_ = bf16[128,768]{1,0:T(8,128)(2,1)S(1)} collective-permute-done((bf16[128,768]{1,0:T(8,128)(2,1)S(1)}, bf16[128,768]{1,0:T(8,128)(2,1)S(1)}, u32[]{:S(2)}, u32[]{:S(2)}) %collective-permute-start.14) | collective-permute-done | bytes 196640 | tf_op jit(solution)/shard_map/ppermute | solution.py:208
  116.6 20.3 %product.1 = (f32[96,896]{1,0:T(8,128)}, bf16[512,768]{1,0:T(8,128)(2,1)}, bf16[512,128]{1,0:T(8,128)(2,1)}) custom-call(s32[64]{0:T(128)} %lengths.5, s32[64]{0:T(128)} %shifts.5, s32[2]{0:T(128)} %pad_add_fusion.own, bf16[8,2,4,672,128]{4,3,2,1,0:T(8,128)(2,1)} %bitcast.6, bf16[512,768]{1,0:T(8,128)(2,1)} %copy-done.2, bf16[256,768]{1,0:T(8,128)(2,1)} %copy-done.7, ...), custom_call_target="tpu_custom_call" | custom-call | flops 5637144576 | bytes 17301504 | tf_op jit(solution)/shard_map/product/pallas_call | solution.py:246
  137.7 2.5 %unpack.1 = (f32[96,896]{1,0:T(8,128)}, f32[96,896]{1,0:T(8,128)}) custom-call(s32[64]{0:T(128)} %lengths.5, s32[64]{0:T(128)} %shifts.5, s32[2]{0:T(128)} %pad_add_fusion.own, bf16[64,16,256]{2,1,0:T(8,128)(2,1)} %copy-done.1), custom_call_target="tpu_custom_call" | custom-call | tf_op jit(solution)/shard_map/unpack/pallas_call | solution.py:275
  (55 shorter events, 8.0 us)
Async XLA Ops:
  7.2 108.7 %all-gather.2.cloned.1.call-start = ((), (), s32[]{:S(2)}) async-start(), calls=%async_computation.1 | async-start | bytes 11698176 | tf_op jit(solution)/shard_map/all_gather | solution.py:221
  22.4 78.9 %copy-start.2 = (bf16[512,768]{1,0:T(8,128)(2,1)}, bf16[512,768]{1,0:T(8,128)(2,1)S(1)}, u32[]{:S(2)}) copy-start(bf16[512,768]{1,0:T(8,128)(2,1)S(1)} %fusion.2.refs_0_) | copy-start | bytes 2359300
  22.4 16.8 %collective-permute-start.1 = (bf16[256,768]{1,0:T(8,128)(2,1)S(1)}, bf16[256,768]{1,0:T(8,128)(2,1)S(1)}, u32[]{:S(2)}, u32[]{:S(2)}) collective-permute-start(bf16[256,768]{1,0:T(8,128)(2,1)S(1)} %get-tuple-element.26), channel_id=1, source_target_pairs={{0,7},{1,0},{2,1},{3,2},{4,3},{5,4},{6,5},{7,6},{8,15},{9,8},{10,9... | collective-permute-start | bytes 1179656 | tf_op jit(solution)/shard_map/ppermute | solution.py:204
  33.4 11.2 %collective-permute-start = (bf16[256,768]{1,0:T(8,128)(2,1)S(1)}, bf16[256,768]{1,0:T(8,128)(2,1)S(1)}, u32[]{:S(2)}, u32[]{:S(2)}) collective-permute-start(bf16[256,768]{1,0:T(8,128)(2,1)S(1)} %get-tuple-element.26), channel_id=1, source_target_pairs={{0,1},{1,2},{2,3},{3,4},{4,5},{5,6},{6,7},{7,0},{8,9},{9,10},{10,1... | collective-permute-start | bytes 1179656 | tf_op jit(solution)/shard_map/ppermute | solution.py:203
  39.3 27.4 %copy-start.6 = (bf16[256,768]{1,0:T(8,128)(2,1)}, bf16[256,768]{1,0:T(8,128)(2,1)S(1)}, u32[]{:S(2)}) copy-start(bf16[256,768]{1,0:T(8,128)(2,1)S(1)} %collective-permute-done.1.refs_2_) | copy-start | bytes 1179652
  39.3 13.8 %collective-permute-start.3 = (bf16[256,768]{1,0:T(8,128)(2,1)S(1)}, bf16[256,768]{1,0:T(8,128)(2,1)S(1)}, u32[]{:S(2)}, u32[]{:S(2)}) collective-permute-start(bf16[256,768]{1,0:T(8,128)(2,1)S(1)} %collective-permute-done.1.refs_2_), channel_id=1, source_target_pairs={{0,7},{1,0},{2,1},{3,2},{4,3},{5,4},{6,5},{7,6},{8,15},{9,8},{10,9... | collective-permute-start | bytes 1179656 | tf_op jit(solution)/shard_map/ppermute | solution.py:204
  44.6 22.1 %copy-start.7 = (bf16[256,768]{1,0:T(8,128)(2,1)}, bf16[256,768]{1,0:T(8,128)(2,1)S(1)}, u32[]{:S(2)}) copy-start(bf16[256,768]{1,0:T(8,128)(2,1)S(1)} %collective-permute-done.refs_1_) | copy-start | bytes 1179652
  44.6 13.0 %collective-permute-start.2 = (bf16[256,768]{1,0:T(8,128)(2,1)S(1)}, bf16[256,768]{1,0:T(8,128)(2,1)S(1)}, u32[]{:S(2)}, u32[]{:S(2)}) collective-permute-start(bf16[256,768]{1,0:T(8,128)(2,1)S(1)} %collective-permute-done.refs_1_), channel_id=1, source_target_pairs={{0,1},{1,2},{2,3},{3,4},{4,5},{5,6},{6,7},{7,0},{8,9},{9,10},{10,1... | collective-permute-start | bytes 1179656 | tf_op jit(solution)/shard_map/ppermute | solution.py:203
  46.5 13.1 %collective-permute-start.9 = (bf16[256,768]{1,0:T(8,128)(2,1)S(1)}, bf16[256,768]{1,0:T(8,128)(2,1)S(1)}, u32[]{:S(2)}, u32[]{:S(2)}) collective-permute-start(bf16[256,768]{1,0:T(8,128)(2,1)S(1)} %get-tuple-element.25), channel_id=1, source_target_pairs={{0,7},{1,0},{2,1},{3,2},{4,3},{5,4},{6,5},{7,6},{8,15},{9,8},{10,9... | collective-permute-start | bytes 1179656 | tf_op jit(solution)/shard_map/ppermute | solution.py:204
  51.1 13.6 %collective-permute-start.8 = (bf16[256,768]{1,0:T(8,128)(2,1)S(1)}, bf16[256,768]{1,0:T(8,128)(2,1)}, u32[]{:S(2)}, u32[]{:S(2)}) collective-permute-start(bf16[256,768]{1,0:T(8,128)(2,1)S(1)} %get-tuple-element.25), channel_id=1, source_target_pairs={{0,1},{1,2},{2,3},{3,4},{4,5},{5,6},{6,7},{7,0},{8,9},{9,10},{10,1... | collective-permute-start | bytes 1179656 | tf_op jit(solution)/shard_map/ppermute | solution.py:203
  53.1 14.6 %collective-permute-start.5 = (bf16[256,768]{1,0:T(8,128)(2,1)S(1)}, bf16[256,768]{1,0:T(8,128)(2,1)S(1)}, u32[]{:S(2)}, u32[]{:S(2)}) collective-permute-start(bf16[256,768]{1,0:T(8,128)(2,1)S(1)} %collective-permute-done.3.refs_4_), channel_id=1, source_target_pairs={{0,7},{1,0},{2,1},{3,2},{4,3},{5,4},{6,5},{7,6},{8,15},{9,8},{10,9... | collective-permute-start | bytes 1179656 | tf_op jit(solution)/shard_map/ppermute | solution.py:204
  57.7 15.5 %collective-permute-start.4 = (bf16[256,768]{1,0:T(8,128)(2,1)S(1)}, bf16[256,768]{1,0:T(8,128)(2,1)S(1)}, u32[]{:S(2)}, u32[]{:S(2)}) collective-permute-start(bf16[256,768]{1,0:T(8,128)(2,1)S(1)} %collective-permute-done.2.refs_3_), channel_id=1, source_target_pairs={{0,1},{1,2},{2,3},{3,4},{4,5},{5,6},{6,7},{7,0},{8,9},{9,10},{10,1... | collective-permute-start | bytes 1179656 | tf_op jit(solution)/shard_map/ppermute | solution.py:203
  59.6 16.5 %collective-permute-start.11 = (bf16[256,768]{1,0:T(8,128)(2,1)S(1)}, bf16[256,768]{1,0:T(8,128)(2,1)}, u32[]{:S(2)}, u32[]{:S(2)}) collective-permute-start(bf16[256,768]{1,0:T(8,128)(2,1)S(1)} %collective-permute-done.9.refs_10_), channel_id=1, source_target_pairs={{0,7},{1,0},{2,1},{3,2},{4,3},{5,4},{6,5},{7,6},{8,15},{9,8},{10,9... | collective-permute-start | bytes 1179656 | tf_op jit(solution)/shard_map/ppermute | solution.py:204
  64.7 16.8 %collective-permute-start.10 = (bf16[256,768]{1,0:T(8,128)(2,1)}, bf16[256,768]{1,0:T(8,128)(2,1)}, u32[]{:S(2)}, u32[]{:S(2)}) collective-permute-start(bf16[256,768]{1,0:T(8,128)(2,1)} %collective-permute-done.8.refs_9_), channel_id=1, source_target_pairs={{0,1},{1,2},{2,3},{3,4},{4,5},{5,6},{6,7},{7,0},{8,9},{9,10},{10,1... | collective-permute-start | bytes 1179656 | tf_op jit(solution)/shard_map/ppermute | solution.py:203
  67.7 48.2 %copy-start.3 = (bf16[256,768]{1,0:T(8,128)(2,1)}, bf16[256,768]{1,0:T(8,128)(2,1)S(1)}, u32[]{:S(2)}) copy-start(bf16[256,768]{1,0:T(8,128)(2,1)S(1)} %collective-permute-done.5.refs_6_) | copy-start | bytes 1179652
  67.7 18.8 %collective-permute-start.7 = (bf16[128,768]{1,0:T(8,128)(2,1)S(1)}, bf16[128,768]{1,0:T(8,128)(2,1)S(1)}, u32[]{:S(2)}, u32[]{:S(2)}) collective-permute-start(bf16[128,768]{1,0:T(8,128)(2,1)S(1)} %slice.26), channel_id=1, source_target_pairs={{0,7},{1,0},{2,1},{3,2},{4,3},{5,4},{6,5},{7,6},{8,15},{9,8},{10,9... | collective-permute-start | bytes 589832 | tf_op jit(solution)/shard_map/ppermute | solution.py:209
  73.2 42.7 %copy-start.4 = (bf16[256,768]{1,0:T(8,128)(2,1)}, bf16[256,768]{1,0:T(8,128)(2,1)S(1)}, u32[]{:S(2)}) copy-start(bf16[256,768]{1,0:T(8,128)(2,1)S(1)} %collective-permute-done.4.refs_5_) | copy-start | bytes 1179652
  73.2 13.4 %collective-permute-start.6 = (bf16[128,768]{1,0:T(8,128)(2,1)S(1)}, bf16[128,768]{1,0:T(8,128)(2,1)}, u32[]{:S(2)}, u32[]{:S(2)}) collective-permute-start(bf16[128,768]{1,0:T(8,128)(2,1)S(1)} %slice.25), channel_id=1, source_target_pairs={{0,1},{1,2},{2,3},{3,4},{4,5},{5,6},{6,7},{7,0},{8,9},{9,10},{10,1... | collective-permute-start | bytes 589832 | tf_op jit(solution)/shard_map/ppermute | solution.py:208
  76.1 25.1 %collective-permute-start.13 = (bf16[256,768]{1,0:T(8,128)(2,1)}, bf16[256,768]{1,0:T(8,128)(2,1)S(1)}, u32[]{:S(2)}, u32[]{:S(2)}) collective-permute-start(bf16[256,768]{1,0:T(8,128)(2,1)} %collective-permute-done.11.refs_12_), channel_id=1, source_target_pairs={{0,7},{1,0},{2,1},{3,2},{4,3},{5,4},{6,5},{7,6},{8,15},{9,8},{10,9... | collective-permute-start | bytes 1179656 | tf_op jit(solution)/shard_map/ppermute | solution.py:204
  81.6 24.6 %collective-permute-start.12 = (bf16[256,768]{1,0:T(8,128)(2,1)}, bf16[256,768]{1,0:T(8,128)(2,1)}, u32[]{:S(2)}, u32[]{:S(2)}) collective-permute-start(bf16[256,768]{1,0:T(8,128)(2,1)} %collective-permute-done.10.refs_11_), channel_id=1, source_target_pairs={{0,1},{1,2},{2,3},{3,4},{4,5},{5,6},{6,7},{7,0},{8,9},{9,10},{10,1... | collective-permute-start | bytes 1179656 | tf_op jit(solution)/shard_map/ppermute | solution.py:203
  86.6 29.3 %copy-start.11 = (bf16[128,768]{1,0:T(8,128)(2,1)}, bf16[128,768]{1,0:T(8,128)(2,1)S(1)}, u32[]{:S(2)}) copy-start(bf16[128,768]{1,0:T(8,128)(2,1)S(1)} %collective-permute-done.7.refs_8_) | copy-start | bytes 589828
  86.6 50.3 %all-to-all-start = ((bf16[64,16,256]{2,1,0:T(8,128)(2,1)}), bf16[64,16,256]{2,1,0:T(8,128)(2,1)S(1)}, u32[]{:S(2)}, u32[]{:S(2)}) async-start(bf16[64,16,256]{2,1,0:T(8,128)(2,1)} %pack.1), calls=%async_computation | async-start | bytes 1048576 | tf_op jit(solution)/shard_map/all_to_all | solution.py:241
  101.3 8.6 %collective-permute-start.15 = (bf16[128,768]{1,0:T(8,128)(2,1)S(1)}, bf16[128,768]{1,0:T(8,128)(2,1)S(1)}, u32[]{:S(2)}, u32[]{:S(2)}) collective-permute-start(bf16[128,768]{1,0:T(8,128)(2,1)S(1)} %slice.29), channel_id=1, source_target_pairs={{0,7},{1,0},{2,1},{3,2},{4,3},{5,4},{6,5},{7,6},{8,15},{9,8},{10,9... | collective-permute-start | bytes 589832 | tf_op jit(solution)/shard_map/ppermute | solution.py:209
  107.1 8.8 %collective-permute-start.14 = (bf16[128,768]{1,0:T(8,128)(2,1)S(1)}, bf16[128,768]{1,0:T(8,128)(2,1)S(1)}, u32[]{:S(2)}, u32[]{:S(2)}) collective-permute-start(bf16[128,768]{1,0:T(8,128)(2,1)S(1)} %slice.28), channel_id=1, source_target_pairs={{0,1},{1,2},{2,3},{3,4},{4,5},{5,6},{6,7},{7,0},{8,9},{9,10},{10,1... | collective-permute-start | bytes 589832 | tf_op jit(solution)/shard_map/ppermute | solution.py:208
  (8 other events, 77.7 us)
Sparse Core Ops, SparseCore 0:
  21.5 77.9 all-gather.1

commit v11 on v10

--- a/solution.py
+++ b/solution.py
@@ -236,8 +236,7 @@
         name="pack",
     )(piece_lengths, piece_shifts, own, old_first, old_second)
     distances, spans, blocks = gather_tokens(ordered)
-    ends = slice(N_Z - 1, N_Z + 1)
-    packed, blocks[ends] = lax.optimization_barrier((packed, blocks[ends]))
+    packed, blocks = lax.optimization_barrier((packed, blocks))
     received = lax.all_to_all(packed, "dp", split_axis=0, concat_axis=0, tiled=True)
 
     query_cols = HQ // lax.axis_size("tensor") * HS

time: 148 us -> 142 us (0.959)
  waiting for transfers between devices: 12.2 us -> 7.7 us
  local copies, waits for them, and re-layouts: 3.37 us -> 1.14 us
    ppermute x2, waiting for transfers between devices: 5.29 us -> 3.01 us  [gather_tokens(): arrays.append(lax.ppermute(from_below[:half], 'tensor', up))]
  transfers between devices with their start and end apart: 18 -> 18, of which waited for: 5 -> 6; matrix products, arithmetic and copies ran while one was open for 2% -> 1% of each run, Pallas kernels for 15% -> 16%
where the time goes in v11:
time: 142 us; the launch traced here: 141 us
  starting transfers between devices  77 us (54%)
  Pallas kernels  25.3 us (18%)
  between operations  14.5 us (10%)
  blocking collectives  12.9 us (9%)
  waiting for transfers between devices  7.7 us (5%)
  other arithmetic  1.75 us (1%)
    ppermute x6, starting transfers between devices, gather_tokens(): from_above = lax.ppermute(from_above, 'tensor', down)  36.4 us
    pallas_call x1, Pallas kernels, per_device(): pl.pallas_call(functools.partial(product_kernel, distances, spans), out_s...  20.3 us
    all_to_all x1, starting transfers between devices, per_device(): lax.all_to_all(packed, 'dp', split_axis=0, concat_axis=0, tiled=True)  14.4 us
    all_gather x1, blocking collectives, per_device(): lax.all_gather(column, 'dp', axis_index_groups=X_GROUPS, axis=0, tiled=True)  12.9 us
    ppermute x6, starting transfers between devices, gather_tokens(): from_below = lax.ppermute(from_below, 'tensor', up)  11.5 us
    ppermute x2, starting transfers between devices, gather_tokens(): arrays.append(lax.ppermute(from_above[half:], 'tensor', down))  10.9 us
    ppermute x6, waiting for transfers between devices, gather_tokens(): from_above = lax.ppermute(from_above, 'tensor', down)  4.63 us
    ppermute x2, starting transfers between devices, gather_tokens(): arrays.append(lax.ppermute(from_below[:half], 'tensor', up))  3.84 us
  transfers between devices with their start and end apart: 18, of which 6 were waited for; matrix products, arithmetic and copies ran while one was open for 1% of the time, Pallas kernels for 16%

profile of v11, /device:TPU:1, one launch (start us, length us, event | category | flops | bytes accessed | tf_op | source)
XLA Modules:
  0.0 141.2 jit_solution(5043781004203359938)
XLA Ops:
  7.2 1.1 convert_element_type.10
  8.5 12.9 %all_gather.6 = bf16[2688,128]{1,0:T(8,128)(2,1)} all-gather(bf16[672,128]{1,0:T(8,128)(2,1)S(1)} %reshape.63), channel_id=1, replica_groups={{0,16,32,48},{8,24,40,56},{64,80,96,112},{72,88,104,120},{128,144,160,1..., dimensions={0}, use_global_device_ids=true | all-gather | bytes 860160 | tf_op jit(solution)/shard_map/all_gather | solution.py:220
  22.4 11.0 %collective-permute-start.9 = (bf16[256,768]{1,0:T(8,128)(2,1)S(1)}, bf16[256,768]{1,0:T(8,128)(2,1)S(1)}, u32[]{:S(2)}, u32[]{:S(2)}) collective-permute-start(bf16[256,768]{1,0:T(8,128)(2,1)S(1)} %get-tuple-element.55), channel_id=1, source_target_pairs={{0,7},{1,0},{2,1},{3,2},{4,3},{5,4},{6,5},{7,6},{8,15},{9,8},{10,9... | collective-permute-start | bytes 1179656 | tf_op jit(solution)/shard_map/ppermute | solution.py:204
  33.4 1.9 %collective-permute-start.8 = (bf16[256,768]{1,0:T(8,128)(2,1)S(1)}, bf16[256,768]{1,0:T(8,128)(2,1)S(1)}, u32[]{:S(2)}, u32[]{:S(2)}) collective-permute-start(bf16[256,768]{1,0:T(8,128)(2,1)S(1)} %get-tuple-element.55), channel_id=1, source_target_pairs={{0,1},{1,2},{2,3},{3,4},{4,5},{5,6},{6,7},{7,0},{8,9},{9,10},{10,1... | collective-permute-start | bytes 1179656 | tf_op jit(solution)/shard_map/ppermute | solution.py:203
  35.4 4.6 %collective-permute-start.1 = (bf16[256,768]{1,0:T(8,128)(2,1)S(1)}, bf16[256,768]{1,0:T(8,128)(2,1)S(1)}, u32[]{:S(2)}, u32[]{:S(2)}) collective-permute-start(bf16[256,768]{1,0:T(8,128)(2,1)S(1)} %get-tuple-element.56), channel_id=1, source_target_pairs={{0,7},{1,0},{2,1},{3,2},{4,3},{5,4},{6,5},{7,6},{8,15},{9,8},{10,9... | collective-permute-start | bytes 1179656 | tf_op jit(solution)/shard_map/ppermute | solution.py:204
  39.9 1.9 %collective-permute-start = (bf16[256,768]{1,0:T(8,128)(2,1)S(1)}, bf16[256,768]{1,0:T(8,128)(2,1)S(1)}, u32[]{:S(2)}, u32[]{:S(2)}) collective-permute-start(bf16[256,768]{1,0:T(8,128)(2,1)S(1)} %get-tuple-element.56), channel_id=1, source_target_pairs={{0,1},{1,2},{2,3},{3,4},{4,5},{5,6},{6,7},{7,0},{8,9},{9,10},{10,1... | collective-permute-start | bytes 1179656 | tf_op jit(solution)/shard_map/ppermute | solution.py:203
  41.9 4.6 %collective-permute-start.11 = (bf16[256,768]{1,0:T(8,128)(2,1)S(1)}, bf16[256,768]{1,0:T(8,128)(2,1)S(1)}, u32[]{:S(2)}, u32[]{:S(2)}) collective-permute-start(bf16[256,768]{1,0:T(8,128)(2,1)S(1)} %collective-permute-done.9.refs_10_), channel_id=1, source_target_pairs={{0,7},{1,0},{2,1},{3,2},{4,3},{5,4},{6,5},{7,6},{8,15},{9,8},{10,9... | collective-permute-start | bytes 1179656 | tf_op jit(solution)/shard_map/ppermute | solution.py:204
  46.5 1.9 %collective-permute-start.10 = (bf16[256,768]{1,0:T(8,128)(2,1)S(1)}, bf16[256,768]{1,0:T(8,128)(2,1)S(1)}, u32[]{:S(2)}, u32[]{:S(2)}) collective-permute-start(bf16[256,768]{1,0:T(8,128)(2,1)S(1)} %collective-permute-done.8.refs_9_), channel_id=1, source_target_pairs={{0,1},{1,2},{2,3},{3,4},{4,5},{5,6},{6,7},{7,0},{8,9},{9,10},{10,1... | collective-permute-start | bytes 1179656 | tf_op jit(solution)/shard_map/ppermute | solution.py:203
  48.9 5.4 %collective-permute-start.3 = (bf16[256,768]{1,0:T(8,128)(2,1)S(1)}, bf16[256,768]{1,0:T(8,128)(2,1)S(1)}, u32[]{:S(2)}, u32[]{:S(2)}) collective-permute-start(bf16[256,768]{1,0:T(8,128)(2,1)S(1)} %collective-permute-done.1.refs_2_), channel_id=1, source_target_pairs={{0,7},{1,0},{2,1},{3,2},{4,3},{5,4},{6,5},{7,6},{8,15},{9,8},{10,9... | collective-permute-start | bytes 1179656 | tf_op jit(solution)/shard_map/ppermute | solution.py:204
  54.4 1.9 %collective-permute-start.2 = (bf16[256,768]{1,0:T(8,128)(2,1)S(1)}, bf16[256,768]{1,0:T(8,128)(2,1)S(1)}, u32[]{:S(2)}, u32[]{:S(2)}) collective-permute-start(bf16[256,768]{1,0:T(8,128)(2,1)S(1)} %collective-permute-done.refs_1_), channel_id=1, source_target_pairs={{0,1},{1,2},{2,3},{3,4},{4,5},{5,6},{6,7},{7,0},{8,9},{9,10},{10,1... | collective-permute-start | bytes 1179656 | tf_op jit(solution)/shard_map/ppermute | solution.py:203
  56.3 1.1 collective-permute-done.11.refs_12_
  57.3 5.4 %collective-permute-start.13 = (bf16[256,768]{1,0:T(8,128)(2,1)S(1)}, bf16[256,768]{1,0:T(8,128)(2,1)S(1)}, u32[]{:S(2)}, u32[]{:S(2)}) collective-permute-start(bf16[256,768]{1,0:T(8,128)(2,1)S(1)} %collective-permute-done.11.refs_12_), channel_id=1, source_target_pairs={{0,7},{1,0},{2,1},{3,2},{4,3},{5,4},{6,5},{7,6},{8,15},{9,8},{10,9... | collective-permute-start | bytes 1179656 | tf_op jit(solution)/shard_map/ppermute | solution.py:204
  62.8 1.9 %collective-permute-start.12 = (bf16[256,768]{1,0:T(8,128)(2,1)S(1)}, bf16[256,768]{1,0:T(8,128)(2,1)S(1)}, u32[]{:S(2)}, u32[]{:S(2)}) collective-permute-start(bf16[256,768]{1,0:T(8,128)(2,1)S(1)} %collective-permute-done.10.refs_11_), channel_id=1, source_target_pairs={{0,1},{1,2},{2,3},{3,4},{4,5},{5,6},{6,7},{7,0},{8,9},{9,10},{10,1... | collective-permute-start | bytes 1179656 | tf_op jit(solution)/shard_map/ppermute | solution.py:203
  65.8 5.4 %collective-permute-start.5 = (bf16[256,768]{1,0:T(8,128)(2,1)S(1)}, bf16[256,768]{1,0:T(8,128)(2,1)S(1)}, u32[]{:S(2)}, u32[]{:S(2)}) collective-permute-start(bf16[256,768]{1,0:T(8,128)(2,1)S(1)} %collective-permute-done.3.refs_4_), channel_id=1, source_target_pairs={{0,7},{1,0},{2,1},{3,2},{4,3},{5,4},{6,5},{7,6},{8,15},{9,8},{10,9... | collective-permute-start | bytes 1179656 | tf_op jit(solution)/shard_map/ppermute | solution.py:204
  71.2 1.9 %collective-permute-start.4 = (bf16[256,768]{1,0:T(8,128)(2,1)S(1)}, bf16[256,768]{1,0:T(8,128)(2,1)S(1)}, u32[]{:S(2)}, u32[]{:S(2)}) collective-permute-start(bf16[256,768]{1,0:T(8,128)(2,1)S(1)} %collective-permute-done.2.refs_3_), channel_id=1, source_target_pairs={{0,1},{1,2},{2,3},{3,4},{4,5},{5,6},{6,7},{7,0},{8,9},{9,10},{10,1... | collective-permute-start | bytes 1179656 | tf_op jit(solution)/shard_map/ppermute | solution.py:203
  74.2 5.4 %collective-permute-start.15 = (bf16[128,768]{1,0:T(8,128)(2,1)S(1)}, bf16[128,768]{1,0:T(8,128)(2,1)S(1)}, u32[]{:S(2)}, u32[]{:S(2)}) collective-permute-start(bf16[128,768]{1,0:T(8,128)(2,1)S(1)} %slice.29), channel_id=1, source_target_pairs={{0,7},{1,0},{2,1},{3,2},{4,3},{5,4},{6,5},{7,6},{8,15},{9,8},{10,9... | collective-permute-start | bytes 589832 | tf_op jit(solution)/shard_map/ppermute | solution.py:209
  79.7 1.9 %collective-permute-start.14 = (bf16[128,768]{1,0:T(8,128)(2,1)S(1)}, bf16[128,768]{1,0:T(8,128)(2,1)}, u32[]{:S(2)}, u32[]{:S(2)}) collective-permute-start(bf16[128,768]{1,0:T(8,128)(2,1)S(1)} %slice.28), channel_id=1, source_target_pairs={{0,1},{1,2},{2,3},{3,4},{4,5},{5,6},{6,7},{7,0},{8,9},{9,10},{10,1... | collective-permute-start | bytes 589832 | tf_op jit(solution)/shard_map/ppermute | solution.py:208
  82.6 5.4 %collective-permute-start.7 = (bf16[128,768]{1,0:T(8,128)(2,1)S(1)}, bf16[128,768]{1,0:T(8,128)(2,1)}, u32[]{:S(2)}, u32[]{:S(2)}) collective-permute-start(bf16[128,768]{1,0:T(8,128)(2,1)S(1)} %slice.26), channel_id=1, source_target_pairs={{0,7},{1,0},{2,1},{3,2},{4,3},{5,4},{6,5},{7,6},{8,15},{9,8},{10,9... | collective-permute-start | bytes 589832 | tf_op jit(solution)/shard_map/ppermute | solution.py:209
  88.1 1.9 %collective-permute-start.6 = (bf16[128,768]{1,0:T(8,128)(2,1)S(1)}, bf16[128,768]{1,0:T(8,128)(2,1)}, u32[]{:S(2)}, u32[]{:S(2)}) collective-permute-start(bf16[128,768]{1,0:T(8,128)(2,1)S(1)} %slice.25), channel_id=1, source_target_pairs={{0,1},{1,2},{2,3},{3,4},{4,5},{5,6},{6,7},{7,0},{8,9},{9,10},{10,1... | collective-permute-start | bytes 589832 | tf_op jit(solution)/shard_map/ppermute | solution.py:208
  90.8 2.4 %pack.1 = bf16[64,16,256]{2,1,0:T(8,128)(2,1)} custom-call(s32[64]{0:T(128)} %lengths.5, s32[64]{0:T(128)} %shifts.5, s32[2]{0:T(128)} %pad_add_fusion.own, f32[96,896]{1,0:T(8,128)} %first.1, f32[96,896]{1,0:T(8,128)} %second.1), custom_call_target="tpu_custom_call" | custom-call | tf_op jit(solution)/shard_map/pack/pallas_call | solution.py:230
  93.2 3.0 %collective-permute-done.6.refs_7_ = bf16[128,768]{1,0:T(8,128)(2,1)} collective-permute-done((bf16[128,768]{1,0:T(8,128)(2,1)S(1)}, bf16[128,768]{1,0:T(8,128)(2,1)}, u32[]{:S(2)}, u32[]{:S(2)}) %collective-permute-start.6) | collective-permute-done | bytes 196640 | tf_op jit(solution)/shard_map/ppermute | solution.py:208
  96.2 14.4 %all-to-all-start = ((bf16[64,16,256]{2,1,0:T(8,128)(2,1)}), bf16[64,16,256]{2,1,0:T(8,128)(2,1)S(1)}, u32[]{:S(2)}, u32[]{:S(2)}) async-start(bf16[64,16,256]{2,1,0:T(8,128)(2,1)} %pack.1), calls=%async_computation | async-start | bytes 1048576 | tf_op jit(solution)/shard_map/all_to_all | solution.py:240
  110.7 20.3 %product.1 = (f32[96,896]{1,0:T(8,128)}, bf16[512,768]{1,0:T(8,128)(2,1)}, bf16[512,128]{1,0:T(8,128)(2,1)}) custom-call(s32[64]{0:T(128)} %lengths.5, s32[64]{0:T(128)} %shifts.5, s32[2]{0:T(128)} %pad_add_fusion.own, bf16[8,2,4,672,128]{4,3,2,1,0:T(8,128)(2,1)} %bitcast.6, bf16[512,768]{1,0:T(8,128)(2,1)} %copy-done.2, bf16[256,768]{1,0:T(8,128)(2,1)} %copy-done.10, ...), custom_call_target="tpu_custom_call" | custom-call | flops 5637144576 | bytes 17301504 | tf_op jit(solution)/shard_map/product/pallas_call | solution.py:245
  131.8 2.5 %unpack.1 = (f32[96,896]{1,0:T(8,128)}, f32[96,896]{1,0:T(8,128)}) custom-call(s32[64]{0:T(128)} %lengths.5, s32[64]{0:T(128)} %shifts.5, s32[2]{0:T(128)} %pad_add_fusion.own, bf16[64,16,256]{2,1,0:T(8,128)(2,1)} %copy-done.1), custom_call_target="tpu_custom_call" | custom-call | tf_op jit(solution)/shard_map/unpack/pallas_call | solution.py:274
  (59 shorter events, 6.5 us)
Async XLA Ops:
  7.2 103.4 %all-gather.2.cloned.1.call-start = ((), (), s32[]{:S(2)}) async-start(), calls=%async_computation.1 | async-start | bytes 11698176 | tf_op jit(solution)/shard_map/all_gather | solution.py:221
  22.4 73.9 %copy-start.2 = (bf16[512,768]{1,0:T(8,128)(2,1)}, bf16[512,768]{1,0:T(8,128)(2,1)S(1)}, u32[]{:S(2)}) copy-start(bf16[512,768]{1,0:T(8,128)(2,1)S(1)} %fusion.2.refs_0_) | copy-start | bytes 2359300
  22.4 19.4 %collective-permute-start.9 = (bf16[256,768]{1,0:T(8,128)(2,1)S(1)}, bf16[256,768]{1,0:T(8,128)(2,1)S(1)}, u32[]{:S(2)}, u32[]{:S(2)}) collective-permute-start(bf16[256,768]{1,0:T(8,128)(2,1)S(1)} %get-tuple-element.55), channel_id=1, source_target_pairs={{0,7},{1,0},{2,1},{3,2},{4,3},{5,4},{6,5},{7,6},{8,15},{9,8},{10,9... | collective-permute-start | bytes 1179656 | tf_op jit(solution)/shard_map/ppermute | solution.py:204
  33.4 13.0 %collective-permute-start.8 = (bf16[256,768]{1,0:T(8,128)(2,1)S(1)}, bf16[256,768]{1,0:T(8,128)(2,1)S(1)}, u32[]{:S(2)}, u32[]{:S(2)}) collective-permute-start(bf16[256,768]{1,0:T(8,128)(2,1)S(1)} %get-tuple-element.55), channel_id=1, source_target_pairs={{0,1},{1,2},{2,3},{3,4},{4,5},{5,6},{6,7},{7,0},{8,9},{9,10},{10,1... | collective-permute-start | bytes 1179656 | tf_op jit(solution)/shard_map/ppermute | solution.py:203
  35.4 13.6 %collective-permute-start.1 = (bf16[256,768]{1,0:T(8,128)(2,1)S(1)}, bf16[256,768]{1,0:T(8,128)(2,1)S(1)}, u32[]{:S(2)}, u32[]{:S(2)}) collective-permute-start(bf16[256,768]{1,0:T(8,128)(2,1)S(1)} %get-tuple-element.56), channel_id=1, source_target_pairs={{0,7},{1,0},{2,1},{3,2},{4,3},{5,4},{6,5},{7,6},{8,15},{9,8},{10,9... | collective-permute-start | bytes 1179656 | tf_op jit(solution)/shard_map/ppermute | solution.py:204
  39.9 14.4 %collective-permute-start = (bf16[256,768]{1,0:T(8,128)(2,1)S(1)}, bf16[256,768]{1,0:T(8,128)(2,1)S(1)}, u32[]{:S(2)}, u32[]{:S(2)}) collective-permute-start(bf16[256,768]{1,0:T(8,128)(2,1)S(1)} %get-tuple-element.56), channel_id=1, source_target_pairs={{0,1},{1,2},{2,3},{3,4},{4,5},{5,6},{6,7},{7,0},{8,9},{9,10},{10,1... | collective-permute-start | bytes 1179656 | tf_op jit(solution)/shard_map/ppermute | solution.py:203
  41.9 31.3 %copy-start.7 = (bf16[256,768]{1,0:T(8,128)(2,1)}, bf16[256,768]{1,0:T(8,128)(2,1)S(1)}, u32[]{:S(2)}) copy-start(bf16[256,768]{1,0:T(8,128)(2,1)S(1)} %collective-permute-done.9.refs_10_) | copy-start | bytes 1179652
  41.9 15.5 %collective-permute-start.11 = (bf16[256,768]{1,0:T(8,128)(2,1)S(1)}, bf16[256,768]{1,0:T(8,128)(2,1)S(1)}, u32[]{:S(2)}, u32[]{:S(2)}) collective-permute-start(bf16[256,768]{1,0:T(8,128)(2,1)S(1)} %collective-permute-done.9.refs_10_), channel_id=1, source_target_pairs={{0,7},{1,0},{2,1},{3,2},{4,3},{5,4},{6,5},{7,6},{8,15},{9,8},{10,9... | collective-permute-start | bytes 1179656 | tf_op jit(solution)/shard_map/ppermute | solution.py:204
  46.5 35.1 %copy-start.8 = (bf16[256,768]{1,0:T(8,128)(2,1)}, bf16[256,768]{1,0:T(8,128)(2,1)S(1)}, u32[]{:S(2)}) copy-start(bf16[256,768]{1,0:T(8,128)(2,1)S(1)} %collective-permute-done.8.refs_9_) | copy-start | bytes 1179652
  46.5 16.3 %collective-permute-start.10 = (bf16[256,768]{1,0:T(8,128)(2,1)S(1)}, bf16[256,768]{1,0:T(8,128)(2,1)S(1)}, u32[]{:S(2)}, u32[]{:S(2)}) collective-permute-start(bf16[256,768]{1,0:T(8,128)(2,1)S(1)} %collective-permute-done.8.refs_9_), channel_id=1, source_target_pairs={{0,1},{1,2},{2,3},{3,4},{4,5},{5,6},{6,7},{7,0},{8,9},{9,10},{10,1... | collective-permute-start | bytes 1179656 | tf_op jit(solution)/shard_map/ppermute | solution.py:203
  48.9 16.9 %collective-permute-start.3 = (bf16[256,768]{1,0:T(8,128)(2,1)S(1)}, bf16[256,768]{1,0:T(8,128)(2,1)S(1)}, u32[]{:S(2)}, u32[]{:S(2)}) collective-permute-start(bf16[256,768]{1,0:T(8,128)(2,1)S(1)} %collective-permute-done.1.refs_2_), channel_id=1, source_target_pairs={{0,7},{1,0},{2,1},{3,2},{4,3},{5,4},{6,5},{7,6},{8,15},{9,8},{10,9... | collective-permute-start | bytes 1179656 | tf_op jit(solution)/shard_map/ppermute | solution.py:204
  54.4 16.8 %collective-permute-start.2 = (bf16[256,768]{1,0:T(8,128)(2,1)S(1)}, bf16[256,768]{1,0:T(8,128)(2,1)S(1)}, u32[]{:S(2)}, u32[]{:S(2)}) collective-permute-start(bf16[256,768]{1,0:T(8,128)(2,1)S(1)} %collective-permute-done.refs_1_), channel_id=1, source_target_pairs={{0,1},{1,2},{2,3},{3,4},{4,5},{5,6},{6,7},{7,0},{8,9},{9,10},{10,1... | collective-permute-start | bytes 1179656 | tf_op jit(solution)/shard_map/ppermute | solution.py:203
  57.3 32.7 %copy-start.11 = (bf16[256,768]{1,0:T(8,128)(2,1)}, bf16[256,768]{1,0:T(8,128)(2,1)S(1)}, u32[]{:S(2)}) copy-start(bf16[256,768]{1,0:T(8,128)(2,1)S(1)} %collective-permute-done.11.refs_12_) | copy-start | bytes 1179652
  57.3 16.9 %collective-permute-start.13 = (bf16[256,768]{1,0:T(8,128)(2,1)S(1)}, bf16[256,768]{1,0:T(8,128)(2,1)S(1)}, u32[]{:S(2)}, u32[]{:S(2)}) collective-permute-start(bf16[256,768]{1,0:T(8,128)(2,1)S(1)} %collective-permute-done.11.refs_12_), channel_id=1, source_target_pairs={{0,7},{1,0},{2,1},{3,2},{4,3},{5,4},{6,5},{7,6},{8,15},{9,8},{10,9... | collective-permute-start | bytes 1179656 | tf_op jit(solution)/shard_map/ppermute | solution.py:204
  62.8 16.9 %collective-permute-start.12 = (bf16[256,768]{1,0:T(8,128)(2,1)S(1)}, bf16[256,768]{1,0:T(8,128)(2,1)S(1)}, u32[]{:S(2)}, u32[]{:S(2)}) collective-permute-start(bf16[256,768]{1,0:T(8,128)(2,1)S(1)} %collective-permute-done.10.refs_11_), channel_id=1, source_target_pairs={{0,1},{1,2},{2,3},{3,4},{4,5},{5,6},{6,7},{7,0},{8,9},{9,10},{10,1... | collective-permute-start | bytes 1179656 | tf_op jit(solution)/shard_map/ppermute | solution.py:203
  65.8 16.9 %collective-permute-start.5 = (bf16[256,768]{1,0:T(8,128)(2,1)S(1)}, bf16[256,768]{1,0:T(8,128)(2,1)S(1)}, u32[]{:S(2)}, u32[]{:S(2)}) collective-permute-start(bf16[256,768]{1,0:T(8,128)(2,1)S(1)} %collective-permute-done.3.refs_4_), channel_id=1, source_target_pairs={{0,7},{1,0},{2,1},{3,2},{4,3},{5,4},{6,5},{7,6},{8,15},{9,8},{10,9... | collective-permute-start | bytes 1179656 | tf_op jit(solution)/shard_map/ppermute | solution.py:204
  71.2 16.9 %collective-permute-start.4 = (bf16[256,768]{1,0:T(8,128)(2,1)S(1)}, bf16[256,768]{1,0:T(8,128)(2,1)S(1)}, u32[]{:S(2)}, u32[]{:S(2)}) collective-permute-start(bf16[256,768]{1,0:T(8,128)(2,1)S(1)} %collective-permute-done.2.refs_3_), channel_id=1, source_target_pairs={{0,1},{1,2},{2,3},{3,4},{4,5},{5,6},{6,7},{7,0},{8,9},{9,10},{10,1... | collective-permute-start | bytes 1179656 | tf_op jit(solution)/shard_map/ppermute | solution.py:203
  74.2 36.4 %copy-start.3 = (bf16[256,768]{1,0:T(8,128)(2,1)}, bf16[256,768]{1,0:T(8,128)(2,1)S(1)}, u32[]{:S(2)}) copy-start(bf16[256,768]{1,0:T(8,128)(2,1)S(1)} %collective-permute-done.13.refs_14_) | copy-start | bytes 1179652
  74.2 19.0 %collective-permute-start.15 = (bf16[128,768]{1,0:T(8,128)(2,1)S(1)}, bf16[128,768]{1,0:T(8,128)(2,1)S(1)}, u32[]{:S(2)}, u32[]{:S(2)}) collective-permute-start(bf16[128,768]{1,0:T(8,128)(2,1)S(1)} %slice.29), channel_id=1, source_target_pairs={{0,7},{1,0},{2,1},{3,2},{4,3},{5,4},{6,5},{7,6},{8,15},{9,8},{10,9... | collective-permute-start | bytes 589832 | tf_op jit(solution)/shard_map/ppermute | solution.py:209
  79.7 31.0 %copy-start.4 = (bf16[256,768]{1,0:T(8,128)(2,1)}, bf16[256,768]{1,0:T(8,128)(2,1)S(1)}, u32[]{:S(2)}) copy-start(bf16[256,768]{1,0:T(8,128)(2,1)S(1)} %collective-permute-done.12.refs_13_) | copy-start | bytes 1179652
  79.7 13.5 %collective-permute-start.14 = (bf16[128,768]{1,0:T(8,128)(2,1)S(1)}, bf16[128,768]{1,0:T(8,128)(2,1)}, u32[]{:S(2)}, u32[]{:S(2)}) collective-permute-start(bf16[128,768]{1,0:T(8,128)(2,1)S(1)} %slice.28), channel_id=1, source_target_pairs={{0,1},{1,2},{2,3},{3,4},{4,5},{5,6},{6,7},{7,0},{8,9},{9,10},{10,1... | collective-permute-start | bytes 589832 | tf_op jit(solution)/shard_map/ppermute | solution.py:208
  82.6 10.6 %collective-permute-start.7 = (bf16[128,768]{1,0:T(8,128)(2,1)S(1)}, bf16[128,768]{1,0:T(8,128)(2,1)}, u32[]{:S(2)}, u32[]{:S(2)}) collective-permute-start(bf16[128,768]{1,0:T(8,128)(2,1)S(1)} %slice.26), channel_id=1, source_target_pairs={{0,7},{1,0},{2,1},{3,2},{4,3},{5,4},{6,5},{7,6},{8,15},{9,8},{10,9... | collective-permute-start | bytes 589832 | tf_op jit(solution)/shard_map/ppermute | solution.py:209
  88.1 8.1 %collective-permute-start.6 = (bf16[128,768]{1,0:T(8,128)(2,1)S(1)}, bf16[128,768]{1,0:T(8,128)(2,1)}, u32[]{:S(2)}, u32[]{:S(2)}) collective-permute-start(bf16[128,768]{1,0:T(8,128)(2,1)S(1)} %slice.25), channel_id=1, source_target_pairs={{0,1},{1,2},{2,3},{3,4},{4,5},{5,6},{6,7},{7,0},{8,9},{9,10},{10,1... | collective-permute-start | bytes 589832 | tf_op jit(solution)/shard_map/ppermute | solution.py:208
  96.2 34.8 %all-to-all-start = ((bf16[64,16,256]{2,1,0:T(8,128)(2,1)}), bf16[64,16,256]{2,1,0:T(8,128)(2,1)S(1)}, u32[]{:S(2)}, u32[]{:S(2)}) async-start(bf16[64,16,256]{2,1,0:T(8,128)(2,1)} %pack.1), calls=%async_computation | async-start | bytes 1048576 | tf_op jit(solution)/shard_map/all_to_all | solution.py:240
  (10 other events, 153.5 us)
Sparse Core Ops, SparseCore 0:
  21.5 77.9 all-gather.1

commit v12 on v11

--- a/solution.py
+++ b/solution.py
@@ -23,6 +23,7 @@
 GROUPS = SLOTS // GROUP
 STEP = 112
 CHAINS = 2
+TIED = 2
 CHUNK = 32
 N_Z = 8
 P_LOW = N_DP // N_Z
@@ -188,7 +189,7 @@
 VMEM = pl.BlockSpec(memory_space=pltpu.VMEM)
 
 
-def gather_tokens(tokens):
+def gather_tokens(tokens, packed):
     up = [(z, (z + 1) % N_Z) for z in range(N_Z)]
     down = [(z, (z - 1) % N_Z) for z in range(N_Z)]
     rows = tokens.shape[0] // CHAINS
@@ -202,12 +203,14 @@
         for distance in range(1, N_Z // 2):
             from_below = lax.ppermute(from_below, "tensor", up)
             from_above = lax.ppermute(from_above, "tensor", down)
+            if distance == TIED and first > 0:
+                from_below, from_above, packed = lax.optimization_barrier((from_below, from_above, packed))
             spans += [(2 * distance - 1, first), (2 * distance, first)]
             arrays += [from_below, from_above]
         spans += [(N_Z - 1, first), (N_Z - 1, first + half)]
         arrays.append(lax.ppermute(from_below[:half], "tensor", up))
         arrays.append(lax.ppermute(from_above[half:], "tensor", down))
-    return tuple(distances), tuple(spans), arrays
+    return tuple(distances), tuple(spans), arrays, packed
 
 
 def per_device(tokens, old_master, old_first, old_second, piece_lengths, piece_shifts):
@@ -235,8 +238,7 @@
         scratch_shapes=[slots, slots],
         name="pack",
     )(piece_lengths, piece_shifts, own, old_first, old_second)
-    distances, spans, blocks = gather_tokens(ordered)
-    packed, blocks = lax.optimization_barrier((packed, blocks))
+    distances, spans, blocks, packed = gather_tokens(ordered, packed)
     received = lax.all_to_all(packed, "dp", split_axis=0, concat_axis=0, tiled=True)
 
     query_cols = HQ // lax.axis_size("tensor") * HS

time: 142 us -> 141 us (level)
  starting transfers between devices: 77 us -> 72.6 us
  local copies, waits for them, and re-layouts: 1.14 us -> 3.38 us
    ppermute x2, starting transfers between devices: 10.9 us -> 6.49 us  [gather_tokens(): arrays.append(lax.ppermute(from_above[half:], 'tensor', down))]
    ppermute x6, starting transfers between devices: 36.4 us -> 32.1 us  [gather_tokens(): from_above = lax.ppermute(from_above, 'tensor', down)]
    ppermute x6, waiting for transfers between devices: 4.63 us -> 0.51 us  [gather_tokens(): from_above = lax.ppermute(from_above, 'tensor', down)]
    ppermute x6, waiting for transfers between devices: 0.02 us -> 3.33 us  [gather_tokens(): from_below = lax.ppermute(from_below, 'tensor', up)]
    ppermute x2, starting transfers between devices: 3.84 us -> 5.28 us  [gather_tokens(): arrays.append(lax.ppermute(from_below[:half], 'tensor', up))]
  transfers between devices with their start and end apart: 18 -> 18, of which waited for: 6 -> 4; matrix products, arithmetic and copies ran while one was open for 1% -> 2% of each run, Pallas kernels for 16% -> 16%
where the time goes in v12:
time: 141 us; the launch traced here: 140 us
  starting transfers between devices  72.6 us (51%)
  Pallas kernels  25.4 us (18%)
  between operations  14.5 us (10%)
  blocking collectives  12.9 us (9%)
  waiting for transfers between devices  8.26 us (6%)
  local copies, waits for them, and re-layouts  3.38 us (2%)
  other arithmetic  1.68 us (1%)
    ppermute x6, starting transfers between devices, gather_tokens(): from_above = lax.ppermute(from_above, 'tensor', down)  32.1 us
    pallas_call x1, Pallas kernels, per_device(): pl.pallas_call(functools.partial(product_kernel, distances, spans), out_s...  20.4 us
    all_to_all x1, starting transfers between devices, per_device(): lax.all_to_all(packed, 'dp', split_axis=0, concat_axis=0, tiled=True)  15.8 us
    all_gather x1, blocking collectives, per_device(): lax.all_gather(column, 'dp', axis_index_groups=X_GROUPS, axis=0, tiled=True)  12.9 us
    ppermute x6, starting transfers between devices, gather_tokens(): from_below = lax.ppermute(from_below, 'tensor', up)  12.9 us
    ppermute x2, starting transfers between devices, gather_tokens(): arrays.append(lax.ppermute(from_above[half:], 'tensor', down))  6.49 us
    ppermute x2, starting transfers between devices, gather_tokens(): arrays.append(lax.ppermute(from_below[:half], 'tensor', up))  5.28 us
    ppermute x6, waiting for transfers between devices, gather_tokens(): from_below = lax.ppermute(from_below, 'tensor', up)  3.33 us
  transfers between devices with their start and end apart: 18, of which 4 were waited for; matrix products, arithmetic and copies ran while one was open for 2% of the time, Pallas kernels for 16%

profile of v12, /device:TPU:1, one launch (start us, length us, event | category | flops | bytes accessed | tf_op | source)
XLA Modules:
  0.0 139.5 jit_solution(14173366892588569840)
XLA Ops:
  8.5 12.9 %all_gather.6 = bf16[2688,128]{1,0:T(8,128)(2,1)} all-gather(bf16[672,128]{1,0:T(8,128)(2,1)S(1)} %reshape.63), channel_id=1, replica_groups={{0,16,32,48},{8,24,40,56},{64,80,96,112},{72,88,104,120},{128,144,160,1..., dimensions={0}, use_global_device_ids=true | all-gather | bytes 860160 | tf_op jit(solution)/shard_map/all_gather | solution.py:223
  22.4 11.0 %collective-permute-start.9 = (bf16[256,768]{1,0:T(8,128)(2,1)S(1)}, bf16[256,768]{1,0:T(8,128)(2,1)S(1)}, u32[]{:S(2)}, u32[]{:S(2)}) collective-permute-start(bf16[256,768]{1,0:T(8,128)(2,1)S(1)} %get-tuple-element.25), channel_id=1, source_target_pairs={{0,7},{1,0},{2,1},{3,2},{4,3},{5,4},{6,5},{7,6},{8,15},{9,8},{10,9... | collective-permute-start | bytes 1179656 | tf_op jit(solution)/shard_map/ppermute | solution.py:205
  33.4 1.9 %collective-permute-start.8 = (bf16[256,768]{1,0:T(8,128)(2,1)S(1)}, bf16[256,768]{1,0:T(8,128)(2,1)S(1)}, u32[]{:S(2)}, u32[]{:S(2)}) collective-permute-start(bf16[256,768]{1,0:T(8,128)(2,1)S(1)} %get-tuple-element.25), channel_id=1, source_target_pairs={{0,1},{1,2},{2,3},{3,4},{4,5},{5,6},{6,7},{7,0},{8,9},{9,10},{10,1... | collective-permute-start | bytes 1179656 | tf_op jit(solution)/shard_map/ppermute | solution.py:204
  35.4 4.6 %collective-permute-start.1 = (bf16[256,768]{1,0:T(8,128)(2,1)S(1)}, bf16[256,768]{1,0:T(8,128)(2,1)S(1)}, u32[]{:S(2)}, u32[]{:S(2)}) collective-permute-start(bf16[256,768]{1,0:T(8,128)(2,1)S(1)} %get-tuple-element.26), channel_id=1, source_target_pairs={{0,7},{1,0},{2,1},{3,2},{4,3},{5,4},{6,5},{7,6},{8,15},{9,8},{10,9... | collective-permute-start | bytes 1179656 | tf_op jit(solution)/shard_map/ppermute | solution.py:205
  39.9 1.9 %collective-permute-start = (bf16[256,768]{1,0:T(8,128)(2,1)S(1)}, bf16[256,768]{1,0:T(8,128)(2,1)}, u32[]{:S(2)}, u32[]{:S(2)}) collective-permute-start(bf16[256,768]{1,0:T(8,128)(2,1)S(1)} %get-tuple-element.26), channel_id=1, source_target_pairs={{0,1},{1,2},{2,3},{3,4},{4,5},{5,6},{6,7},{7,0},{8,9},{9,10},{10,1... | collective-permute-start | bytes 1179656 | tf_op jit(solution)/shard_map/ppermute | solution.py:204
  41.9 4.6 %collective-permute-start.11 = (bf16[256,768]{1,0:T(8,128)(2,1)S(1)}, bf16[256,768]{1,0:T(8,128)(2,1)}, u32[]{:S(2)}, u32[]{:S(2)}) collective-permute-start(bf16[256,768]{1,0:T(8,128)(2,1)S(1)} %collective-permute-done.9.refs_10_), channel_id=1, source_target_pairs={{0,7},{1,0},{2,1},{3,2},{4,3},{5,4},{6,5},{7,6},{8,15},{9,8},{10,9... | collective-permute-start | bytes 1179656 | tf_op jit(solution)/shard_map/ppermute | solution.py:205
  46.5 1.9 %collective-permute-start.10 = (bf16[256,768]{1,0:T(8,128)(2,1)S(1)}, bf16[256,768]{1,0:T(8,128)(2,1)}, u32[]{:S(2)}, u32[]{:S(2)}) collective-permute-start(bf16[256,768]{1,0:T(8,128)(2,1)S(1)} %collective-permute-done.8.refs_9_), channel_id=1, source_target_pairs={{0,1},{1,2},{2,3},{3,4},{4,5},{5,6},{6,7},{7,0},{8,9},{9,10},{10,1... | collective-permute-start | bytes 1179656 | tf_op jit(solution)/shard_map/ppermute | solution.py:204
  48.9 5.4 %collective-permute-start.3 = (bf16[256,768]{1,0:T(8,128)(2,1)S(1)}, bf16[256,768]{1,0:T(8,128)(2,1)}, u32[]{:S(2)}, u32[]{:S(2)}) collective-permute-start(bf16[256,768]{1,0:T(8,128)(2,1)S(1)} %collective-permute-done.1.refs_2_), channel_id=1, source_target_pairs={{0,7},{1,0},{2,1},{3,2},{4,3},{5,4},{6,5},{7,6},{8,15},{9,8},{10,9... | collective-permute-start | bytes 1179656 | tf_op jit(solution)/shard_map/ppermute | solution.py:205
  54.4 1.9 %collective-permute-start.2 = (bf16[256,768]{1,0:T(8,128)(2,1)}, bf16[256,768]{1,0:T(8,128)(2,1)}, u32[]{:S(2)}, u32[]{:S(2)}) collective-permute-start(bf16[256,768]{1,0:T(8,128)(2,1)} %collective-permute-done.refs_1_), channel_id=1, source_target_pairs={{0,1},{1,2},{2,3},{3,4},{4,5},{5,6},{6,7},{7,0},{8,9},{9,10},{10,1... | collective-permute-start | bytes 1179656 | tf_op jit(solution)/shard_map/ppermute | solution.py:204
  56.9 2.4 %pack.1 = bf16[64,16,256]{2,1,0:T(8,128)(2,1)} custom-call(s32[64]{0:T(128)} %lengths.5, s32[64]{0:T(128)} %shifts.5, s32[2]{0:T(128)} %pad_add_fusion.own, f32[96,896]{1,0:T(8,128)} %first.1, f32[96,896]{1,0:T(8,128)} %second.1), custom_call_target="tpu_custom_call" | custom-call | tf_op jit(solution)/shard_map/pack/pallas_call | solution.py:233
  59.3 3.3 %collective-permute-done.10.refs_11_ = bf16[256,768]{1,0:T(8,128)(2,1)} collective-permute-done((bf16[256,768]{1,0:T(8,128)(2,1)S(1)}, bf16[256,768]{1,0:T(8,128)(2,1)}, u32[]{:S(2)}, u32[]{:S(2)}) %collective-permute-start.10) | collective-permute-done | bytes 393248 | tf_op jit(solution)/shard_map/ppermute | solution.py:204
  62.6 1.9 %collective-permute-start.12 = (bf16[256,768]{1,0:T(8,128)(2,1)}, bf16[256,768]{1,0:T(8,128)(2,1)S(1)}, u32[]{:S(2)}, u32[]{:S(2)}) collective-permute-start(bf16[256,768]{1,0:T(8,128)(2,1)} %collective-permute-done.10.refs_11_), channel_id=1, source_target_pairs={{0,1},{1,2},{2,3},{3,4},{4,5},{5,6},{6,7},{7,0},{8,9},{9,10},{10,1... | collective-permute-start | bytes 1179656 | tf_op jit(solution)/shard_map/ppermute | solution.py:204
  64.6 4.6 %collective-permute-start.13 = (bf16[256,768]{1,0:T(8,128)(2,1)}, bf16[256,768]{1,0:T(8,128)(2,1)S(1)}, u32[]{:S(2)}, u32[]{:S(2)}) collective-permute-start(bf16[256,768]{1,0:T(8,128)(2,1)} %collective-permute-done.11.refs_12_), channel_id=1, source_target_pairs={{0,7},{1,0},{2,1},{3,2},{4,3},{5,4},{6,5},{7,6},{8,15},{9,8},{10,9... | collective-permute-start | bytes 1179656 | tf_op jit(solution)/shard_map/ppermute | solution.py:205
  69.2 2.0 %collective-permute-start.5 = (bf16[256,768]{1,0:T(8,128)(2,1)}, bf16[256,768]{1,0:T(8,128)(2,1)S(1)}, u32[]{:S(2)}, u32[]{:S(2)}) collective-permute-start(bf16[256,768]{1,0:T(8,128)(2,1)} %collective-permute-done.3.refs_4_), channel_id=1, source_target_pairs={{0,7},{1,0},{2,1},{3,2},{4,3},{5,4},{6,5},{7,6},{8,15},{9,8},{10,9... | collective-permute-start | bytes 1179656 | tf_op jit(solution)/shard_map/ppermute | solution.py:205
  71.2 3.3 %collective-permute-start.4 = (bf16[256,768]{1,0:T(8,128)(2,1)}, bf16[256,768]{1,0:T(8,128)(2,1)}, u32[]{:S(2)}, u32[]{:S(2)}) collective-permute-start(bf16[256,768]{1,0:T(8,128)(2,1)} %collective-permute-done.2.refs_3_), channel_id=1, source_target_pairs={{0,1},{1,2},{2,3},{3,4},{4,5},{5,6},{6,7},{7,0},{8,9},{9,10},{10,1... | collective-permute-start | bytes 1179656 | tf_op jit(solution)/shard_map/ppermute | solution.py:204
  74.5 15.8 %all-to-all-start = ((bf16[64,16,256]{2,1,0:T(8,128)(2,1)}), bf16[64,16,256]{2,1,0:T(8,128)(2,1)S(1)}, u32[]{:S(2)}, u32[]{:S(2)}) async-start(bf16[64,16,256]{2,1,0:T(8,128)(2,1)} %pack.1), calls=%async_computation | async-start | bytes 1048576 | tf_op jit(solution)/shard_map/all_to_all | solution.py:242
  90.3 1.9 %collective-permute-start.14 = (bf16[128,768]{1,0:T(8,128)(2,1)S(1)}, bf16[128,768]{1,0:T(8,128)(2,1)S(1)}, u32[]{:S(2)}, u32[]{:S(2)}) collective-permute-start(bf16[128,768]{1,0:T(8,128)(2,1)S(1)} %slice.28), channel_id=1, source_target_pairs={{0,1},{1,2},{2,3},{3,4},{4,5},{5,6},{6,7},{7,0},{8,9},{9,10},{10,1... | collective-permute-start | bytes 589832 | tf_op jit(solution)/shard_map/ppermute | solution.py:211
  92.3 4.6 %collective-permute-start.15 = (bf16[128,768]{1,0:T(8,128)(2,1)S(1)}, bf16[128,768]{1,0:T(8,128)(2,1)S(1)}, u32[]{:S(2)}, u32[]{:S(2)}) collective-permute-start(bf16[128,768]{1,0:T(8,128)(2,1)S(1)} %slice.29), channel_id=1, source_target_pairs={{0,7},{1,0},{2,1},{3,2},{4,3},{5,4},{6,5},{7,6},{8,15},{9,8},{10,9... | collective-permute-start | bytes 589832 | tf_op jit(solution)/shard_map/ppermute | solution.py:212
  96.9 1.9 %collective-permute-start.7 = (bf16[128,768]{1,0:T(8,128)(2,1)S(1)}, bf16[128,768]{1,0:T(8,128)(2,1)S(1)}, u32[]{:S(2)}, u32[]{:S(2)}) collective-permute-start(bf16[128,768]{1,0:T(8,128)(2,1)S(1)} %slice.26), channel_id=1, source_target_pairs={{0,7},{1,0},{2,1},{3,2},{4,3},{5,4},{6,5},{7,6},{8,15},{9,8},{10,9... | collective-permute-start | bytes 589832 | tf_op jit(solution)/shard_map/ppermute | solution.py:212
  99.8 3.4 %collective-permute-start.6 = (bf16[128,768]{1,0:T(8,128)(2,1)S(1)}, bf16[128,768]{1,0:T(8,128)(2,1)S(1)}, u32[]{:S(2)}, u32[]{:S(2)}) collective-permute-start(bf16[128,768]{1,0:T(8,128)(2,1)S(1)} %slice.25), channel_id=1, source_target_pairs={{0,1},{1,2},{2,3},{3,4},{4,5},{5,6},{6,7},{7,0},{8,9},{9,10},{10,1... | collective-permute-start | bytes 589832 | tf_op jit(solution)/shard_map/ppermute | solution.py:211
  103.2 1.3 collective-permute-done.7.refs_8_
  105.2 3.1 %collective-permute-done.6.refs_7_ = bf16[128,768]{1,0:T(8,128)(2,1)S(1)} collective-permute-done((bf16[128,768]{1,0:T(8,128)(2,1)S(1)}, bf16[128,768]{1,0:T(8,128)(2,1)S(1)}, u32[]{:S(2)}, u32[]{:S(2)}) %collective-permute-start.6) | collective-permute-done | bytes 196640 | tf_op jit(solution)/shard_map/ppermute | solution.py:211
  108.9 20.4 %product.1 = (f32[96,896]{1,0:T(8,128)}, bf16[512,768]{1,0:T(8,128)(2,1)}, bf16[512,128]{1,0:T(8,128)(2,1)}) custom-call(s32[64]{0:T(128)} %lengths.5, s32[64]{0:T(128)} %shifts.5, s32[2]{0:T(128)} %pad_add_fusion.own, bf16[8,2,4,672,128]{4,3,2,1,0:T(8,128)(2,1)} %bitcast.6, bf16[512,768]{1,0:T(8,128)(2,1)} %copy-done.2, ...), custom_call_target="tpu_custom_call" | custom-call | flops 5637144576 | bytes 17301504 | tf_op jit(solution)/shard_map/product/pallas_call | solution.py:247
  130.2 2.5 %unpack.1 = (f32[96,896]{1,0:T(8,128)}, f32[96,896]{1,0:T(8,128)}) custom-call(s32[64]{0:T(128)} %lengths.5, s32[64]{0:T(128)} %shifts.5, s32[2]{0:T(128)} %pad_add_fusion.own, bf16[64,16,256]{2,1,0:T(8,128)(2,1)} %copy-done.1), custom_call_target="tpu_custom_call" | custom-call | tf_op jit(solution)/shard_map/unpack/pallas_call | solution.py:276
  (53 shorter events, 6.6 us)
Async XLA Ops:
  7.2 14.2 %copy-start = (bf16[512,768]{1,0:T(8,128)(2,1)S(1)}, bf16[512,768]{1,0:T(8,128)(2,1)}, u32[]{:S(2)}) copy-start(bf16[512,768]{1,0:T(8,128)(2,1)} %param.6) | copy-start | bytes 2359300
  7.2 101.1 %all-gather.2.cloned.1.call-start = ((), (), s32[]{:S(2)}) async-start(), calls=%async_computation.1 | async-start | bytes 11698176 | tf_op jit(solution)/shard_map/all_gather | solution.py:224
  22.4 74.5 %copy-start.2 = (bf16[512,768]{1,0:T(8,128)(2,1)}, bf16[512,768]{1,0:T(8,128)(2,1)S(1)}, u32[]{:S(2)}) copy-start(bf16[512,768]{1,0:T(8,128)(2,1)S(1)} %fusion.2.refs_0_) | copy-start | bytes 2359300
  22.4 19.4 %collective-permute-start.9 = (bf16[256,768]{1,0:T(8,128)(2,1)S(1)}, bf16[256,768]{1,0:T(8,128)(2,1)S(1)}, u32[]{:S(2)}, u32[]{:S(2)}) collective-permute-start(bf16[256,768]{1,0:T(8,128)(2,1)S(1)} %get-tuple-element.25), channel_id=1, source_target_pairs={{0,7},{1,0},{2,1},{3,2},{4,3},{5,4},{6,5},{7,6},{8,15},{9,8},{10,9... | collective-permute-start | bytes 1179656 | tf_op jit(solution)/shard_map/ppermute | solution.py:205
  33.4 13.0 %collective-permute-start.8 = (bf16[256,768]{1,0:T(8,128)(2,1)S(1)}, bf16[256,768]{1,0:T(8,128)(2,1)S(1)}, u32[]{:S(2)}, u32[]{:S(2)}) collective-permute-start(bf16[256,768]{1,0:T(8,128)(2,1)S(1)} %get-tuple-element.25), channel_id=1, source_target_pairs={{0,1},{1,2},{2,3},{3,4},{4,5},{5,6},{6,7},{7,0},{8,9},{9,10},{10,1... | collective-permute-start | bytes 1179656 | tf_op jit(solution)/shard_map/ppermute | solution.py:204
  35.4 13.6 %collective-permute-start.1 = (bf16[256,768]{1,0:T(8,128)(2,1)S(1)}, bf16[256,768]{1,0:T(8,128)(2,1)S(1)}, u32[]{:S(2)}, u32[]{:S(2)}) collective-permute-start(bf16[256,768]{1,0:T(8,128)(2,1)S(1)} %get-tuple-element.26), channel_id=1, source_target_pairs={{0,7},{1,0},{2,1},{3,2},{4,3},{5,4},{6,5},{7,6},{8,15},{9,8},{10,9... | collective-permute-start | bytes 1179656 | tf_op jit(solution)/shard_map/ppermute | solution.py:205
  39.9 14.4 %collective-permute-start = (bf16[256,768]{1,0:T(8,128)(2,1)S(1)}, bf16[256,768]{1,0:T(8,128)(2,1)}, u32[]{:S(2)}, u32[]{:S(2)}) collective-permute-start(bf16[256,768]{1,0:T(8,128)(2,1)S(1)} %get-tuple-element.26), channel_id=1, source_target_pairs={{0,1},{1,2},{2,3},{3,4},{4,5},{5,6},{6,7},{7,0},{8,9},{9,10},{10,1... | collective-permute-start | bytes 1179656 | tf_op jit(solution)/shard_map/ppermute | solution.py:204
  41.9 32.6 %copy-start.6 = (bf16[256,768]{1,0:T(8,128)(2,1)}, bf16[256,768]{1,0:T(8,128)(2,1)S(1)}, u32[]{:S(2)}) copy-start(bf16[256,768]{1,0:T(8,128)(2,1)S(1)} %collective-permute-done.9.refs_10_) | copy-start | bytes 1179652
  41.9 17.4 %collective-permute-start.11 = (bf16[256,768]{1,0:T(8,128)(2,1)S(1)}, bf16[256,768]{1,0:T(8,128)(2,1)}, u32[]{:S(2)}, u32[]{:S(2)}) collective-permute-start(bf16[256,768]{1,0:T(8,128)(2,1)S(1)} %collective-permute-done.9.refs_10_), channel_id=1, source_target_pairs={{0,7},{1,0},{2,1},{3,2},{4,3},{5,4},{6,5},{7,6},{8,15},{9,8},{10,9... | collective-permute-start | bytes 1179656 | tf_op jit(solution)/shard_map/ppermute | solution.py:205
  46.5 16.2 %collective-permute-start.10 = (bf16[256,768]{1,0:T(8,128)(2,1)S(1)}, bf16[256,768]{1,0:T(8,128)(2,1)}, u32[]{:S(2)}, u32[]{:S(2)}) collective-permute-start(bf16[256,768]{1,0:T(8,128)(2,1)S(1)} %collective-permute-done.8.refs_9_), channel_id=1, source_target_pairs={{0,1},{1,2},{2,3},{3,4},{4,5},{5,6},{6,7},{7,0},{8,9},{9,10},{10,1... | collective-permute-start | bytes 1179656 | tf_op jit(solution)/shard_map/ppermute | solution.py:204
  48.9 20.2 %copy-start.8 = (bf16[256,768]{1,0:T(8,128)(2,1)}, bf16[256,768]{1,0:T(8,128)(2,1)S(1)}, u32[]{:S(2)}) copy-start(bf16[256,768]{1,0:T(8,128)(2,1)S(1)} %collective-permute-done.1.refs_2_) | copy-start | bytes 1179652
  48.9 20.2 %collective-permute-start.3 = (bf16[256,768]{1,0:T(8,128)(2,1)S(1)}, bf16[256,768]{1,0:T(8,128)(2,1)}, u32[]{:S(2)}, u32[]{:S(2)}) collective-permute-start(bf16[256,768]{1,0:T(8,128)(2,1)S(1)} %collective-permute-done.1.refs_2_), channel_id=1, source_target_pairs={{0,7},{1,0},{2,1},{3,2},{4,3},{5,4},{6,5},{7,6},{8,15},{9,8},{10,9... | collective-permute-start | bytes 1179656 | tf_op jit(solution)/shard_map/ppermute | solution.py:205
  54.4 16.8 %collective-permute-start.2 = (bf16[256,768]{1,0:T(8,128)(2,1)}, bf16[256,768]{1,0:T(8,128)(2,1)}, u32[]{:S(2)}, u32[]{:S(2)}) collective-permute-start(bf16[256,768]{1,0:T(8,128)(2,1)} %collective-permute-done.refs_1_), channel_id=1, source_target_pairs={{0,1},{1,2},{2,3},{3,4},{4,5},{5,6},{6,7},{7,0},{8,9},{9,10},{10,1... | collective-permute-start | bytes 1179656 | tf_op jit(solution)/shard_map/ppermute | solution.py:204
  62.6 27.6 %collective-permute-start.12 = (bf16[256,768]{1,0:T(8,128)(2,1)}, bf16[256,768]{1,0:T(8,128)(2,1)S(1)}, u32[]{:S(2)}, u32[]{:S(2)}) collective-permute-start(bf16[256,768]{1,0:T(8,128)(2,1)} %collective-permute-done.10.refs_11_), channel_id=1, source_target_pairs={{0,1},{1,2},{2,3},{3,4},{4,5},{5,6},{6,7},{7,0},{8,9},{9,10},{10,1... | collective-permute-start | bytes 1179656 | tf_op jit(solution)/shard_map/ppermute | solution.py:204
  64.6 27.7 %collective-permute-start.13 = (bf16[256,768]{1,0:T(8,128)(2,1)}, bf16[256,768]{1,0:T(8,128)(2,1)S(1)}, u32[]{:S(2)}, u32[]{:S(2)}) collective-permute-start(bf16[256,768]{1,0:T(8,128)(2,1)} %collective-permute-done.11.refs_12_), channel_id=1, source_target_pairs={{0,7},{1,0},{2,1},{3,2},{4,3},{5,4},{6,5},{7,6},{8,15},{9,8},{10,9... | collective-permute-start | bytes 1179656 | tf_op jit(solution)/shard_map/ppermute | solution.py:205
  69.2 27.7 %collective-permute-start.5 = (bf16[256,768]{1,0:T(8,128)(2,1)}, bf16[256,768]{1,0:T(8,128)(2,1)S(1)}, u32[]{:S(2)}, u32[]{:S(2)}) collective-permute-start(bf16[256,768]{1,0:T(8,128)(2,1)} %collective-permute-done.3.refs_4_), channel_id=1, source_target_pairs={{0,7},{1,0},{2,1},{3,2},{4,3},{5,4},{6,5},{7,6},{8,15},{9,8},{10,9... | collective-permute-start | bytes 1179656 | tf_op jit(solution)/shard_map/ppermute | solution.py:205
  71.2 27.6 %collective-permute-start.4 = (bf16[256,768]{1,0:T(8,128)(2,1)}, bf16[256,768]{1,0:T(8,128)(2,1)}, u32[]{:S(2)}, u32[]{:S(2)}) collective-permute-start(bf16[256,768]{1,0:T(8,128)(2,1)} %collective-permute-done.2.refs_3_), channel_id=1, source_target_pairs={{0,1},{1,2},{2,3},{3,4},{4,5},{5,6},{6,7},{7,0},{8,9},{9,10},{10,1... | collective-permute-start | bytes 1179656 | tf_op jit(solution)/shard_map/ppermute | solution.py:204
  74.5 54.9 %all-to-all-start = ((bf16[64,16,256]{2,1,0:T(8,128)(2,1)}), bf16[64,16,256]{2,1,0:T(8,128)(2,1)S(1)}, u32[]{:S(2)}, u32[]{:S(2)}) async-start(bf16[64,16,256]{2,1,0:T(8,128)(2,1)} %pack.1), calls=%async_computation | async-start | bytes 1048576 | tf_op jit(solution)/shard_map/all_to_all | solution.py:242
  90.3 18.0 %copy-start.3 = (bf16[256,768]{1,0:T(8,128)(2,1)}, bf16[256,768]{1,0:T(8,128)(2,1)S(1)}, u32[]{:S(2)}) copy-start(bf16[256,768]{1,0:T(8,128)(2,1)S(1)} %collective-permute-done.12.refs_13_) | copy-start | bytes 1179652
  90.3 12.9 %collective-permute-start.14 = (bf16[128,768]{1,0:T(8,128)(2,1)S(1)}, bf16[128,768]{1,0:T(8,128)(2,1)S(1)}, u32[]{:S(2)}, u32[]{:S(2)}) collective-permute-start(bf16[128,768]{1,0:T(8,128)(2,1)S(1)} %slice.28), channel_id=1, source_target_pairs={{0,1},{1,2},{2,3},{3,4},{4,5},{5,6},{6,7},{7,0},{8,9},{9,10},{10,1... | collective-permute-start | bytes 589832 | tf_op jit(solution)/shard_map/ppermute | solution.py:211
  92.2 16.0 %copy-start.4 = (bf16[256,768]{1,0:T(8,128)(2,1)}, bf16[256,768]{1,0:T(8,128)(2,1)S(1)}, u32[]{:S(2)}) copy-start(bf16[256,768]{1,0:T(8,128)(2,1)S(1)} %collective-permute-done.13.refs_14_) | copy-start | bytes 1179652
  92.3 10.9 %collective-permute-start.15 = (bf16[128,768]{1,0:T(8,128)(2,1)S(1)}, bf16[128,768]{1,0:T(8,128)(2,1)S(1)}, u32[]{:S(2)}, u32[]{:S(2)}) collective-permute-start(bf16[128,768]{1,0:T(8,128)(2,1)S(1)} %slice.29), channel_id=1, source_target_pairs={{0,7},{1,0},{2,1},{3,2},{4,3},{5,4},{6,5},{7,6},{8,15},{9,8},{10,9... | collective-permute-start | bytes 589832 | tf_op jit(solution)/shard_map/ppermute | solution.py:212
  96.9 7.6 %collective-permute-start.7 = (bf16[128,768]{1,0:T(8,128)(2,1)S(1)}, bf16[128,768]{1,0:T(8,128)(2,1)S(1)}, u32[]{:S(2)}, u32[]{:S(2)}) collective-permute-start(bf16[128,768]{1,0:T(8,128)(2,1)S(1)} %slice.26), channel_id=1, source_target_pairs={{0,7},{1,0},{2,1},{3,2},{4,3},{5,4},{6,5},{7,6},{8,15},{9,8},{10,9... | collective-permute-start | bytes 589832 | tf_op jit(solution)/shard_map/ppermute | solution.py:212
  99.8 8.5 %collective-permute-start.6 = (bf16[128,768]{1,0:T(8,128)(2,1)S(1)}, bf16[128,768]{1,0:T(8,128)(2,1)S(1)}, u32[]{:S(2)}, u32[]{:S(2)}) collective-permute-start(bf16[128,768]{1,0:T(8,128)(2,1)S(1)} %slice.25), channel_id=1, source_target_pairs={{0,1},{1,2},{2,3},{3,4},{4,5},{5,6},{6,7},{7,0},{8,9},{9,10},{10,1... | collective-permute-start | bytes 589832 | tf_op jit(solution)/shard_map/ppermute | solution.py:211
  (7 other events, 32.9 us)
Sparse Core Ops, SparseCore 0:
  21.5 86.2 all-gather.1
